TPU v7x, 512 devices: a whole 4x8x8 slice. The times are simulated.
512 devices in a mesh: particle: 16 (over x, z_lo, core), rows: 32 (over z_hi, y).
Axes of the slice: x: 4, y: 8, z: 8 (z_hi: 4, z_lo: 2; z = z_hi * 2 + z_lo), core: 2. Of those that a mesh axis runs over, the one named last changes fastest.
Arguments:
- latent: bfloat16 [16, 128, 24, 640], P('particle', 'rows'), may hold values from -20 to 20
- ada_scale: float32 [640], replicated, may hold values from -0.5 to 0.5
- ada_shift: float32 [640], replicated, may hold values from -3 to 3
- conv_weight: bfloat16 [5760, 640], P('rows'), may hold values from -0.078125 to 0.078125
- qkv_weight: bfloat16 [640, 1920], replicated, may hold values from -1.4230249 to 1.4230249
- out_weight: bfloat16 [640, 640], replicated, may hold values from -0.25 to 0.25
- ancestors: int32 [16], replicated, may hold values from 0 to 15
Outputs:
- resampled: bfloat16 [16, 128, 24, 640], P('particle', 'rows')
All inputs are finite; a program needn't handle non-finite values.
Results may differ from a plain program's by a relative error of at most 0.0081.
Values may be sent and summed in bfloat16 or wider, within the bound.
No kernel may reach another device: no remote copies, remote signals or barrier semaphores. Data moves between devices by JAX's collectives and lax.ppermute only.
A program may use at most 64 MiB of HBM per device.

v0:
```python
import jax
import jax.numpy as jnp
from jax import lax
from jax.sharding import Mesh
from jax.sharding import PartitionSpec as P

HEADS = 10
GROUPS = 32
ROWS = ("rows_0", "rows_1")


def copy_for_each(shard, axis):
    copies = jnp.broadcast_to(shard, (lax.axis_size(axis), *shard.shape))
    return lax.all_to_all(copies, axis, split_axis=0, concat_axis=0, tiled=True)


def of_everyone(shard, axis):
    return copy_for_each(shard, axis).sum(axis=0)


def with_halo(shard, sides, width):
    for axis, dim in sides:
        count, length = (lax.axis_size(axis), shard.shape[dim])
        up = [(i, (i + 1) % count) for i in range(count - 1)]
        down = [(j, i) for i, j in up]
        last = lax.slice_in_dim(shard, length - width, length, axis=dim)
        initial = lax.slice_in_dim(shard, 0, width, axis=dim)
        before = lax.ppermute(last, axis, up)
        after = lax.ppermute(initial, axis, down)
        shard = jnp.concatenate([before, shard, after], axis=dim)
    return shard


def in_order(pieces, dim):
    pieces = jnp.moveaxis(pieces, 0, dim)
    shape = pieces.shape
    return pieces.reshape(*shape[:dim], shape[dim] * shape[dim + 1], *shape[dim + 2 :])


def all_blocks(shard, axes, turns):
    pieces = shard
    for k in turns:
        pieces = lax.all_gather(pieces, axes[k])
    done = turns[::-1]
    back = [done.index(k) for k in range(len(axes))]
    pieces = pieces.transpose(*back, *range(len(axes), pieces.ndim))
    return pieces.reshape(-1, *shard.shape)


def whole_of(shard, axes, turns, dim):
    return in_order(all_blocks(shard, axes, turns), dim)


def side_by_side(arrays, axis, dim, along):
    both = jnp.concatenate(arrays, axis=along)
    out, at, done = (lax.all_gather(both, axis, axis=dim, tiled=True), 0, [])
    for a in arrays:
        done.append(lax.slice_in_dim(out, at, at + a.shape[along], axis=along))
        at += a.shape[along]
    return tuple(done)


def group_sums(values):
    grouped = values.reshape(values.shape[0], GROUPS, -1)
    return (jnp.sum(grouped, axis=(0, 2)), jnp.sum(grouped * grouped, axis=(0, 2)))


def finish_norm(totals, count, chans):
    mean_g = totals[0] / count
    inverse = lax.rsqrt(totals[1] / count - mean_g * mean_g + 1e-05)
    per_group = chans // GROUPS
    return (jnp.repeat(mean_g, per_group), jnp.repeat(inverse, per_group))


def per_device(latent, ada_scale, ada_shift, conv_weight, qkv_weight, out_weight, ancestors):
    rows_here = latent.shape[1]
    width = latent.shape[2]
    chans = latent.shape[3]
    tokens = rows_here * width
    row_count = lax.axis_size(ROWS)
    count = rows_here * row_count * width * (chans // GROUPS)
    slab = latent[0]
    field = slab.astype(jnp.float32).reshape(tokens, chans)
    totals = jax.tree.map(lambda part: of_everyone(part, ROWS), group_sums(field))
    mean_c, inverse_c = finish_norm(totals, count, chans)
    active = (
        jax.nn.silu((field - mean_c) * inverse_c * (1.0 + ada_scale) + ada_shift)
        .astype(jnp.bfloat16)
        .reshape(rows_here, width, chans)
    )
    padded = with_halo(active, ((ROWS, 0),), 1)
    padded = jnp.pad(padded, ((0, 0), (1, 1), (0, 0)))
    patches = jnp.concatenate(
        [
            padded[row_off : row_off + rows_here, col_off : col_off + width]
            for row_off in range(3)
            for col_off in range(3)
        ],
        axis=-1,
    ).reshape(tokens, 9 * chans)
    conv = jnp.dot(
        patches, whole_of(conv_weight, ROWS, (0, 1), 0), preferred_element_type=jnp.float32
    )
    resid = lax.optimization_barrier((field + conv).astype(jnp.bfloat16))
    resid_f = resid.astype(jnp.float32)
    totals_mid = jax.tree.map(lambda part: of_everyone(part, ROWS), group_sums(resid_f))
    mean_m, inverse_m = finish_norm(totals_mid, count, chans)
    normed = ((resid_f - mean_m) * inverse_m).astype(jnp.bfloat16)
    project = jnp.dot(normed, qkv_weight, preferred_element_type=jnp.float32).astype(jnp.bfloat16)
    head_dim = chans // HEADS
    scale = head_dim ** (-0.5)
    query = project[:, :chans].reshape(tokens, HEADS, head_dim)
    keys_here = project[:, chans : 2 * chans]
    values_here = project[:, 2 * chans :]
    keys_all, values_all = side_by_side((keys_here, values_here), ROWS, 0, 1)
    key_heads = keys_all.reshape(-1, HEADS, head_dim)
    value_heads = values_all.reshape(-1, HEADS, head_dim)
    scores = (
        jnp.einsum("qhd,khd->hqk", query, key_heads, preferred_element_type=jnp.float32) * scale
    )
    top = jnp.max(scores, axis=2, keepdims=True)
    weights = jnp.exp(scores - top)
    total = jnp.sum(weights, axis=2, keepdims=True)
    summed = jnp.einsum(
        "hqk,khd->hqd",
        weights.astype(jnp.bfloat16),
        value_heads,
        preferred_element_type=jnp.float32,
    )
    mixed = summed / total
    attended = mixed.transpose(1, 0, 2).reshape(tokens, chans).astype(jnp.bfloat16)
    output = resid_f + jnp.dot(attended, out_weight, preferred_element_type=jnp.float32)
    block = output.astype(jnp.bfloat16).reshape(1, rows_here, width, chans)
    particle_index = lax.axis_index("particle")
    source = lax.dynamic_index_in_dim(ancestors, particle_index, 0, keepdims=False)
    particle_count = ancestors.shape[0]
    wanted = ancestors == particle_index
    copies = jnp.broadcast_to(block, (particle_count,) + block.shape[1:])
    outgoing = jnp.where(wanted[:, None, None, None], copies, jnp.zeros_like(copies))
    incoming = lax.all_to_all(outgoing, "particle", split_axis=0, concat_axis=0, tiled=True)
    return lax.dynamic_index_in_dim(incoming, source, 0, keepdims=True)


def solution(mesh):
    split = Mesh(
        mesh.devices.reshape(mesh.shape["particle"], 4, 8), ("particle", "rows_0", "rows_1")
    )
    placed = (P("particle", ROWS, None, None), P(), P(), P(ROWS, None), P(), P(), P())
    return jax.shard_map(
        per_device,
        mesh=split,
        in_specs=placed,
        out_specs=P("particle", ROWS, None, None),
        check_vma=False,
    )
```

profile of v0, /device:TPU:1, one launch (start us, length us, event | category | flops | bytes accessed | tf_op | source)
XLA Modules:
  0.0 385.6 jit_solution(12511476286540781688)
XLA Ops:
  6.5 27.3 %all-gather.2 = bf16[4,180,640]{2,1,0:T(8,128)(2,1)} all-gather(bf16[1,180,640]{2,1,0:T(8,128)(2,1)} %bitcast.89), channel_id=2, replica_groups=mesh['particle'=16,'rows_0'=4,'rows_1'=8] {'rows_0'}, dimensions={0}, use_global_device_ids=true | all-gather | bytes 1152000 | tf_op jit(solution)/shard_map/all_gather | solution.py:43
  33.9 0.9 convert_reduce_fusion.1
  35.1 0.6 broadcast_in_dim.48
  35.7 9.3 %all-to-all-start = ((f32[32,1,32]{2,1,0:T(1,128)}), f32[32,1,32]{2,1,0:T(1,128)S(1)}, u32[]{:S(2)}, u32[]{:S(2)}) async-start(f32[32,1,32]{2,1,0:T(1,128)} %broadcast_in_dim.48), calls=%async_computation | async-start | bytes 32768 | tf_op jit(solution)/shard_map/all_to_all | solution.py:14
  45.2 10.8 %all-to-all-done = f32[32,1,32]{2,1,0:T(1,128)S(1)} async-done(((f32[32,1,32]{2,1,0:T(1,128)}), f32[32,1,32]{2,1,0:T(1,128)S(1)}, u32[]{:S(2)}, u32[]{:S(2)}) %all-to-all-start) | async-done | bytes 4128 | tf_op jit(solution)/shard_map/all_to_all | solution.py:14
  56.0 0.6 broadcast_in_dim.50
  56.6 3.8 all-to-all-start.1
  60.4 0.7 broadcast_add_fusion
  61.2 10.3 %all-to-all-done.1 = f32[32,1,32]{2,1,0:T(1,128)S(1)} async-done(((f32[32,1,32]{2,1,0:T(1,128)}), f32[32,1,32]{2,1,0:T(1,128)S(1)}, u32[]{:S(2)}, u32[]{:S(2)}) %all-to-all-start.1) | async-done | bytes 4128 | tf_op jit(solution)/shard_map/all_to_all | solution.py:14
  72.0 2.3 collective-permute-start
  74.4 1.3 collective-permute-start.1
  75.8 4.2 %collective-permute-done.1 = bf16[1,24,640]{2,1,0:T(8,128)(2,1)S(1)} collective-permute-done((bf16[1,24,640]{2,1,0:T(8,128)(2,1)S(1)}, bf16[1,24,640]{2,1,0:T(8,128)(2,1)S(1)}, u32[]{:S(2)}, u32[]{:S(2)}) %collective-permute-start.1) | collective-permute-done | bytes 30752 | tf_op jit(solution)/shard_map/ppermute | solution.py:29
  80.1 0.7 slice_dynamic-update-slice_fusion.5
  80.8 0.7 fusion.47
  81.5 0.7 slice_dynamic-update-slice_fusion.4
  82.2 0.7 slice_dynamic-update-slice_fusion.3
  82.8 0.8 constant_dynamic-update-slice_fusion
  83.6 0.7 slice_dynamic-update-slice_fusion.2
  84.3 0.7 slice_dynamic-update-slice_fusion.1
  85.0 0.7 fusion.46
  85.7 0.7 slice_dynamic-update-slice_fusion
  86.4 40.3 %all-gather.8.cloned.1.call-done = bf16[32,180,640]{2,1,0:T(8,128)(2,1)} async-done(((bf16[4,180,640]{2,1,0:T(8,128)(2,1)}), bf16[32,180,640]{2,1,0:T(8,128)(2,1)}) %all-gather.8.cloned.1.call-update) | async-done | bytes 7372816 | tf_op jit(solution)/shard_map/all_gather | solution.py:43
  126.7 6.9 %copy.32 = bf16[8,4,180,640]{3,2,0,1:T(8,128)(2,1)} copy(bf16[8,4,180,640]{3,2,1,0:T(8,128)(2,1)} %bitcast.84) | data formatting | bytes 14745600 | tf_op jit(solution)/shard_map/all_gather | solution.py:43
  133.6 8.8 %reshape_reshape.4 = bf16[5760,640]{1,0:T(8,128)(2,1)} reshape(bf16[4,8,180,640]{3,2,1,0:T(8,128)(2,1)} %bitcast.83) | data formatting | bytes 14745600 | tf_op jit(solution)/shard_map/reshape;reshape | solution.py:37
  142.4 4.8 %fusion.10 = bf16[96,640]{1,0:T(8,128)(2,1)S(1)} fusion(bf16[96,5760]{1,0:T(8,128)(2,1)} %bitcast.6, bf16[5760,640]{1,0:T(8,128)(2,1)} %reshape_reshape.4, bf16[96,640]{1,0:T(8,128)(2,1)S(1)} %bitcast.86), kind=kOutput, calls=%fused_computation.14 | convolution fusion | flops 707973120 | bytes 8724480 | tf_op jit(solution)/shard_map/dot_general | solution.py:101
  147.5 0.6 broadcast_in_dim.52
  148.1 9.9 %all-to-all-start.2 = ((f32[32,1,32]{2,1,0:T(1,128)}), f32[32,1,32]{2,1,0:T(1,128)S(1)}, u32[]{:S(2)}, u32[]{:S(2)}) async-start(f32[32,1,32]{2,1,0:T(1,128)} %broadcast_in_dim.52), calls=%async_computation.2 | async-start | bytes 32768 | tf_op jit(solution)/shard_map/all_to_all | solution.py:14
  158.2 10.8 %all-to-all-done.2 = f32[32,1,32]{2,1,0:T(1,128)S(1)} async-done(((f32[32,1,32]{2,1,0:T(1,128)}), f32[32,1,32]{2,1,0:T(1,128)S(1)}, u32[]{:S(2)}, u32[]{:S(2)}) %all-to-all-start.2) | async-done | bytes 4128 | tf_op jit(solution)/shard_map/all_to_all | solution.py:14
  169.0 0.6 broadcast_in_dim.54
  169.6 3.8 all-to-all-start.3
  173.4 0.2 all-gather.6.cloned.1.call-start
  173.7 10.7 %all-to-all-done.3 = f32[32,1,32]{2,1,0:T(1,128)S(1)} async-done(((f32[32,1,32]{2,1,0:T(1,128)}), f32[32,1,32]{2,1,0:T(1,128)S(1)}, u32[]{:S(2)}, u32[]{:S(2)}) %all-to-all-start.3) | async-done | bytes 4128 | tf_op jit(solution)/shard_map/all_to_all | solution.py:14
  184.8 0.5 convolution_convert_fusion
  185.3 0.7 concatenate.20
  186.1 0.2 copy.28
  186.3 129.1 %all-gather.6.cloned.1.call-done = bf16[3072,1280]{1,0:T(8,128)(2,1)} async-done(((bf16[96,1280]{1,0:T(8,128)(2,1)}), bf16[3072,1280]{1,0:T(8,128)(2,1)}) %all-gather.6.cloned.1.call-update) | async-done | bytes 7864336 | tf_op jit(solution)/shard_map/all_gather | solution.py:56
  315.4 5.5 %fusion.51 = (bf16[3072,640]{1,0:T(8,128)(2,1)}, bf16[3072,640]{1,0:T(8,128)(2,1)}) fusion(bf16[3072,1280]{1,0:T(8,128)(2,1)} %all-gather.6.cloned.1.call-done), kind=kLoop, calls=%fused_computation.77 | loop fusion | bytes 15728640 | tf_op jit(solution)/shard_map/slice | solution.py:58
  320.9 6.3 %copy.29 = bf16[3072,640]{0,1:T(8,128)(2,1)} copy(bf16[3072,640]{1,0:T(8,128)(2,1)} %get-tuple-element.9) | data formatting | bytes 7864320 | tf_op jit(solution)/shard_map/slice | solution.py:58
  327.1 6.3 %copy.30 = bf16[3072,640]{0,1:T(8,128)(2,1)} copy(bf16[3072,640]{1,0:T(8,128)(2,1)} %get-tuple-element.10) | data formatting | bytes 7864320 | tf_op jit(solution)/shard_map/slice | solution.py:58
  333.4 3.9 %multiply_reduce_fusion = (f32[10,96]{1,0:T(8,128)S(1)}, f32[10,96,3072]{2,1,0:T(8,128)S(1)}) fusion(bf16[96,10,64]{0,2,1:T(8,128)(2,1)S(1)} %bitcast.87, bf16[3072,10,64]{0,2,1:T(8,128)(2,1)} %bitcast.82), kind=kOutput, calls=%fused_computation.1 | convolution fusion | flops 383384640 | bytes 15855360 | tf_op jit(solution)/shard_map/qhd,khd->hqk/dot_general | solution.py:119
  337.3 2.1 fusion
  339.4 4.8 %fusion.14 = bf16[96,10,64]{0,2,1:T(8,128)(2,1)S(1)} fusion(bf16[3072,10,64]{0,2,1:T(8,128)(2,1)} %bitcast.85, f32[10,96,3072]{2,1,0:T(8,128)S(1)} %get-tuple-element.18, f32[10,96]{1,0:T(8,128)S(1)} %get-tuple-element.17, f32[96,10]{0,1:T(8,128)S(1)} %bitcast.95), kind=kOutput, calls=%fused_computation.16 | convolution fusion | flops 386457600 | bytes 15859200 | tf_op jit(solution)/shard_map/hqk,khd->hqd/dot_general | solution.py:124
  344.2 0.3 fusion.9
  344.5 1.5 broadcast_select_fusion
  346.0 5.4 %all-to-all-start.4 = ((bf16[16,4,24,640]{3,2,1,0:T(8,128)(2,1)}), bf16[16,4,24,640]{3,2,1,0:T(8,128)(2,1)}, u32[]{:S(2)}, u32[]{:S(2)}) async-start(bf16[16,4,24,640]{3,2,1,0:T(8,128)(2,1)} %broadcast_select_fusion), calls=%async_computation.4 | async-start | bytes 3932160 | tf_op jit(solution)/shard_map/all_to_all | solution.py:140
  351.4 0.6 dynamic_slice.8
  353.9 23.3 %all-to-all-done.4 = bf16[16,4,24,640]{3,2,1,0:T(8,128)(2,1)} async-done(((bf16[16,4,24,640]{3,2,1,0:T(8,128)(2,1)}), bf16[16,4,24,640]{3,2,1,0:T(8,128)(2,1)}, u32[]{:S(2)}, u32[]{:S(2)}) %all-to-all-start.4) | async-done | bytes 1966112 | tf_op jit(solution)/shard_map/all_to_all | solution.py:140
  377.2 1.6 constant_dynamic-slice_fusion
  (45 shorter events, 2.1 us)
Async XLA Ops:
  6.5 178.3 %copy-start = (bf16[640,1920]{1,0:T(8,128)(2,1)S(1)}, bf16[640,1920]{1,0:T(8,128)(2,1)}, u32[]{:S(2)}) copy-start(bf16[640,1920]{1,0:T(8,128)(2,1)} %param.11) | copy-start | bytes 7372804
  6.5 65.4 %copy-start.2 = (bf16[1,4,24,640]{3,2,1,0:T(8,128)(2,1)S(1)}, bf16[1,4,24,640]{3,2,1,0:T(8,128)(2,1)}, u32[]{:S(2)}) copy-start(bf16[1,4,24,640]{3,2,1,0:T(8,128)(2,1)} %param.7) | copy-start | bytes 368644
  6.5 65.4 %copy-start.4 = (f32[640]{0:T(1024)S(1)}, f32[640]{0:T(1024)}, u32[]{:S(2)}) copy-start(f32[640]{0:T(1024)} %param.9) | copy-start | bytes 7684
  6.5 120.1 %all-gather.8.cloned.1.call-start = ((), (), s32[]{:S(2)}) async-start(), calls=%async_computation.6 | async-start | bytes 8478720 | tf_op jit(solution)/shard_map/all_gather | solution.py:43
  35.7 20.3 %all-to-all-start = ((f32[32,1,32]{2,1,0:T(1,128)}), f32[32,1,32]{2,1,0:T(1,128)S(1)}, u32[]{:S(2)}, u32[]{:S(2)}) async-start(f32[32,1,32]{2,1,0:T(1,128)} %broadcast_in_dim.48), calls=%async_computation | async-start | bytes 32768 | tf_op jit(solution)/shard_map/all_to_all | solution.py:14
  56.6 14.9 %all-to-all-start.1 = ((f32[32,1,32]{2,1,0:T(1,128)}), f32[32,1,32]{2,1,0:T(1,128)S(1)}, u32[]{:S(2)}, u32[]{:S(2)}) async-start(f32[32,1,32]{2,1,0:T(1,128)} %broadcast_in_dim.50), calls=%async_computation.1 | async-start | bytes 32768 | tf_op jit(solution)/shard_map/all_to_all | solution.py:14
  72.0 3.8 collective-permute-start
  74.4 5.7 %collective-permute-start.1 = (bf16[1,24,640]{2,1,0:T(8,128)(2,1)S(1)}, bf16[1,24,640]{2,1,0:T(8,128)(2,1)S(1)}, u32[]{:S(2)}, u32[]{:S(2)}) collective-permute-start(bf16[1,24,640]{2,1,0:T(8,128)(2,1)S(1)} %get-tuple-element.12), channel_id=1, source_target_pairs={{1,0},{2,1},{3,2},{4,3},{5,4},{6,5},{7,6},{8,7},{9,8},{10,9},{11,1... | collective-permute-start | bytes 92168 | tf_op jit(solution)/shard_map/ppermute | solution.py:29
  147.2 38.8 %copy-start.5 = (s32[16]{0:T(128)S(1)}, s32[16]{0:T(128)}, u32[]{:S(2)}) copy-start(s32[16]{0:T(128)} %param.13) | copy-start | bytes 196
  148.1 20.9 %all-to-all-start.2 = ((f32[32,1,32]{2,1,0:T(1,128)}), f32[32,1,32]{2,1,0:T(1,128)S(1)}, u32[]{:S(2)}, u32[]{:S(2)}) async-start(f32[32,1,32]{2,1,0:T(1,128)} %broadcast_in_dim.52), calls=%async_computation.2 | async-start | bytes 32768 | tf_op jit(solution)/shard_map/all_to_all | solution.py:14
  169.6 14.8 %all-to-all-start.3 = ((f32[32,1,32]{2,1,0:T(1,128)}), f32[32,1,32]{2,1,0:T(1,128)S(1)}, u32[]{:S(2)}, u32[]{:S(2)}) async-start(f32[32,1,32]{2,1,0:T(1,128)} %broadcast_in_dim.54), calls=%async_computation.3 | async-start | bytes 32768 | tf_op jit(solution)/shard_map/all_to_all | solution.py:14
  173.4 141.9 %all-gather.6.cloned.1.call-start = ((), (), s32[]{:S(2)}) async-start(), calls=%async_computation.5 | async-start | bytes 8110080 | tf_op jit(solution)/shard_map/all_gather | solution.py:56
  339.4 4.8 %copy-start.3 = (bf16[640,640]{1,0:T(8,128)(2,1)S(1)}, bf16[640,640]{1,0:T(8,128)(2,1)}, u32[]{:S(2)}) copy-start(bf16[640,640]{1,0:T(8,128)(2,1)} %param.12) | copy-start | bytes 2457604
  344.5 34.3 %copy-start.1 = (bf16[640,1920]{1,0:T(8,128)(2,1)S(1)}, bf16[640,1920]{1,0:T(8,128)(2,1)}, u32[]{:S(2)}) copy-start(bf16[640,1920]{1,0:T(8,128)(2,1)} %param.11) | copy-start | bytes 7372804
  346.0 31.2 %all-to-all-start.4 = ((bf16[16,4,24,640]{3,2,1,0:T(8,128)(2,1)}), bf16[16,4,24,640]{3,2,1,0:T(8,128)(2,1)}, u32[]{:S(2)}, u32[]{:S(2)}) async-start(bf16[16,4,24,640]{3,2,1,0:T(8,128)(2,1)} %broadcast_select_fusion), calls=%async_computation.4 | async-start | bytes 3932160 | tf_op jit(solution)/shard_map/all_to_all | solution.py:140
Sparse Core Ops, SparseCore 0:
  34.0 92.5 all-gather.7
  186.2 129.1 all-gather.5
where the time goes:
time: 387 us; the launch traced here: 386 us
  waiting for transfers between devices  240 us (62%)
  local copies, waits for them, and re-layouts  44.5 us (11%)
  starting transfers between devices  36.1 us (9%)
  blocking collectives  27.3 us (7%)
  between operations  15.6 us (4%)
  matrix products  14.3 us (4%)
  other arithmetic  8.25 us (2%)
    all_gather x1, waiting for transfers between devices, side_by_side(): out, at, done = (lax.all_gather(both, axis, axis=dim, tiled=True), 0, [])  129 us
    all_to_all x4, waiting for transfers between devices, copy_for_each(): return lax.all_to_all(copies, axis, split_axis=0, concat_axis=0, tiled=True)  42.6 us
    all_gather x1, waiting for transfers between devices, all_blocks(): pieces = lax.all_gather(pieces, axes[k])  40.3 us
    all_gather x1, blocking collectives, all_blocks(): pieces = lax.all_gather(pieces, axes[k])  27.3 us
    all_to_all x4, starting transfers between devices, copy_for_each(): return lax.all_to_all(copies, axis, split_axis=0, concat_axis=0, tiled=True)  26.9 us
    all_to_all x1, waiting for transfers between devices, per_device(): lax.all_to_all(outgoing, 'particle', split_axis=0, concat_axis=0, tiled=T...  23.3 us
    slice x3, local copies, waits for them, and re-layouts, side_by_side(): done.append(lax.slice_in_dim(out, at, at + a.shape[along], axis=along))  18 us
    another operation x1, local copies, waits for them, and re-layouts, in_order(): pieces.reshape(*shape[:dim], shape[dim] * shape[dim + 1], *shape[dim + 2:])  8.82 us
  transfers between devices with their start and end apart: 9, of which 8 were waited for; matrix products, arithmetic and copies ran while one was open for 3% of the time, Pallas kernels for 0%

commit v1 on v0

v1 whole, which is shorter than its diff:
```python
import functools

import jax
import jax.numpy as jnp
from jax import lax
from jax.experimental import pallas as pl
from jax.experimental.pallas import tpu as pltpu
from jax.sharding import Mesh
from jax.sharding import PartitionSpec as P

HEADS = 10
GROUPS = 32
CHANS = 640
WIDTH = 24
ROWS_HERE = 4
TOKENS = ROWS_HERE * WIDTH
PARTICLES = 16
ROW_DEVS = 32
PER_GROUP = CHANS // GROUPS
SLICE = CHANS // PARTICLES
COUNT = ROWS_HERE * ROW_DEVS * WIDTH * PER_GROUP
LANES = 128
KERNEL_ROWS = 9 * CHANS // ROW_DEVS
QUERY_BLOCKS = 3
SLOT = TOKENS + 16

PART = ("x", "z_lo", "core")
CHIPS = ("x", "z_lo")
ROWS = ("z_hi", "y")

NT = (((1,), (1,)), ((), ()))
F32 = jnp.float32
BF16 = jnp.bfloat16
SMEM = pl.BlockSpec(memory_space=pltpu.SMEM)
VMEM = pl.BlockSpec(memory_space=pltpu.VMEM)


def call(kernel, out_shape, in_specs, flops, size, vmem=16, scratch=()):
    out_specs = jax.tree.map(lambda _: VMEM, out_shape)
    return pl.pallas_call(
        kernel,
        out_shape=out_shape,
        in_specs=in_specs,
        out_specs=out_specs,
        scratch_shapes=list(scratch),
        compiler_params=pltpu.CompilerParams(vmem_limit_bytes=vmem * 1024 * 1024),
        cost_estimate=pl.CostEstimate(flops=flops, bytes_accessed=size, transcendentals=0),
    )


def shaped(*shape, dtype=BF16):
    return jax.ShapeDtypeStruct(shape, dtype)


def iota(shape, dim):
    return lax.broadcasted_iota(jnp.int32, shape, dim)


def exact_dot(a, b):
    return jnp.dot(a, b, precision=lax.Precision.HIGHEST, preferred_element_type=F32)


def group_row(values):
    sums = jnp.sum(values, axis=0, keepdims=True)
    squares = jnp.sum(values * values, axis=0, keepdims=True)
    chan, lane = iota((CHANS, LANES), 0), iota((CHANS, LANES), 1)
    first = ((chan >= lane * PER_GROUP) & (chan < (lane + 1) * PER_GROUP)).astype(F32)
    other = lane - GROUPS
    second = ((chan >= other * PER_GROUP) & (chan < (other + 1) * PER_GROUP)).astype(F32)
    eight = lambda row: jnp.broadcast_to(row, (8, CHANS))
    return exact_dot(eight(sums), first) + exact_dot(eight(squares), second)


def mean_and_inverse(totals):
    lane, chan = iota((LANES, CHANS), 0), iota((LANES, CHANS), 1)
    first = ((chan >= lane * PER_GROUP) & (chan < (lane + 1) * PER_GROUP)).astype(F32)
    other = lane - GROUPS
    second = ((chan >= other * PER_GROUP) & (chan < (other + 1) * PER_GROUP)).astype(F32)
    mean = exact_dot(totals, first) * (1.0 / COUNT)
    square = exact_dot(totals, second) * (1.0 / COUNT)
    return mean, lax.rsqrt(square - mean * mean + 1e-05)


def sums_kernel(x_ref, out_ref):
    row = group_row(x_ref[...].astype(F32))
    out_ref[...] = jnp.broadcast_to(row[None], out_ref.shape)


def total_kernel(x_ref, out_ref):
    out_ref[...] = jnp.broadcast_to(jnp.sum(x_ref[...], axis=0)[None], out_ref.shape)


def pick_kernel(p_ref, w_ref, out_ref):
    row, col = iota((48, CHANS), 0), iota((48, CHANS), 1)
    chosen = ((col == row + p_ref[0] * SLICE) & (row < SLICE)).astype(F32).astype(BF16)
    picked = lax.dot_general(chosen, w_ref[...], NT, preferred_element_type=F32)
    out_ref[...] = jnp.zeros_like(out_ref)
    for r in range(ROW_DEVS):
        out_ref[r, :, :KERNEL_ROWS] = picked.astype(BF16)


PLACE = {1: 0, 0: 1, 2: 2}


def weights_kernel(x_ref, out_ref, flat_ref, tall_ref):
    flat_ref[...] = jnp.zeros_like(flat_ref)
    for r in range(ROW_DEVS):
        at = r * KERNEL_ROWS
        block, off = at // LANES, at % LANES
        piece = x_ref[r].astype(F32)
        wide = jnp.concatenate([piece, jnp.zeros((48, LANES), F32)], axis=1)
        if off:
            wide = pltpu.roll(wide, off, 1)
        spot = slice(block * LANES, (block + 3) * LANES)
        flat_ref[:, spot] = flat_ref[:, spot] + wide
    tall_ref[...] = jnp.zeros_like(tall_ref)
    for a in range(3):
        for b in range(3):
            tap = 3 * a + b
            top = a * LANES + PLACE[b] * SLICE
            tall_ref[top : top + SLICE, :] = flat_ref[:SLICE, tap * CHANS : (tap + 1) * CHANS]
    out_ref[...] = tall_ref[...].astype(BF16)


def conv_kernel(place_ref, own_ref, other_ref, totals_ref, scale_ref, shift_ref, w_ref,
                part_ref, up_ref, down_ref, gain_ref, bias_ref):
    mean, inverse = mean_and_inverse(totals_ref[:, 0, :])
    gain = inverse * (1.0 + scale_ref[...])
    gain_ref[...] = gain
    bias_ref[...] = shift_ref[...] - mean * gain
    p, core = place_ref[0], place_ref[1]
    row, col = iota((LANES, CHANS), 0), iota((LANES, CHANS), 1)
    chosen = ((col == row + p * SLICE) & (row < SLICE)).astype(F32).astype(BF16)
    weights = w_ref[...]
    each = 2
    for which, ref in ((0, own_ref), (1, other_ref)):
        first = core if which == 0 else 1 - core
        for step in range(PARTICLES // 2 // each):
            active, raw = [], []
            for k in range(each):
                j = step * each + k
                q = 2 * j + first
                x = ref[j]
                v = x.astype(F32) * gain_ref[pl.ds(q, 1), :] + bias_ref[pl.ds(q, 1), :]
                half = 0.5 * v
                active.append((half + half * jnp.tanh(half)).astype(BF16))
                raw.append(x)
            active = jnp.concatenate(active, axis=0)
            raw = jnp.concatenate(raw, axis=0)
            taps = lax.dot_general(active, weights, NT, preferred_element_type=F32)
            field = lax.dot_general(raw, chosen, NT, preferred_element_type=F32)
            for k in range(each):
                q = 2 * (step * each + k) + first
                rows = slice(k * TOKENS, (k + 1) * TOKENS)
                t0, t1, t2 = (taps[rows, n * LANES : (n + 1) * LANES] for n in range(3))
                base = t1 + field[rows]
                last = TOKENS - WIDTH
                part_ref[q, :WIDTH] = base[:WIDTH] + t2[WIDTH : 2 * WIDTH]
                part_ref[q, WIDTH:last] = (
                    base[WIDTH:last] + t0[: last - WIDTH] + t2[2 * WIDTH :]
                )
                part_ref[q, last:] = base[last:] + t0[last - WIDTH : last]
                up_ref[q] = t2[:WIDTH]
                down_ref[q] = t0[last:]


def finish_kernel(anc_ref, part_ref, above_ref, below_ref, out_ref):
    row, lane = iota((TOKENS, LANES), 0), iota((TOKENS, LANES), 1)
    at = lax.rem(row, WIDTH)
    lane_s = iota((32, LANES), 1)
    last = TOKENS - WIDTH
    for p in range(PARTICLES):
        q = anc_ref[p]
        full = jnp.concatenate(
            [
                part_ref[q, :WIDTH] + above_ref[q],
                part_ref[q, WIDTH:last],
                part_ref[q, last:] + below_ref[q],
            ],
            axis=0,
        )
        left = pltpu.roll(pltpu.roll(full, 1, 0), LANES - SLICE, 1)
        right = pltpu.roll(pltpu.roll(full, TOKENS - 1, 0), LANES - 2 * SLICE, 1)
        total = full + jnp.where(at == 0, 0.0, left) + jnp.where(at == WIDTH - 1, 0.0, right)
        total = jnp.where(lane < SLICE, total, 0.0)
        packed = total[:32]
        for t in (1, 2):
            packed = packed + pltpu.roll(total[32 * t : 32 * (t + 1)], SLICE * t, 1)
        out_ref[p] = packed.astype(BF16)


def gather_kernel(x_ref, resid_ref, out_ref, wide_ref):
    lane = iota((32, LANES), 1)
    for t in range(3):
        blocks = [jnp.zeros((32, LANES), F32) for _ in range(CHANS // LANES)]
        for p in range(PARTICLES):
            block, off = (p * SLICE) // LANES, (p * SLICE) % LANES
            turn = (off - t * SLICE) % LANES
            piece = x_ref[p].astype(F32)
            if turn:
                piece = pltpu.roll(piece, turn, 1)
            end = off + SLICE
            blocks[block] = jnp.where((lane >= off) & (lane < end), piece, blocks[block])
            if end > LANES:
                blocks[block + 1] = jnp.where(lane < end - LANES, piece, blocks[block + 1])
        for n, value in enumerate(blocks):
            wide_ref[32 * t : 32 * (t + 1), n * LANES : (n + 1) * LANES] = value
    wide = wide_ref[...]
    resid_ref[...] = wide.astype(BF16)
    out_ref[...] = jnp.broadcast_to(group_row(wide)[None], out_ref.shape)


def project_kernel(totals_ref, resid_ref, w_ref, out_ref, both_ref):
    mean, inverse = mean_and_inverse(jnp.sum(totals_ref[...], axis=0))
    normed = ((resid_ref[...].astype(F32) - mean[:1]) * inverse[:1]).astype(BF16)
    both_ref[...] = jnp.dot(normed, w_ref[...], preferred_element_type=F32)
    low = iota((TOKENS, LANES), 1) < 64
    low_s = iota((16, LANES), 1) < 64
    for pair in range(HEADS // 2):
        q, k, v = (
            both_ref[:, n * CHANS + pair * LANES : n * CHANS + (pair + 1) * LANES] for n in range(3)
        )
        q_turn, k_turn, v_turn = (pltpu.roll(x, 64, 1) for x in (q, k, v))
        mixed = (jnp.where(low, k, v_turn), jnp.where(low, k_turn, v))
        lows, highs = (q, q_turn), (q_turn, q)
        for side in range(2):
            keys_values = mixed[side].astype(BF16)
            for b in range(QUERY_BLOCKS):
                slot = (2 * pair + side) * QUERY_BLOCKS + b
                at = 32 * b
                two = jnp.where(low_s, lows[side][at : at + 16], highs[side][at + 16 : at + 32])
                out_ref[slot, :TOKENS] = keys_values
                out_ref[slot, TOKENS:] = two.astype(BF16)
    for slot in range(HEADS * QUERY_BLOCKS, ROW_DEVS):
        out_ref[slot] = jnp.zeros((SLOT, LANES), BF16)


def attend_kernel(x_ref, out_ref, keys_ref, ones_ref, query_ref, half_ref):
    low = iota((TOKENS, LANES), 1) < 64
    for r in range(ROW_DEVS):
        block = x_ref[r, :TOKENS]
        keys_ref[r * TOKENS : (r + 1) * TOKENS] = block
        ones_ref[r * TOKENS : (r + 1) * TOKENS] = jnp.where(low, jnp.ones_like(block), block)
        query_ref[r * 16 : (r + 1) * 16] = x_ref[r, TOKENS:].astype(F32)
    size = 256
    low_q = iota((size, LANES), 1) < 64
    factor = 0.125 * 1.4426950408889634
    for n in range(2):
        here = query_ref[n * size : (n + 1) * size]
        for side in range(2):
            turned = here if side == 0 else pltpu.roll(here, 64, 1)
            query = jnp.where(low_q, turned, 0.0).astype(BF16)
            scores = lax.dot_general(query, keys_ref[...], NT, preferred_element_type=F32)
            top = jnp.max(scores, axis=1, keepdims=True)
            weights = jnp.exp2((scores - top) * factor).astype(BF16)
            result = jnp.dot(weights, ones_ref[...], preferred_element_type=F32)
            other = pltpu.roll(result, 64, 1)
            if side == 0:
                half_ref[...] = other / result
            else:
                both = jnp.where(low_q, half_ref[...], result / other).astype(BF16)
                for r in range(size // 16):
                    out_ref[n * (size // 16) + r] = both[r * 16 : (r + 1) * 16]


def output_kernel(x_ref, resid_ref, w_ref, out_ref, wide_ref):
    low = iota((16, LANES), 1) < 64
    for pair in range(HEADS // 2):
        for b in range(QUERY_BLOCKS):
            first = x_ref[2 * pair * QUERY_BLOCKS + b].astype(F32)
            second = x_ref[(2 * pair + 1) * QUERY_BLOCKS + b].astype(F32)
            cols = slice(pair * LANES, (pair + 1) * LANES)
            at = 32 * b
            wide_ref[at : at + 16, cols] = jnp.where(low, first, pltpu.roll(second, 64, 1))
            wide_ref[at + 16 : at + 32, cols] = jnp.where(low, pltpu.roll(first, 64, 1), second)
    mixed = wide_ref[...].astype(BF16)
    product = jnp.dot(mixed, w_ref[...], preferred_element_type=F32)
    out_ref[...] = (resid_ref[...].astype(F32) + product).astype(BF16)


def exchange(values, axes):
    return lax.all_to_all(values, axes, split_axis=0, concat_axis=0, tiled=True)


def per_device(latent, ada_scale, ada_shift, conv_weight, qkv_weight, out_weight, ancestors):
    slab = latent.reshape(TOKENS, CHANS)
    particle = lax.axis_index(PART).astype(jnp.int32)
    core = lax.axis_index("core").astype(jnp.int32)
    where = jnp.stack([particle, core])

    sums = call(sums_kernel, shaped(ROW_DEVS, 8, LANES, dtype=F32), [VMEM], 10**6, 10**5)(slab)
    sums = exchange(sums, ROWS)
    totals = call(total_kernel, shaped(PARTICLES, 8, LANES, dtype=F32), [VMEM], 10**5, 10**5)(sums)
    totals = exchange(totals, PART)

    own = exchange(jnp.broadcast_to(slab[None], (PARTICLES // 2, TOKENS, CHANS)), CHIPS)
    other = lax.ppermute(own, "core", [(0, 1), (1, 0)])

    picked = call(pick_kernel, shaped(ROW_DEVS, 48, 256), [SMEM, VMEM], 10**7, 10**6)(
        where, conv_weight
    )
    picked = exchange(picked, ROWS)
    weights = call(
        weights_kernel,
        shaped(3 * LANES, CHANS),
        [VMEM],
        10**6,
        10**6,
        scratch=(
            pltpu.VMEM((48, 9 * CHANS + 2 * LANES), F32),
            pltpu.VMEM((3 * LANES, CHANS), F32),
        ),
    )(picked)

    edge = shaped(PARTICLES, WIDTH, LANES, dtype=F32)
    part, up, down = call(
        conv_kernel,
        [shaped(PARTICLES, TOKENS, LANES, dtype=F32), edge, edge],
        [SMEM] + [VMEM] * 6,
        2 * 10**9,
        4 * 10**6,
        vmem=32,
        scratch=(pltpu.VMEM((PARTICLES, CHANS), F32), pltpu.VMEM((PARTICLES, CHANS), F32)),
    )(where, own, other, totals, ada_scale[None], ada_shift[None], weights)
    above = lax.ppermute(down, ROWS, [(i, i + 1) for i in range(ROW_DEVS - 1)])
    below = lax.ppermute(up, ROWS, [(i + 1, i) for i in range(ROW_DEVS - 1)])
    pieces = call(
        finish_kernel, shaped(PARTICLES, 32, LANES), [SMEM] + [VMEM] * 3, 10**6, 10**6
    )(ancestors, part, above, below)
    pieces = exchange(pieces, PART)

    resid, sums = call(
        gather_kernel,
        [shaped(TOKENS, CHANS), shaped(ROW_DEVS, 8, LANES, dtype=F32)],
        [VMEM],
        10**6,
        10**6,
        scratch=(pltpu.VMEM((TOKENS, CHANS), F32),),
    )(pieces)
    sums = exchange(sums, ROWS)
    slots = call(
        project_kernel,
        shaped(ROW_DEVS, SLOT, LANES),
        [VMEM] * 3,
        3 * 10**8,
        4 * 10**6,
        scratch=(pltpu.VMEM((TOKENS, 3 * CHANS), F32),),
    )(sums, resid, qkv_weight)
    slots = exchange(slots, ROWS)
    rows = ROW_DEVS * TOKENS
    mixed = call(
        attend_kernel,
        shaped(ROW_DEVS, 16, LANES),
        [VMEM],
        2 * 10**9,
        2 * 10**6,
        vmem=40,
        scratch=(
            pltpu.VMEM((rows, LANES), BF16),
            pltpu.VMEM((rows, LANES), BF16),
            pltpu.VMEM((ROW_DEVS * 16, LANES), F32),
            pltpu.VMEM((256, LANES), F32),
        ),
    )(slots)
    mixed = exchange(mixed, ROWS)
    block = call(
        output_kernel,
        shaped(TOKENS, CHANS),
        [VMEM] * 3,
        10**8,
        10**6,
        scratch=(pltpu.VMEM((TOKENS, CHANS), F32),),
    )(mixed, resid, out_weight)
    return block.reshape(1, ROWS_HERE, WIDTH, CHANS)


def solution(mesh):
    split = Mesh(mesh.devices.reshape(4, 2, 2, 4, 8), PART + ROWS)
    placed = (P(PART, ROWS, None, None), P(), P(), P(ROWS, None), P(), P(), P())
    return jax.shard_map(
        per_device,
        mesh=split,
        in_specs=placed,
        out_specs=P(PART, ROWS, None, None),
        check_vma=False,
    )
```

time: 387 us -> 195 us (0.50)
  waiting for transfers between devices: 240 us -> 36.5 us
  blocking collectives: 27.3 us -> 108 us
  local copies, waits for them, and re-layouts: 44.5 us -> 1.96 us
  Pallas kernels: 0 us -> 15.9 us
  between operations: 15.6 us -> 0.13 us
  matrix products: 14.3 us -> 0 us
  other arithmetic: 8.25 us -> 0.07 us
  starting transfers between devices: 36.1 us -> 29.3 us
    all_gather x2 -> x0, waiting for transfers between devices: 169 us -> none  [the longest x1 129 us: side_by_side(): out, at, done = (lax.all_gather(both, axis, axis=dim, tiled=True), 0, [])]
    all_to_all x0 -> x5, blocking collectives: none -> 108 us  [exchange(): return lax.all_to_all(values, axes, split_axis=0, concat_axis=0, tiled=True)]
    all_to_all x5 -> x3, waiting for transfers between devices: 65.8 us -> 30.2 us  [exchange(): return lax.all_to_all(values, axes, split_axis=0, concat_axis=0, tiled=True)]
    all_gather x1 -> x0, blocking collectives: 27.3 us -> none  [all_blocks(): pieces = lax.all_gather(pieces, axes[k])]
    slice x6 -> x0, local copies, waits for them, and re-layouts: 18.2 us -> none  [the longest x3 18 us: side_by_side(): done.append(lax.slice_in_dim(out, at, at + a.shape[along], axis=along))]
    pallas_call x0 -> x10, Pallas kernels: none -> 15.9 us  [the longest x1 4.53 us: per_device(): call(attend_kernel, shaped(ROW_DEVS, 16, LANES), [VMEM], 2 * 10 ** 9, 2 *...]
    dot_general x5 -> x0, matrix products: 14.3 us -> none  [the longest x1 4.8 us: per_device(): jnp.dot(patches, whole_of(conv_weight, ROWS, (0, 1), 0), preferred_elemen...]
    all_to_all x5 -> x3, starting transfers between devices: 32.3 us -> 18.1 us  [exchange(): return lax.all_to_all(values, axes, split_axis=0, concat_axis=0, tiled=True)]
  transfers between devices with their start and end apart: 9 -> 6, of which waited for: 8 -> 5; matrix products, arithmetic and copies ran while one was open for 3% -> 0% of each run, Pallas kernels for 0% -> 1%
where the time goes in v1:
time: 195 us; the launch traced here: 192 us
  blocking collectives  108 us (55%)
  waiting for transfers between devices  36.5 us (19%)
  starting transfers between devices  29.3 us (15%)
  Pallas kernels  15.9 us (8%)
  local copies, waits for them, and re-layouts  1.96 us (1%)
    all_to_all x5, blocking collectives, exchange(): return lax.all_to_all(values, axes, split_axis=0, concat_axis=0, tiled=True)  108 us
    all_to_all x3, waiting for transfers between devices, exchange(): return lax.all_to_all(values, axes, split_axis=0, concat_axis=0, tiled=True)  30.2 us
    all_to_all x3, starting transfers between devices, exchange(): return lax.all_to_all(values, axes, split_axis=0, concat_axis=0, tiled=True)  18.1 us
    ppermute x1, starting transfers between devices, per_device(): other = lax.ppermute(own, 'core', [(0, 1), (1, 0)])  5.14 us
    ppermute x1, starting transfers between devices, per_device(): above = lax.ppermute(down, ROWS, [(i, i + 1) for i in range(ROW_DEVS - 1)])  4.81 us
    pallas_call x1, Pallas kernels, per_device(): call(attend_kernel, shaped(ROW_DEVS, 16, LANES), [VMEM], 2 * 10 ** 9, 2 *...  4.53 us
  transfers between devices with their start and end apart: 6, of which 5 were waited for; matrix products, arithmetic and copies ran while one was open for 0% of the time, Pallas kernels for 1%

profile of v1, /device:TPU:1, one launch (start us, length us, event | category | flops | bytes accessed | tf_op | source)
XLA Modules:
  0.0 192.1 jit_solution(5816279142696986637)
XLA Ops:
  0.0 0.0 copy-start.2
  0.0 0.9 copy-done.2
  0.9 0.0 copy-start.3
  0.9 0.6 shard_map.73
  1.5 27.9 %all_to_all.40.x_ref = f32[32,8,128]{2,1,0:T(8,128)S(1)} all-to-all(f32[32,8,128]{2,1,0:T(8,128)S(1)} %shard_map.73), channel_id=1, replica_groups=mesh['x'=4,'z_lo'=2,'core'=2,'z_hi'=4,'y'=8] {'z_hi','y'}, dimensions={0} | all-to-all | bytes 262144 | tf_op jit(solution)/shard_map/all_to_all | solution.py:282
  29.4 1.0 broadcast_in_dim.14
  30.4 0.0 copy-start.5
  30.4 0.0 copy-start.6
  30.4 5.0 %all-to-all-start = ((bf16[8,96,640]{2,1,0:T(8,128)(2,1)}), bf16[8,96,640]{2,1,0:T(8,128)(2,1)S(1)}, u32[]{:S(2)}, u32[]{:S(2)}) async-start(bf16[8,96,640]{2,1,0:T(8,128)(2,1)} %broadcast_in_dim.14), calls=%async_computation | async-start | bytes 1966080 | tf_op jit(solution)/shard_map/all_to_all | solution.py:282
  35.4 0.1 pad_add_fusion.p_ref.place_ref
  35.5 0.0 copy-done.3
  35.5 1.8 shard_map.75
  37.3 10.9 %all-to-all-done.own_ref = bf16[8,96,640]{2,1,0:T(8,128)(2,1)S(1)} async-done(((bf16[8,96,640]{2,1,0:T(8,128)(2,1)}), bf16[8,96,640]{2,1,0:T(8,128)(2,1)S(1)}, u32[]{:S(2)}, u32[]{:S(2)}) %all-to-all-start) | async-done | bytes 983072 | tf_op jit(solution)/shard_map/all_to_all | solution.py:282
  48.2 3.9 %all-to-all-start.3 = ((bf16[32,48,256]{2,1,0:T(8,128)(2,1)}), bf16[32,48,256]{2,1,0:T(8,128)(2,1)S(1)}, u32[]{:S(2)}, u32[]{:S(2)}) async-start(bf16[32,48,256]{2,1,0:T(8,128)(2,1)} %shard_map.75), calls=%async_computation.3 | async-start | bytes 1572864 | tf_op jit(solution)/shard_map/all_to_all | solution.py:282
  52.1 5.1 %collective-permute-start = (bf16[8,96,640]{2,1,0:T(8,128)(2,1)S(1)}, bf16[8,96,640]{2,1,0:T(8,128)(2,1)S(1)}, u32[]{:S(2)}, u32[]{:S(2)}) collective-permute-start(bf16[8,96,640]{2,1,0:T(8,128)(2,1)S(1)} %all-to-all-done.own_ref), channel_id=1, source_target_pairs={{0,32},{32,0},{1,33},{33,1},{2,34},{34,2},{3,35},{35,3},{4,36},{36... | collective-permute-start | bytes 2949128 | tf_op jit(solution)/shard_map/ppermute | solution.py:297
  57.3 0.7 shard_map.74
  57.9 13.8 %all-to-all-done.3.x_ref = bf16[32,48,256]{2,1,0:T(8,128)(2,1)S(1)} async-done(((bf16[32,48,256]{2,1,0:T(8,128)(2,1)}), bf16[32,48,256]{2,1,0:T(8,128)(2,1)S(1)}, u32[]{:S(2)}, u32[]{:S(2)}) %all-to-all-start.3) | async-done | bytes 786464 | tf_op jit(solution)/shard_map/all_to_all | solution.py:282
  71.7 9.1 %all-to-all-start.2 = ((f32[16,8,128]{2,1,0:T(8,128)}), f32[16,8,128]{2,1,0:T(8,128)S(1)}, u32[]{:S(2)}, u32[]{:S(2)}) async-start(f32[16,8,128]{2,1,0:T(8,128)} %shard_map.74), calls=%async_computation.2 | async-start | bytes 131072 | tf_op jit(solution)/shard_map/all_to_all | solution.py:282
  80.9 0.0 copy-done.5
  80.9 0.0 copy-done.6
  80.9 0.3 shard_map.76.w_ref
  81.2 0.0 copy-start.4
  81.2 5.5 %all-to-all-done.2.totals_ref = f32[16,8,128]{2,1,0:T(8,128)S(1)} async-done(((f32[16,8,128]{2,1,0:T(8,128)}), f32[16,8,128]{2,1,0:T(8,128)S(1)}, u32[]{:S(2)}, u32[]{:S(2)}) %all-to-all-start.2) | async-done | bytes 65568 | tf_op jit(solution)/shard_map/all_to_all | solution.py:282
  86.7 0.0 collective-permute-done.other_ref
  86.7 0.0 copy-start
  86.7 3.3 %shard_map.77 = (f32[16,96,128]{2,1,0:T(8,128)S(1)}, f32[16,24,128]{2,1,0:T(8,128)S(1)}, f32[16,24,128]{2,1,0:T(8,128)S(1)}) custom-call(s32[2]{0:T(128)S(1)} %pad_add_fusion.p_ref.place_ref, bf16[8,96,640]{2,1,0:T(8,128)(2,1)S(1)} %all-to-all-done.own_ref, bf16[8,96,640]{2,1,0:T(8,128)(2,1)S(1)} %collective-permute-done.other_ref, ...), custom_call_target="tpu_custom_call" | custom-call | flops 2000000000 | bytes 4000000 | tf_op jit(solution)/shard_map/pallas_call | solution.py:316
  90.0 4.8 %collective-permute-start.1 = (f32[16,24,128]{2,1,0:T(8,128)S(1)}, f32[16,24,128]{2,1,0:T(8,128)S(1)}, u32[]{:S(2)}, u32[]{:S(2)}) collective-permute-start(f32[16,24,128]{2,1,0:T(8,128)S(1)} %get-tuple-element.11), channel_id=1, source_target_pairs={{0,1},{1,2},{2,3},{3,4},{4,5},{5,6},{6,7},{7,8},{8,9},{9,10},{10,1... | collective-permute-start | bytes 589832 | tf_op jit(solution)/shard_map/ppermute | solution.py:325
  94.8 1.3 collective-permute-start.2
  96.1 2.5 %collective-permute-done.1.above_ref = f32[16,24,128]{2,1,0:T(8,128)S(1)} collective-permute-done((f32[16,24,128]{2,1,0:T(8,128)S(1)}, f32[16,24,128]{2,1,0:T(8,128)S(1)}, u32[]{:S(2)}, u32[]{:S(2)}) %collective-permute-start.1) | collective-permute-done | bytes 196640 | tf_op jit(solution)/shard_map/ppermute | solution.py:325
  98.6 3.8 %collective-permute-done.2.below_ref = f32[16,24,128]{2,1,0:T(8,128)S(1)} collective-permute-done((f32[16,24,128]{2,1,0:T(8,128)S(1)}, f32[16,24,128]{2,1,0:T(8,128)S(1)}, u32[]{:S(2)}, u32[]{:S(2)}) %collective-permute-start.2) | collective-permute-done | bytes 196640 | tf_op jit(solution)/shard_map/ppermute | solution.py:326
  102.4 0.0 copy-done.4
  102.4 2.0 %shard_map.78 = bf16[16,32,128]{2,1,0:T(8,128)(2,1)S(1)} custom-call(s32[16]{0:T(128)S(1)} %copy-done.4, f32[16,96,128]{2,1,0:T(8,128)S(1)} %get-tuple-element.10.part_ref, f32[16,24,128]{2,1,0:T(8,128)S(1)} %collective-permute-done.1.above_ref, f32[16,24,128]{2,1,0:T(8,128)S(1)} %collective-permute-done.2.below_ref), custom_call_target="tpu_custom_call" | custom-call | flops 1000000 | bytes 1000000 | tf_op jit(solution)/shard_map/pallas_call | solution.py:327
  104.4 10.2 %all_to_all.41.x_ref = bf16[16,32,128]{2,1,0:T(8,128)(2,1)S(1)} all-to-all(bf16[16,32,128]{2,1,0:T(8,128)(2,1)S(1)} %shard_map.78), channel_id=1, replica_groups=mesh['x'=4,'z_lo'=2,'core'=2,'z_hi'=4,'y'=8] {'x','z_lo','core'}, dimensions={0} | all-to-all | bytes 262144 | tf_op jit(solution)/shard_map/all_to_all | solution.py:282
  114.6 0.7 shard_map.79
  115.4 23.1 %all_to_all.42.totals_ref = f32[32,8,128]{2,1,0:T(8,128)S(1)} all-to-all(f32[32,8,128]{2,1,0:T(8,128)S(1)} %get-tuple-element.13), channel_id=1, replica_groups=mesh['x'=4,'z_lo'=2,'core'=2,'z_hi'=4,'y'=8] {'z_hi','y'}, dimensions={0} | all-to-all | bytes 262144 | tf_op jit(solution)/shard_map/all_to_all | solution.py:282
  138.4 0.0 copy-done
  138.4 1.1 shard_map.80
  139.6 26.5 %all_to_all.43.x_ref = bf16[32,112,128]{2,1,0:T(8,128)(2,1)S(1)} all-to-all(bf16[32,112,128]{2,1,0:T(8,128)(2,1)S(1)} %shard_map.80), channel_id=1, replica_groups=mesh['x'=4,'z_lo'=2,'core'=2,'z_hi'=4,'y'=8] {'z_hi','y'}, dimensions={0} | all-to-all | bytes 1835008 | tf_op jit(solution)/shard_map/all_to_all | solution.py:282
  166.1 0.0 copy-start.1
  166.1 4.5 %shard_map.81 = bf16[32,16,128]{2,1,0:T(8,128)(2,1)S(1)} custom-call(bf16[32,112,128]{2,1,0:T(8,128)(2,1)S(1)} %all_to_all.43.x_ref), custom_call_target="tpu_custom_call" | custom-call | flops 2000000000 | bytes 2000000 | tf_op jit(solution)/shard_map/pallas_call | solution.py:351
  170.6 20.4 %all_to_all.44.x_ref = bf16[32,16,128]{2,1,0:T(8,128)(2,1)S(1)} all-to-all(bf16[32,16,128]{2,1,0:T(8,128)(2,1)S(1)} %shard_map.81), channel_id=1, replica_groups=mesh['x'=4,'z_lo'=2,'core'=2,'z_hi'=4,'y'=8] {'z_hi','y'}, dimensions={0} | all-to-all | bytes 262144 | tf_op jit(solution)/shard_map/all_to_all | solution.py:282
  191.1 0.0 copy-done.1
  191.1 1.0 shard_map.82
  (2 shorter events, 0.0 us)
Async XLA Ops:
  0.0 0.9 copy-start.2
  0.9 34.6 %copy-start.3 = (bf16[180,640]{1,0:T(8,128)(2,1)S(1)}, bf16[180,640]{1,0:T(8,128)(2,1)}, u32[]{:S(2)}) copy-start(bf16[180,640]{1,0:T(8,128)(2,1)} %w_ref.3) | copy-start | bytes 691204
  30.4 50.5 %copy-start.5 = (f32[640]{0:T(1024)S(1)}, f32[640]{0:T(1024)}, u32[]{:S(2)}) copy-start(f32[640]{0:T(1024)} %param.8) | copy-start | bytes 7684
  30.4 50.5 %copy-start.6 = (f32[640]{0:T(1024)S(1)}, f32[640]{0:T(1024)}, u32[]{:S(2)}) copy-start(f32[640]{0:T(1024)} %param.9) | copy-start | bytes 7684
  30.4 17.8 %all-to-all-start = ((bf16[8,96,640]{2,1,0:T(8,128)(2,1)}), bf16[8,96,640]{2,1,0:T(8,128)(2,1)S(1)}, u32[]{:S(2)}, u32[]{:S(2)}) async-start(bf16[8,96,640]{2,1,0:T(8,128)(2,1)} %broadcast_in_dim.14), calls=%async_computation | async-start | bytes 1966080 | tf_op jit(solution)/shard_map/all_to_all | solution.py:282
  48.2 23.5 %all-to-all-start.3 = ((bf16[32,48,256]{2,1,0:T(8,128)(2,1)}), bf16[32,48,256]{2,1,0:T(8,128)(2,1)S(1)}, u32[]{:S(2)}, u32[]{:S(2)}) async-start(bf16[32,48,256]{2,1,0:T(8,128)(2,1)} %shard_map.75), calls=%async_computation.3 | async-start | bytes 1572864 | tf_op jit(solution)/shard_map/all_to_all | solution.py:282
  52.1 34.6 %collective-permute-start = (bf16[8,96,640]{2,1,0:T(8,128)(2,1)S(1)}, bf16[8,96,640]{2,1,0:T(8,128)(2,1)S(1)}, u32[]{:S(2)}, u32[]{:S(2)}) collective-permute-start(bf16[8,96,640]{2,1,0:T(8,128)(2,1)S(1)} %all-to-all-done.own_ref), channel_id=1, source_target_pairs={{0,32},{32,0},{1,33},{33,1},{2,34},{34,2},{3,35},{35,3},{4,36},{36... | collective-permute-start | bytes 2949128 | tf_op jit(solution)/shard_map/ppermute | solution.py:297
  71.7 14.9 %all-to-all-start.2 = ((f32[16,8,128]{2,1,0:T(8,128)}), f32[16,8,128]{2,1,0:T(8,128)S(1)}, u32[]{:S(2)}, u32[]{:S(2)}) async-start(f32[16,8,128]{2,1,0:T(8,128)} %shard_map.74), calls=%async_computation.2 | async-start | bytes 131072 | tf_op jit(solution)/shard_map/all_to_all | solution.py:282
  81.2 21.3 %copy-start.4 = (s32[16]{0:T(128)S(1)}, s32[16]{0:T(128)}, u32[]{:S(2)}) copy-start(s32[16]{0:T(128)} %anc_ref.1) | copy-start | bytes 196
  86.7 51.8 %copy-start = (bf16[640,1920]{1,0:T(8,128)(2,1)S(1)}, bf16[640,1920]{1,0:T(8,128)(2,1)}, u32[]{:S(2)}) copy-start(bf16[640,1920]{1,0:T(8,128)(2,1)} %w_ref.4) | copy-start | bytes 7372804
  90.0 8.6 %collective-permute-start.1 = (f32[16,24,128]{2,1,0:T(8,128)S(1)}, f32[16,24,128]{2,1,0:T(8,128)S(1)}, u32[]{:S(2)}, u32[]{:S(2)}) collective-permute-start(f32[16,24,128]{2,1,0:T(8,128)S(1)} %get-tuple-element.11), channel_id=1, source_target_pairs={{0,1},{1,2},{2,3},{3,4},{4,5},{5,6},{6,7},{7,8},{8,9},{9,10},{10,1... | collective-permute-start | bytes 589832 | tf_op jit(solution)/shard_map/ppermute | solution.py:325
  94.8 7.6 %collective-permute-start.2 = (f32[16,24,128]{2,1,0:T(8,128)S(1)}, f32[16,24,128]{2,1,0:T(8,128)S(1)}, u32[]{:S(2)}, u32[]{:S(2)}) collective-permute-start(f32[16,24,128]{2,1,0:T(8,128)S(1)} %get-tuple-element.12), channel_id=1, source_target_pairs={{1,0},{2,1},{3,2},{4,3},{5,4},{6,5},{7,6},{8,7},{9,8},{10,9},{11,1... | collective-permute-start | bytes 589832 | tf_op jit(solution)/shard_map/ppermute | solution.py:326
  166.1 25.0 %copy-start.1 = (bf16[640,640]{1,0:T(8,128)(2,1)S(1)}, bf16[640,640]{1,0:T(8,128)(2,1)}, u32[]{:S(2)}) copy-start(bf16[640,640]{1,0:T(8,128)(2,1)} %w_ref.5) | copy-start | bytes 2457604

commit v2 on v1

--- a/solution.py
+++ b/solution.py
@@ -21,11 +21,11 @@
 COUNT = ROWS_HERE * ROW_DEVS * WIDTH * PER_GROUP
 LANES = 128
 KERNEL_ROWS = 9 * CHANS // ROW_DEVS
+TAIL = KERNEL_ROWS - LANES
 QUERY_BLOCKS = 3
 SLOT = TOKENS + 16
 
 PART = ("x", "z_lo", "core")
-CHIPS = ("x", "z_lo")
 ROWS = ("z_hi", "y")
 
 NT = (((1,), (1,)), ((), ()))
@@ -81,22 +81,38 @@
     return mean, lax.rsqrt(square - mean * mean + 1e-05)
 
 
-def sums_kernel(x_ref, out_ref):
-    row = group_row(x_ref[...].astype(F32))
+def thirds(value):
+    parts = []
+    for _ in range(3):
+        top = value.astype(BF16).astype(F32)
+        parts.append(top)
+        value = value - top
+    return parts
+
+
+def pick_kernel(place_ref, x_ref, w_ref, out_ref):
+    row, col = iota((48, CHANS), 0), iota((48, CHANS), 1)
+    chosen = ((col == row + place_ref[0] * SLICE) & (row < SLICE)).astype(F32).astype(BF16)
+    picked = lax.dot_general(chosen, w_ref[...], NT, preferred_element_type=F32)
+    head = picked[:, :LANES]
+    rest = jnp.concatenate([picked[:, LANES:], jnp.zeros((48, LANES - TAIL), F32)], axis=1)
+    turned = pltpu.roll(pltpu.roll(rest, 48 - 20, 0), 64, 1)
+    sums = thirds(group_row(x_ref[...].astype(F32)))
+    row, lane = iota((24, LANES), 0), iota((24, LANES), 1)
+    low = jnp.where(lane < 64, rest[:24], turned[:24])
+    for n in range(3):
+        low = jnp.where(row == 20 + n, sums[n][:1], low)
+    low = jnp.where(row == 23, 0.0, low)
+    slot = jnp.concatenate([head[:SLICE], low], axis=0).astype(BF16)
+    out_ref[...] = jnp.broadcast_to(slot[None], out_ref.shape)
+
+
+def total_kernel(x_ref, out_ref):
+    total = jnp.zeros((16, LANES), F32)
+    for r in range(ROW_DEVS):
+        total = total + x_ref[r, 48:64].astype(F32)
+    row = total[12:13] + total[13:14] + total[14:15]
     out_ref[...] = jnp.broadcast_to(row[None], out_ref.shape)
-
-
-def total_kernel(x_ref, out_ref):
-    out_ref[...] = jnp.broadcast_to(jnp.sum(x_ref[...], axis=0)[None], out_ref.shape)
-
-
-def pick_kernel(p_ref, w_ref, out_ref):
-    row, col = iota((48, CHANS), 0), iota((48, CHANS), 1)
-    chosen = ((col == row + p_ref[0] * SLICE) & (row < SLICE)).astype(F32).astype(BF16)
-    picked = lax.dot_general(chosen, w_ref[...], NT, preferred_element_type=F32)
-    out_ref[...] = jnp.zeros_like(out_ref)
-    for r in range(ROW_DEVS):
-        out_ref[r, :, :KERNEL_ROWS] = picked.astype(BF16)
 
 
 PLACE = {1: 0, 0: 1, 2: 2}
@@ -104,11 +120,15 @@
 
 def weights_kernel(x_ref, out_ref, flat_ref, tall_ref):
     flat_ref[...] = jnp.zeros_like(flat_ref)
+    row, lane = iota((SLICE, LANES), 0), iota((SLICE, LANES), 1)
     for r in range(ROW_DEVS):
         at = r * KERNEL_ROWS
         block, off = at // LANES, at % LANES
-        piece = x_ref[r].astype(F32)
-        wide = jnp.concatenate([piece, jnp.zeros((48, LANES), F32)], axis=1)
+        slot = x_ref[r].astype(F32)
+        low = jnp.concatenate([slot[SLICE:], jnp.zeros((16, LANES), F32)], axis=0)
+        rest = jnp.where(row < 20, low, pltpu.roll(pltpu.roll(low, 20, 0), 64, 1))
+        rest = jnp.where(lane < TAIL, rest, 0.0)
+        wide = jnp.concatenate([slot[:SLICE], rest, jnp.zeros((SLICE, LANES), F32)], axis=1)
         if off:
             wide = pltpu.roll(wide, off, 1)
         spot = slice(block * LANES, (block + 3) * LANES)
@@ -118,75 +138,108 @@
         for b in range(3):
             tap = 3 * a + b
             top = a * LANES + PLACE[b] * SLICE
-            tall_ref[top : top + SLICE, :] = flat_ref[:SLICE, tap * CHANS : (tap + 1) * CHANS]
+            tall_ref[top : top + SLICE, :] = flat_ref[:, tap * CHANS : (tap + 1) * CHANS]
     out_ref[...] = tall_ref[...].astype(BF16)
 
 
-def conv_kernel(place_ref, own_ref, other_ref, totals_ref, scale_ref, shift_ref, w_ref,
-                part_ref, up_ref, down_ref, gain_ref, bias_ref):
+def gain_and_bias(totals_ref, scale_ref, shift_ref):
     mean, inverse = mean_and_inverse(totals_ref[:, 0, :])
     gain = inverse * (1.0 + scale_ref[...])
-    gain_ref[...] = gain
-    bias_ref[...] = shift_ref[...] - mean * gain
-    p, core = place_ref[0], place_ref[1]
+    return gain, shift_ref[...] - mean * gain
+
+
+def silu(v):
+    half = 0.5 * v
+    return (half + half * jnp.tanh(half)).astype(BF16)
+
+
+def across(full):
+    rows = full.shape[0]
+    at = lax.rem(iota((rows, LANES), 0), WIDTH)
+    left = pltpu.roll(pltpu.roll(full, 1, 0), LANES - SLICE, 1)
+    right = pltpu.roll(pltpu.roll(full, rows - 1, 0), LANES - 2 * SLICE, 1)
+    total = full + jnp.where(at == 0, 0.0, left) + jnp.where(at == WIDTH - 1, 0.0, right)
+    return jnp.where(iota((rows, LANES), 1) < SLICE, total, 0.0)
+
+
+def packed(value):
+    n = value.shape[0] // 3
+    out = value[:n]
+    for t in (1, 2):
+        out = out + pltpu.roll(value[n * t : n * (t + 1)], SLICE * t, 1)
+    return out
+
+
+def unpacked(value):
+    return jnp.concatenate(
+        [value] + [pltpu.roll(value, LANES - SLICE * t, 1) for t in (1, 2)], axis=0
+    )
+
+
+def edge_kernel(x_ref, totals_ref, scale_ref, shift_ref, w_ref, up_ref, down_ref):
+    gain, bias = gain_and_bias(totals_ref, scale_ref, shift_ref)
+    for rows, tap, ref in (
+        (slice(0, WIDTH), 2, up_ref),
+        (slice(TOKENS - WIDTH, TOKENS), 0, down_ref),
+    ):
+        active = []
+        for q in range(PARTICLES):
+            x = x_ref[q].astype(F32)[rows]
+            active.append(silu(x * gain[q : q + 1] + bias[q : q + 1]))
+        active = jnp.concatenate(active, axis=0)
+        weights = w_ref[tap * LANES : (tap + 1) * LANES, :]
+        full = lax.dot_general(active, weights, NT, preferred_element_type=F32)
+        full = across(full)
+        for q in range(PARTICLES):
+            ref[q] = packed(full[q * WIDTH : (q + 1) * WIDTH])
+
+
+def conv_kernel(place_ref, x_ref, totals_ref, scale_ref, shift_ref, w_ref, part_ref):
+    gain, bias = gain_and_bias(totals_ref, scale_ref, shift_ref)
     row, col = iota((LANES, CHANS), 0), iota((LANES, CHANS), 1)
-    chosen = ((col == row + p * SLICE) & (row < SLICE)).astype(F32).astype(BF16)
+    chosen = ((col == row + place_ref[0] * SLICE) & (row < SLICE)).astype(F32).astype(BF16)
     weights = w_ref[...]
     each = 2
-    for which, ref in ((0, own_ref), (1, other_ref)):
-        first = core if which == 0 else 1 - core
-        for step in range(PARTICLES // 2 // each):
-            active, raw = [], []
-            for k in range(each):
-                j = step * each + k
-                q = 2 * j + first
-                x = ref[j]
-                v = x.astype(F32) * gain_ref[pl.ds(q, 1), :] + bias_ref[pl.ds(q, 1), :]
-                half = 0.5 * v
-                active.append((half + half * jnp.tanh(half)).astype(BF16))
-                raw.append(x)
-            active = jnp.concatenate(active, axis=0)
-            raw = jnp.concatenate(raw, axis=0)
-            taps = lax.dot_general(active, weights, NT, preferred_element_type=F32)
-            field = lax.dot_general(raw, chosen, NT, preferred_element_type=F32)
-            for k in range(each):
-                q = 2 * (step * each + k) + first
-                rows = slice(k * TOKENS, (k + 1) * TOKENS)
-                t0, t1, t2 = (taps[rows, n * LANES : (n + 1) * LANES] for n in range(3))
-                base = t1 + field[rows]
-                last = TOKENS - WIDTH
-                part_ref[q, :WIDTH] = base[:WIDTH] + t2[WIDTH : 2 * WIDTH]
-                part_ref[q, WIDTH:last] = (
-                    base[WIDTH:last] + t0[: last - WIDTH] + t2[2 * WIDTH :]
-                )
-                part_ref[q, last:] = base[last:] + t0[last - WIDTH : last]
-                up_ref[q] = t2[:WIDTH]
-                down_ref[q] = t0[last:]
+    last = TOKENS - WIDTH
+    for step in range(PARTICLES // each):
+        active, raw = [], []
+        for q in range(step * each, (step + 1) * each):
+            x = x_ref[q]
+            raw.append(x)
+            active.append(silu(x.astype(F32) * gain[q : q + 1] + bias[q : q + 1]))
+        active = jnp.concatenate(active, axis=0)
+        raw = jnp.concatenate(raw, axis=0)
+        taps = lax.dot_general(active, weights, NT, preferred_element_type=F32)
+        field = lax.dot_general(raw, chosen, NT, preferred_element_type=F32)
+        for k in range(each):
+            rows = slice(k * TOKENS, (k + 1) * TOKENS)
+            t0, t1, t2 = (taps[rows, n * LANES : (n + 1) * LANES] for n in range(3))
+            base = t1 + field[rows]
+            full = jnp.concatenate(
+                [
+                    base[:WIDTH] + t2[WIDTH : 2 * WIDTH],
+                    base[WIDTH:last] + t0[: last - WIDTH] + t2[2 * WIDTH :],
+                    base[last:] + t0[last - WIDTH : last],
+                ],
+                axis=0,
+            )
+            part_ref[step * each + k] = across(full)
 
 
 def finish_kernel(anc_ref, part_ref, above_ref, below_ref, out_ref):
-    row, lane = iota((TOKENS, LANES), 0), iota((TOKENS, LANES), 1)
-    at = lax.rem(row, WIDTH)
-    lane_s = iota((32, LANES), 1)
     last = TOKENS - WIDTH
+    lane = iota((TOKENS, LANES), 1)
     for p in range(PARTICLES):
         q = anc_ref[p]
-        full = jnp.concatenate(
+        total = jnp.concatenate(
             [
-                part_ref[q, :WIDTH] + above_ref[q],
+                part_ref[q, :WIDTH] + unpacked(above_ref[q]),
                 part_ref[q, WIDTH:last],
-                part_ref[q, last:] + below_ref[q],
+                part_ref[q, last:] + unpacked(below_ref[q]),
             ],
             axis=0,
         )
-        left = pltpu.roll(pltpu.roll(full, 1, 0), LANES - SLICE, 1)
-        right = pltpu.roll(pltpu.roll(full, TOKENS - 1, 0), LANES - 2 * SLICE, 1)
-        total = full + jnp.where(at == 0, 0.0, left) + jnp.where(at == WIDTH - 1, 0.0, right)
-        total = jnp.where(lane < SLICE, total, 0.0)
-        packed = total[:32]
-        for t in (1, 2):
-            packed = packed + pltpu.roll(total[32 * t : 32 * (t + 1)], SLICE * t, 1)
-        out_ref[p] = packed.astype(BF16)
+        out_ref[p] = packed(jnp.where(lane < SLICE, total, 0.0)).astype(BF16)
 
 
 def gather_kernel(x_ref, resid_ref, out_ref, wide_ref):
@@ -284,22 +337,16 @@
 
 def per_device(latent, ada_scale, ada_shift, conv_weight, qkv_weight, out_weight, ancestors):
     slab = latent.reshape(TOKENS, CHANS)
-    particle = lax.axis_index(PART).astype(jnp.int32)
-    core = lax.axis_index("core").astype(jnp.int32)
-    where = jnp.stack([particle, core])
-
-    sums = call(sums_kernel, shaped(ROW_DEVS, 8, LANES, dtype=F32), [VMEM], 10**6, 10**5)(slab)
-    sums = exchange(sums, ROWS)
-    totals = call(total_kernel, shaped(PARTICLES, 8, LANES, dtype=F32), [VMEM], 10**5, 10**5)(sums)
-    totals = exchange(totals, PART)
-
-    own = exchange(jnp.broadcast_to(slab[None], (PARTICLES // 2, TOKENS, CHANS)), CHIPS)
-    other = lax.ppermute(own, "core", [(0, 1), (1, 0)])
-
-    picked = call(pick_kernel, shaped(ROW_DEVS, 48, 256), [SMEM, VMEM], 10**7, 10**6)(
-        where, conv_weight
+    place = lax.axis_index(PART).astype(jnp.int32)[None]
+
+    slabs = lax.all_gather(slab, PART)
+
+    picked = call(pick_kernel, shaped(ROW_DEVS, 64, LANES), [SMEM, VMEM, VMEM], 10**7, 10**6)(
+        place, slab, conv_weight
     )
     picked = exchange(picked, ROWS)
+    totals = call(total_kernel, shaped(PARTICLES, 8, LANES, dtype=F32), [VMEM], 10**5, 10**5)(picked)
+    totals = exchange(totals, PART)
     weights = call(
         weights_kernel,
         shaped(3 * LANES, CHANS),
@@ -307,23 +354,26 @@
         10**6,
         10**6,
         scratch=(
-            pltpu.VMEM((48, 9 * CHANS + 2 * LANES), F32),
+            pltpu.VMEM((SLICE, 9 * CHANS + 2 * LANES), F32),
             pltpu.VMEM((3 * LANES, CHANS), F32),
         ),
     )(picked)
 
-    edge = shaped(PARTICLES, WIDTH, LANES, dtype=F32)
-    part, up, down = call(
+    scale, shift = ada_scale[None], ada_shift[None]
+    edge = shaped(PARTICLES, WIDTH // 3, LANES, dtype=F32)
+    up, down = call(edge_kernel, [edge, edge], [VMEM] * 5, 10**8, 10**6)(
+        slabs, totals, scale, shift, weights
+    )
+    above = lax.ppermute(down, ROWS, [(i, i + 1) for i in range(ROW_DEVS - 1)])
+    below = lax.ppermute(up, ROWS, [(i + 1, i) for i in range(ROW_DEVS - 1)])
+    part = call(
         conv_kernel,
-        [shaped(PARTICLES, TOKENS, LANES, dtype=F32), edge, edge],
-        [SMEM] + [VMEM] * 6,
+        shaped(PARTICLES, TOKENS, LANES, dtype=F32),
+        [SMEM] + [VMEM] * 5,
         2 * 10**9,
         4 * 10**6,
         vmem=32,
-        scratch=(pltpu.VMEM((PARTICLES, CHANS), F32), pltpu.VMEM((PARTICLES, CHANS), F32)),
-    )(where, own, other, totals, ada_scale[None], ada_shift[None], weights)
-    above = lax.ppermute(down, ROWS, [(i, i + 1) for i in range(ROW_DEVS - 1)])
-    below = lax.ppermute(up, ROWS, [(i + 1, i) for i in range(ROW_DEVS - 1)])
+    )(place, slabs, totals, scale, shift, weights)
     pieces = call(
         finish_kernel, shaped(PARTICLES, 32, LANES), [SMEM] + [VMEM] * 3, 10**6, 10**6
     )(ancestors, part, above, below)

time: 195 us -> 174 us (0.89)
  waiting for transfers between devices: 36.5 us -> 11.1 us
  starting transfers between devices: 29.3 us -> 12.3 us
  between operations: 0.13 us -> 13.5 us
  blocking collectives: 108 us -> 115 us
    all_to_all x3 -> x1, waiting for transfers between devices: 30.2 us -> 4.25 us  [exchange(): return lax.all_to_all(values, axes, split_axis=0, concat_axis=0, tiled=True)]
    all_to_all x3 -> x1, starting transfers between devices: 18.1 us -> 8.86 us  [exchange(): return lax.all_to_all(values, axes, split_axis=0, concat_axis=0, tiled=True)]
    all_to_all x5, blocking collectives: 108 us -> 115 us  [exchange(): return lax.all_to_all(values, axes, split_axis=0, concat_axis=0, tiled=True)]
    ppermute x1 -> x0, starting transfers between devices: 5.14 us -> none  [per_device(): other = lax.ppermute(own, 'core', [(0, 1), (1, 0)])]
    all_gather x0 -> x1, waiting for transfers between devices: none -> 4.44 us  [per_device(): slabs = lax.all_gather(slab, PART)]
    ppermute x1, starting transfers between devices: 4.81 us -> 2.11 us  [per_device(): above = lax.ppermute(down, ROWS, [(i, i + 1) for i in range(ROW_DEVS - 1)])]
    ppermute x1, waiting for transfers between devices: 2.5 us -> 0.01 us  [per_device(): above = lax.ppermute(down, ROWS, [(i, i + 1) for i in range(ROW_DEVS - 1)])]
    unnamed x14 -> x18, local copies, waits for them, and re-layouts: 0.93 us -> 3.41 us
  transfers between devices with their start and end apart: 6 -> 4, of which waited for: 5 -> 3; matrix products, arithmetic and copies ran while one was open for 0% -> 0% of each run, Pallas kernels for 1% -> 3%
where the time goes in v2:
time: 174 us; the launch traced here: 172 us
  blocking collectives  115 us (66%)
  Pallas kernels  15.9 us (9%)
  between operations  13.5 us (8%)
  starting transfers between devices  12.3 us (7%)
  waiting for transfers between devices  11.1 us (6%)
  local copies, waits for them, and re-layouts  3.41 us (2%)
    all_to_all x5, blocking collectives, exchange(): return lax.all_to_all(values, axes, split_axis=0, concat_axis=0, tiled=True)  115 us
    all_to_all x1, starting transfers between devices, exchange(): return lax.all_to_all(values, axes, split_axis=0, concat_axis=0, tiled=True)  8.86 us
    pallas_call x1, Pallas kernels, per_device(): call(attend_kernel, shaped(ROW_DEVS, 16, LANES), [VMEM], 2 * 10 ** 9, 2 *...  4.53 us
    all_gather x1, waiting for transfers between devices, per_device(): slabs = lax.all_gather(slab, PART)  4.44 us
    all_to_all x1, waiting for transfers between devices, exchange(): return lax.all_to_all(values, axes, split_axis=0, concat_axis=0, tiled=True)  4.25 us
  transfers between devices with their start and end apart: 4, of which 3 were waited for; matrix products, arithmetic and copies ran while one was open for 0% of the time, Pallas kernels for 3%

profile of v2, /device:TPU:1, one launch (start us, length us, event | category | flops | bytes accessed | tf_op | source)
XLA Modules:
  0.0 171.5 jit_solution(4272218115387122266)
XLA Ops:
  6.5 0.0 copy-start.7
  6.5 0.0 copy-start.8
  6.5 0.0 all-gather.2.cloned.1.call-start
  6.5 0.7 all-gather.2.cloned.1.call-update
  7.3 0.0 copy-start.4
  7.3 0.9 copy-done.4
  8.2 0.0 copy-start.5
  8.2 0.9 copy-done.5
  9.1 0.7 shard_map.73
  9.8 32.6 %all_to_all.30.x_ref = bf16[32,64,128]{2,1,0:T(8,128)(2,1)S(1)} all-to-all(bf16[32,64,128]{2,1,0:T(8,128)(2,1)S(1)} %shard_map.73), channel_id=1, replica_groups=mesh['x'=4,'z_lo'=2,'core'=2,'z_hi'=4,'y'=8] {'z_hi','y'}, dimensions={0} | all-to-all | bytes 1048576 | tf_op jit(solution)/shard_map/all_to_all | solution.py:335
  42.4 0.7 shard_map.74
  43.1 8.9 %all-to-all-start.1 = ((f32[16,8,128]{2,1,0:T(8,128)}), f32[16,8,128]{2,1,0:T(8,128)S(1)}, u32[]{:S(2)}, u32[]{:S(2)}) async-start(f32[16,8,128]{2,1,0:T(8,128)} %shard_map.74), calls=%async_computation.1 | async-start | bytes 131072 | tf_op jit(solution)/shard_map/all_to_all | solution.py:335
  51.9 0.0 copy-done.7
  51.9 0.0 copy-done.8
  52.0 1.5 shard_map.75.w_ref
  53.5 4.2 %all-to-all-done.1.totals_ref = f32[16,8,128]{2,1,0:T(8,128)S(1)} async-done(((f32[16,8,128]{2,1,0:T(8,128)}), f32[16,8,128]{2,1,0:T(8,128)S(1)}, u32[]{:S(2)}, u32[]{:S(2)}) %all-to-all-start.1) | async-done | bytes 65568 | tf_op jit(solution)/shard_map/all_to_all | solution.py:335
  57.7 4.4 %all-gather.2.cloned.1.call-done.x_ref = bf16[16,96,640]{2,1,0:T(8,128)(2,1)} async-done(((bf16[1,96,640]{2,1,0:T(8,128)(2,1)}), bf16[16,96,640]{2,1,0:T(8,128)(2,1)}) %all-gather.2.cloned.1.call-update) | async-done | bytes 1966096 | tf_op jit(solution)/shard_map/all_gather | solution.py:342
  62.2 0.0 copy-start.1
  62.2 1.5 copy-done.1
  63.7 0.0 copy-start.2
  63.7 1.5 shard_map.77
  65.2 2.1 %collective-permute-start = (f32[16,8,128]{2,1,0:T(8,128)S(1)}, f32[16,8,128]{2,1,0:T(8,128)S(1)}, u32[]{:S(2)}, u32[]{:S(2)}) collective-permute-start(f32[16,8,128]{2,1,0:T(8,128)S(1)} %get-tuple-element.9), channel_id=1, source_target_pairs={{0,1},{1,2},{2,3},{3,4},{4,5},{5,6},{6,7},{7,8},{8,9},{9,10},{10,1... | collective-permute-start | bytes 196616 | tf_op jit(solution)/shard_map/ppermute | solution.py:367
  67.4 0.0 copy-start.6
  67.4 1.3 collective-permute-start.1
  68.7 0.0 copy-done.2
  68.7 0.0 copy-start
  68.7 3.0 %shard_map.76.part_ref = f32[16,96,128]{2,1,0:T(8,128)S(1)} custom-call(s32[1]{0:T(128)} %bitcast.place_ref, bf16[16,96,640]{2,1,0:T(8,128)(2,1)S(1)} %copy-done.2, f32[16,8,128]{2,1,0:T(8,128)S(1)} %all-to-all-done.1.totals_ref, f32[1,640]{1,0:T(1,128)S(1)} %broadcast_in_dim.10.scale_ref, f32[1,640]{1,0:T(1,128)S(1)} %broadcast_in_dim.11.shift_ref, ...), custom_call_target="tpu_custom_call" | custom-call | flops 2000000000 | bytes 4000000 | tf_op jit(solution)/shard_map/pallas_call | solution.py:369
  71.7 0.0 collective-permute-done.above_ref
  71.7 1.7 collective-permute-done.1.below_ref
  73.4 0.0 copy-done.6
  73.4 1.2 shard_map.78
  74.5 11.9 %all_to_all.31.x_ref = bf16[16,32,128]{2,1,0:T(8,128)(2,1)S(1)} all-to-all(bf16[16,32,128]{2,1,0:T(8,128)(2,1)S(1)} %shard_map.78), channel_id=1, replica_groups=mesh['x'=4,'z_lo'=2,'core'=2,'z_hi'=4,'y'=8] {'x','z_lo','core'}, dimensions={0} | all-to-all | bytes 262144 | tf_op jit(solution)/shard_map/all_to_all | solution.py:335
  86.4 0.7 shard_map.79
  87.1 24.0 %all_to_all.32.totals_ref = f32[32,8,128]{2,1,0:T(8,128)S(1)} all-to-all(f32[32,8,128]{2,1,0:T(8,128)S(1)} %get-tuple-element.11), channel_id=1, replica_groups=mesh['x'=4,'z_lo'=2,'core'=2,'z_hi'=4,'y'=8] {'z_hi','y'}, dimensions={0} | all-to-all | bytes 262144 | tf_op jit(solution)/shard_map/all_to_all | solution.py:335
  111.1 0.0 copy-done
  111.1 1.1 shard_map.80
  112.2 26.5 %all_to_all.33.x_ref = bf16[32,112,128]{2,1,0:T(8,128)(2,1)S(1)} all-to-all(bf16[32,112,128]{2,1,0:T(8,128)(2,1)S(1)} %shard_map.80), channel_id=1, replica_groups=mesh['x'=4,'z_lo'=2,'core'=2,'z_hi'=4,'y'=8] {'z_hi','y'}, dimensions={0} | all-to-all | bytes 1835008 | tf_op jit(solution)/shard_map/all_to_all | solution.py:335
  138.7 0.0 copy-start.3
  138.7 4.5 %shard_map.81 = bf16[32,16,128]{2,1,0:T(8,128)(2,1)S(1)} custom-call(bf16[32,112,128]{2,1,0:T(8,128)(2,1)S(1)} %all_to_all.33.x_ref), custom_call_target="tpu_custom_call" | custom-call | flops 2000000000 | bytes 2000000 | tf_op jit(solution)/shard_map/pallas_call | solution.py:401
  143.3 20.4 %all_to_all.34.x_ref = bf16[32,16,128]{2,1,0:T(8,128)(2,1)S(1)} all-to-all(bf16[32,16,128]{2,1,0:T(8,128)(2,1)S(1)} %shard_map.81), channel_id=1, replica_groups=mesh['x'=4,'z_lo'=2,'core'=2,'z_hi'=4,'y'=8] {'z_hi','y'}, dimensions={0} | all-to-all | bytes 262144 | tf_op jit(solution)/shard_map/all_to_all | solution.py:335
  163.7 0.0 copy-done.3
  163.7 1.0 shard_map.82
  (2 shorter events, 0.0 us)
Async XLA Ops:
  6.5 45.4 %copy-start.7 = (f32[640]{0:T(1024)S(1)}, f32[640]{0:T(1024)}, u32[]{:S(2)}) copy-start(f32[640]{0:T(1024)} %param.8) | copy-start | bytes 7684
  6.5 45.4 %copy-start.8 = (f32[640]{0:T(1024)S(1)}, f32[640]{0:T(1024)}, u32[]{:S(2)}) copy-start(f32[640]{0:T(1024)} %param.9) | copy-start | bytes 7684
  6.5 55.6 %all-gather.2.cloned.1.call-start = ((), (), s32[]{:S(2)}) async-start(), calls=%async_computation.6 | async-start | bytes 2088960 | tf_op jit(solution)/shard_map/all_gather | solution.py:342
  7.3 0.9 copy-start.4
  8.2 0.9 copy-start.5
  43.1 14.7 %all-to-all-start.1 = ((f32[16,8,128]{2,1,0:T(8,128)}), f32[16,8,128]{2,1,0:T(8,128)S(1)}, u32[]{:S(2)}, u32[]{:S(2)}) async-start(f32[16,8,128]{2,1,0:T(8,128)} %shard_map.74), calls=%async_computation.1 | async-start | bytes 131072 | tf_op jit(solution)/shard_map/all_to_all | solution.py:335
  62.2 1.5 copy-start.1
  63.7 4.9 %copy-start.2 = (bf16[16,96,640]{2,1,0:T(8,128)(2,1)S(1)}, bf16[16,96,640]{2,1,0:T(8,128)(2,1)}, u32[]{:S(2)}) copy-start(bf16[16,96,640]{2,1,0:T(8,128)(2,1)} %all-gather.2.cloned.1.call-done.x_ref) | copy-start | bytes 5898244
  65.2 6.4 %collective-permute-start = (f32[16,8,128]{2,1,0:T(8,128)S(1)}, f32[16,8,128]{2,1,0:T(8,128)S(1)}, u32[]{:S(2)}, u32[]{:S(2)}) collective-permute-start(f32[16,8,128]{2,1,0:T(8,128)S(1)} %get-tuple-element.9), channel_id=1, source_target_pairs={{0,1},{1,2},{2,3},{3,4},{4,5},{5,6},{6,7},{7,8},{8,9},{9,10},{10,1... | collective-permute-start | bytes 196616 | tf_op jit(solution)/shard_map/ppermute | solution.py:367
  67.4 6.0 %copy-start.6 = (s32[16]{0:T(128)S(1)}, s32[16]{0:T(128)}, u32[]{:S(2)}) copy-start(s32[16]{0:T(128)} %anc_ref.1) | copy-start | bytes 196
  67.4 6.0 %collective-permute-start.1 = (f32[16,8,128]{2,1,0:T(8,128)S(1)}, f32[16,8,128]{2,1,0:T(8,128)S(1)}, u32[]{:S(2)}, u32[]{:S(2)}) collective-permute-start(f32[16,8,128]{2,1,0:T(8,128)S(1)} %get-tuple-element.10), channel_id=1, source_target_pairs={{1,0},{2,1},{3,2},{4,3},{5,4},{6,5},{7,6},{8,7},{9,8},{10,9},{11,1... | collective-permute-start | bytes 196616 | tf_op jit(solution)/shard_map/ppermute | solution.py:368
  68.7 42.4 %copy-start = (bf16[640,1920]{1,0:T(8,128)(2,1)S(1)}, bf16[640,1920]{1,0:T(8,128)(2,1)}, u32[]{:S(2)}) copy-start(bf16[640,1920]{1,0:T(8,128)(2,1)} %w_ref.4) | copy-start | bytes 7372804
  138.7 25.0 %copy-start.3 = (bf16[640,640]{1,0:T(8,128)(2,1)S(1)}, bf16[640,640]{1,0:T(8,128)(2,1)}, u32[]{:S(2)}) copy-start(bf16[640,640]{1,0:T(8,128)(2,1)} %w_ref.5) | copy-start | bytes 2457604
Sparse Core Ops, SparseCore 0:
  9.5 52.6 all-gather.1

commit v3 on v2

--- a/solution.py
+++ b/solution.py
@@ -142,8 +142,30 @@
     out_ref[...] = tall_ref[...].astype(BF16)
 
 
-def gain_and_bias(totals_ref, scale_ref, shift_ref):
-    mean, inverse = mean_and_inverse(totals_ref[:, 0, :])
+STEPS = (0, 1, 3, 2)
+
+
+def order(place_ref):
+    x, z, core = place_ref[1], place_ref[2], place_ref[3]
+    return [
+        lax.rem(x + dx, 4) * 4 + lax.rem(z + dz, 2) * 2 + lax.rem(core + dc, 2)
+        for dc in range(2)
+        for dx in STEPS
+        for dz in range(2)
+    ]
+
+
+def spot(place_ref, q):
+    dx = lax.rem(q // 4 + 4 - place_ref[1], 4)
+    dz = lax.rem(lax.rem(q // 2, 2) + place_ref[2], 2)
+    dc = lax.rem(lax.rem(q, 2) + place_ref[3], 2)
+    step = jnp.where(dx == 2, 3, jnp.where(dx == 3, 2, dx))
+    return dc * 8 + step * 2 + dz
+
+
+def gain_and_bias(place_ref, totals_ref, scale_ref, shift_ref):
+    totals = jnp.concatenate([totals_ref[q, :1] for q in order(place_ref)], axis=0)
+    mean, inverse = mean_and_inverse(totals)
     gain = inverse * (1.0 + scale_ref[...])
     return gain, shift_ref[...] - mean * gain
 
@@ -176,15 +198,16 @@
     )
 
 
-def edge_kernel(x_ref, totals_ref, scale_ref, shift_ref, w_ref, up_ref, down_ref):
-    gain, bias = gain_and_bias(totals_ref, scale_ref, shift_ref)
+def edge_kernel(place_ref, totals_ref, scale_ref, shift_ref, w_ref, *refs):
+    slabs, (up_ref, down_ref) = refs[:8], refs[8:]
+    gain, bias = gain_and_bias(place_ref, totals_ref, scale_ref, shift_ref)
     for rows, tap, ref in (
         (slice(0, WIDTH), 2, up_ref),
         (slice(TOKENS - WIDTH, TOKENS), 0, down_ref),
     ):
         active = []
         for q in range(PARTICLES):
-            x = x_ref[q].astype(F32)[rows]
+            x = slabs[q // 2][q % 2].astype(F32)[rows]
             active.append(silu(x * gain[q : q + 1] + bias[q : q + 1]))
         active = jnp.concatenate(active, axis=0)
         weights = w_ref[tap * LANES : (tap + 1) * LANES, :]
@@ -194,8 +217,9 @@
             ref[q] = packed(full[q * WIDTH : (q + 1) * WIDTH])
 
 
-def conv_kernel(place_ref, x_ref, totals_ref, scale_ref, shift_ref, w_ref, part_ref):
-    gain, bias = gain_and_bias(totals_ref, scale_ref, shift_ref)
+def conv_kernel(place_ref, totals_ref, scale_ref, shift_ref, w_ref, *refs):
+    slabs, part_ref = refs[:8], refs[8]
+    gain, bias = gain_and_bias(place_ref, totals_ref, scale_ref, shift_ref)
     row, col = iota((LANES, CHANS), 0), iota((LANES, CHANS), 1)
     chosen = ((col == row + place_ref[0] * SLICE) & (row < SLICE)).astype(F32).astype(BF16)
     weights = w_ref[...]
@@ -204,7 +228,7 @@
     for step in range(PARTICLES // each):
         active, raw = [], []
         for q in range(step * each, (step + 1) * each):
-            x = x_ref[q]
+            x = slabs[q // 2][q % 2]
             raw.append(x)
             active.append(silu(x.astype(F32) * gain[q : q + 1] + bias[q : q + 1]))
         active = jnp.concatenate(active, axis=0)
@@ -226,11 +250,11 @@
             part_ref[step * each + k] = across(full)
 
 
-def finish_kernel(anc_ref, part_ref, above_ref, below_ref, out_ref):
+def finish_kernel(place_ref, anc_ref, part_ref, above_ref, below_ref, out_ref):
     last = TOKENS - WIDTH
     lane = iota((TOKENS, LANES), 1)
     for p in range(PARTICLES):
-        q = anc_ref[p]
+        q = spot(place_ref, anc_ref[p])
         total = jnp.concatenate(
             [
                 part_ref[q, :WIDTH] + unpacked(above_ref[q]),
@@ -337,9 +361,15 @@
 
 def per_device(latent, ada_scale, ada_shift, conv_weight, qkv_weight, out_weight, ancestors):
     slab = latent.reshape(TOKENS, CHANS)
-    place = lax.axis_index(PART).astype(jnp.int32)[None]
-
-    slabs = lax.all_gather(slab, PART)
+    particle = lax.axis_index(PART).astype(jnp.int32)
+    place = jnp.stack([particle] + [lax.axis_index(a).astype(jnp.int32) for a in PART])
+
+    swap = [(0, 1), (1, 0)]
+    pair = jnp.stack([slab, lax.ppermute(slab, "z_lo", swap)])
+    near = [pair] + [
+        lax.ppermute(pair, "x", [((i + d) % 4, i) for i in range(4)]) for d in (1, 3, 2)
+    ]
+    slabs = near + [lax.ppermute(values, "core", swap) for values in near]
 
     picked = call(pick_kernel, shaped(ROW_DEVS, 64, LANES), [SMEM, VMEM, VMEM], 10**7, 10**6)(
         place, slab, conv_weight
@@ -361,22 +391,22 @@
 
     scale, shift = ada_scale[None], ada_shift[None]
     edge = shaped(PARTICLES, WIDTH // 3, LANES, dtype=F32)
-    up, down = call(edge_kernel, [edge, edge], [VMEM] * 5, 10**8, 10**6)(
-        slabs, totals, scale, shift, weights
+    up, down = call(edge_kernel, [edge, edge], [SMEM] + [VMEM] * 12, 10**8, 10**6)(
+        place, totals, scale, shift, weights, *slabs
     )
     above = lax.ppermute(down, ROWS, [(i, i + 1) for i in range(ROW_DEVS - 1)])
     below = lax.ppermute(up, ROWS, [(i + 1, i) for i in range(ROW_DEVS - 1)])
     part = call(
         conv_kernel,
         shaped(PARTICLES, TOKENS, LANES, dtype=F32),
-        [SMEM] + [VMEM] * 5,
+        [SMEM] + [VMEM] * 12,
         2 * 10**9,
         4 * 10**6,
         vmem=32,
-    )(place, slabs, totals, scale, shift, weights)
+    )(place, totals, scale, shift, weights, *slabs)
     pieces = call(
-        finish_kernel, shaped(PARTICLES, 32, LANES), [SMEM] + [VMEM] * 3, 10**6, 10**6
-    )(ancestors, part, above, below)
+        finish_kernel, shaped(PARTICLES, 32, LANES), [SMEM, SMEM] + [VMEM] * 3, 10**6, 10**6
+    )(place, ancestors, part, above, below)
     pieces = exchange(pieces, PART)
 
     resid, sums = call(

time: 174 us -> 177 us (1.017)
  starting transfers between devices: 12.3 us -> 52 us
  blocking collectives: 115 us -> 82 us
  between operations: 13.5 us -> 0.26 us
  waiting for transfers between devices: 11.1 us -> 18.5 us
  Pallas kernels: 15.9 us -> 18.2 us
    all_to_all x5 -> x4, blocking collectives: 115 us -> 82 us  [exchange(): return lax.all_to_all(values, axes, split_axis=0, concat_axis=0, tiled=True)]
    ppermute x0 -> x8, starting transfers between devices: none -> 28 us  [the longest x4 15 us: per_device(): slabs = near + [lax.ppermute(values, 'core', swap) for values in near]]
    ppermute x0 -> x8, waiting for transfers between devices: none -> 14 us  [the longest x1 14 us: per_device(): pair = jnp.stack([slab, lax.ppermute(slab, 'z_lo', swap)])]
    all_to_all x1 -> x2, starting transfers between devices: 8.86 us -> 20.3 us  [exchange(): return lax.all_to_all(values, axes, split_axis=0, concat_axis=0, tiled=True)]
    all_gather x1 -> x0, waiting for transfers between devices: 4.44 us -> none  [per_device(): slabs = lax.all_gather(slab, PART)]
    all_to_all x1 -> x2, waiting for transfers between devices: 4.25 us -> 4.27 us  [exchange(): return lax.all_to_all(values, axes, split_axis=0, concat_axis=0, tiled=True)]
  transfers between devices with their start and end apart: 4 -> 12, of which waited for: 3 -> 3; matrix products, arithmetic and copies ran while one was open for 0% -> 1% of each run, Pallas kernels for 3% -> 3%
where the time goes in v3:
time: 177 us; the launch traced here: 174 us
  blocking collectives  82 us (46%)
  starting transfers between devices  52 us (29%)
  waiting for transfers between devices  18.5 us (10%)
  Pallas kernels  18.2 us (10%)
  local copies, waits for them, and re-layouts  1.87 us (1%)
    all_to_all x4, blocking collectives, exchange(): return lax.all_to_all(values, axes, split_axis=0, concat_axis=0, tiled=True)  82 us
    all_to_all x2, starting transfers between devices, exchange(): return lax.all_to_all(values, axes, split_axis=0, concat_axis=0, tiled=True)  20.3 us
    ppermute x4, starting transfers between devices, per_device(): slabs = near + [lax.ppermute(values, 'core', swap) for values in near]  15 us
    ppermute x1, waiting for transfers between devices, per_device(): pair = jnp.stack([slab, lax.ppermute(slab, 'z_lo', swap)])  14 us
    ppermute x3, starting transfers between devices, per_device(): lax.ppermute(pair, 'x', [((i + d) % 4, i) for i in range(4)])  9.93 us
    pallas_call x1, Pallas kernels, per_device(): call(attend_kernel, shaped(ROW_DEVS, 16, LANES), [VMEM], 2 * 10 ** 9, 2 *...  4.54 us
    all_to_all x2, waiting for transfers between devices, exchange(): return lax.all_to_all(values, axes, split_axis=0, concat_axis=0, tiled=True)  4.27 us
  transfers between devices with their start and end apart: 12, of which 3 were waited for; matrix products, arithmetic and copies ran while one was open for 1% of the time, Pallas kernels for 3%

profile of v3, /device:TPU:1, one launch (start us, length us, event | category | flops | bytes accessed | tf_op | source)
XLA Modules:
  0.0 173.9 jit_solution(11822498455398313904)
XLA Ops:
  0.0 0.1 pad_add_fusion.place_ref
  0.1 0.9 copy-done.2
  1.0 0.9 copy-done.3
  1.9 2.0 %shard_map.73 = bf16[32,64,128]{2,1,0:T(8,128)(2,1)} custom-call(s32[4]{0:T(128)S(1)} %pad_add_fusion.place_ref, bf16[96,640]{1,0:T(8,128)(2,1)S(1)} %bitcast.10, bf16[180,640]{1,0:T(8,128)(2,1)S(1)} %copy-done.3), custom_call_target="tpu_custom_call" | custom-call | flops 10000000 | bytes 1000000 | tf_op jit(solution)/shard_map/pallas_call | solution.py:374
  3.9 16.5 %all-to-all-start = ((bf16[32,64,128]{2,1,0:T(8,128)(2,1)}), bf16[32,64,128]{2,1,0:T(8,128)(2,1)S(1)}, u32[]{:S(2)}, u32[]{:S(2)}) async-start(bf16[32,64,128]{2,1,0:T(8,128)(2,1)} %shard_map.73), calls=%async_computation | async-start | bytes 1048576 | tf_op jit(solution)/shard_map/all_to_all | solution.py:359
  20.5 3.1 %collective-permute-start = (bf16[96,640]{1,0:T(8,128)(2,1)}, bf16[96,640]{1,0:T(8,128)(2,1)S(1)}, u32[]{:S(2)}, u32[]{:S(2)}) collective-permute-start(bf16[96,640]{1,0:T(8,128)(2,1)} %bitcast.8), channel_id=1, source_target_pairs={{0,64},{64,0},{1,65},{65,1},{2,66},{66,2},{3,67},{67,3},{4,68},{68... | collective-permute-start | bytes 368648 | tf_op jit(solution)/shard_map/ppermute | solution.py:368
  23.6 14.0 %collective-permute-done = bf16[96,640]{1,0:T(8,128)(2,1)S(1)} collective-permute-done((bf16[96,640]{1,0:T(8,128)(2,1)}, bf16[96,640]{1,0:T(8,128)(2,1)S(1)}, u32[]{:S(2)}, u32[]{:S(2)}) %collective-permute-start) | collective-permute-done | bytes 122912 | tf_op jit(solution)/shard_map/ppermute | solution.py:368
  37.5 0.9 pad_maximum_fusion.refs_0_
  38.5 4.4 %collective-permute-start.1 = (bf16[2,96,640]{2,1,0:T(8,128)(2,1)S(1)}, bf16[2,96,640]{2,1,0:T(8,128)(2,1)S(1)}, u32[]{:S(2)}, u32[]{:S(2)}) collective-permute-start(bf16[2,96,640]{2,1,0:T(8,128)(2,1)S(1)} %pad_maximum_fusion.refs_0_), channel_id=1, source_target_pairs={{128,0},{256,128},{384,256},{0,384},{129,1},{257,129},{385,257},{1... | collective-permute-start | bytes 737288 | tf_op jit(solution)/shard_map/ppermute | solution.py:370
  42.9 1.9 %collective-permute-start.2 = (bf16[2,96,640]{2,1,0:T(8,128)(2,1)S(1)}, bf16[2,96,640]{2,1,0:T(8,128)(2,1)S(1)}, u32[]{:S(2)}, u32[]{:S(2)}) collective-permute-start(bf16[2,96,640]{2,1,0:T(8,128)(2,1)S(1)} %pad_maximum_fusion.refs_0_), channel_id=1, source_target_pairs={{384,0},{0,128},{128,256},{256,384},{385,1},{1,129},{129,257},{257... | collective-permute-start | bytes 737288 | tf_op jit(solution)/shard_map/ppermute | solution.py:370
  44.8 3.6 %collective-permute-start.3 = (bf16[2,96,640]{2,1,0:T(8,128)(2,1)S(1)}, bf16[2,96,640]{2,1,0:T(8,128)(2,1)S(1)}, u32[]{:S(2)}, u32[]{:S(2)}) collective-permute-start(bf16[2,96,640]{2,1,0:T(8,128)(2,1)S(1)} %pad_maximum_fusion.refs_0_), channel_id=1, source_target_pairs={{256,0},{384,128},{0,256},{128,384},{257,1},{385,129},{1,257},{129... | collective-permute-start | bytes 737288 | tf_op jit(solution)/shard_map/ppermute | solution.py:370
  48.4 3.7 %collective-permute-start.4 = (bf16[2,96,640]{2,1,0:T(8,128)(2,1)S(1)}, bf16[2,96,640]{2,1,0:T(8,128)(2,1)S(1)}, u32[]{:S(2)}, u32[]{:S(2)}) collective-permute-start(bf16[2,96,640]{2,1,0:T(8,128)(2,1)S(1)} %pad_maximum_fusion.refs_0_), channel_id=1, source_target_pairs={{0,32},{32,0},{1,33},{33,1},{2,34},{34,2},{3,35},{35,3},{4,36},{36... | collective-permute-start | bytes 737288 | tf_op jit(solution)/shard_map/ppermute | solution.py:372
  52.1 0.0 collective-permute-done.1.refs_1_
  52.1 1.9 %collective-permute-start.5 = (bf16[2,96,640]{2,1,0:T(8,128)(2,1)S(1)}, bf16[2,96,640]{2,1,0:T(8,128)(2,1)S(1)}, u32[]{:S(2)}, u32[]{:S(2)}) collective-permute-start(bf16[2,96,640]{2,1,0:T(8,128)(2,1)S(1)} %collective-permute-done.1.refs_1_), channel_id=1, source_target_pairs={{0,32},{32,0},{1,33},{33,1},{2,34},{34,2},{3,35},{35,3},{4,36},{36... | collective-permute-start | bytes 737288 | tf_op jit(solution)/shard_map/ppermute | solution.py:372
  54.1 0.0 collective-permute-done.2.refs_2_
  54.1 7.4 %collective-permute-start.6 = (bf16[2,96,640]{2,1,0:T(8,128)(2,1)S(1)}, bf16[2,96,640]{2,1,0:T(8,128)(2,1)S(1)}, u32[]{:S(2)}, u32[]{:S(2)}) collective-permute-start(bf16[2,96,640]{2,1,0:T(8,128)(2,1)S(1)} %collective-permute-done.2.refs_2_), channel_id=1, source_target_pairs={{0,32},{32,0},{1,33},{33,1},{2,34},{34,2},{3,35},{35,3},{4,36},{36... | collective-permute-start | bytes 737288 | tf_op jit(solution)/shard_map/ppermute | solution.py:372
  61.5 0.0 collective-permute-done.3.refs_3_
  61.5 1.9 %collective-permute-start.7 = (bf16[2,96,640]{2,1,0:T(8,128)(2,1)S(1)}, bf16[2,96,640]{2,1,0:T(8,128)(2,1)S(1)}, u32[]{:S(2)}, u32[]{:S(2)}) collective-permute-start(bf16[2,96,640]{2,1,0:T(8,128)(2,1)S(1)} %collective-permute-done.3.refs_3_), channel_id=1, source_target_pairs={{0,32},{32,0},{1,33},{33,1},{2,34},{34,2},{3,35},{35,3},{4,36},{36... | collective-permute-start | bytes 737288 | tf_op jit(solution)/shard_map/ppermute | solution.py:372
  63.5 0.0 all-to-all-done.x_ref
  63.5 0.7 shard_map.74
  64.1 3.8 %all-to-all-start.1 = ((f32[16,8,128]{2,1,0:T(8,128)}), f32[16,8,128]{2,1,0:T(8,128)S(1)}, u32[]{:S(2)}, u32[]{:S(2)}) async-start(f32[16,8,128]{2,1,0:T(8,128)} %shard_map.74), calls=%async_computation.1 | async-start | bytes 131072 | tf_op jit(solution)/shard_map/all_to_all | solution.py:359
  67.9 0.0 copy-done.5
  67.9 0.0 copy-done.6
  68.0 1.5 shard_map.75.w_ref
  69.5 0.0 collective-permute-done.4.refs_4_
  69.5 0.0 collective-permute-done.5.refs_5_
  69.5 0.0 collective-permute-done.6.refs_6_
  69.5 0.0 collective-permute-done.7.refs_7_
  69.5 4.3 %all-to-all-done.1.totals_ref = f32[16,8,128]{2,1,0:T(8,128)S(1)} async-done(((f32[16,8,128]{2,1,0:T(8,128)}), f32[16,8,128]{2,1,0:T(8,128)S(1)}, u32[]{:S(2)}, u32[]{:S(2)}) %all-to-all-start.1) | async-done | bytes 65568 | tf_op jit(solution)/shard_map/all_to_all | solution.py:359
  73.8 2.0 %shard_map.77 = (f32[16,8,128]{2,1,0:T(8,128)S(1)}, f32[16,8,128]{2,1,0:T(8,128)S(1)}) custom-call(s32[4]{0:T(128)S(1)} %pad_add_fusion.place_ref, f32[16,8,128]{2,1,0:T(8,128)S(1)} %all-to-all-done.1.totals_ref, f32[1,640]{1,0:T(1,128)S(1)} %broadcast_in_dim.6.scale_ref, f32[1,640]{1,0:T(1,128)S(1)} %broadcast_in_dim.7.shift_ref, ...), custom_call_target="tpu_custom_call" | custom-call | flops 100000000 | bytes 1000000 | tf_op jit(solution)/shard_map/pallas_call | solution.py:394
  75.9 2.4 %collective-permute-start.8 = (f32[16,8,128]{2,1,0:T(8,128)S(1)}, f32[16,8,128]{2,1,0:T(8,128)S(1)}, u32[]{:S(2)}, u32[]{:S(2)}) collective-permute-start(f32[16,8,128]{2,1,0:T(8,128)S(1)} %get-tuple-element.9), channel_id=1, source_target_pairs={{0,1},{1,2},{2,3},{3,4},{4,5},{5,6},{6,7},{7,8},{8,9},{9,10},{10,1... | collective-permute-start | bytes 196616 | tf_op jit(solution)/shard_map/ppermute | solution.py:397
  78.3 0.0 copy-start.4
  78.3 1.3 collective-permute-start.9
  79.6 0.0 copy-start
  79.6 3.4 %shard_map.76.part_ref = f32[16,96,128]{2,1,0:T(8,128)S(1)} custom-call(s32[4]{0:T(128)S(1)} %pad_add_fusion.place_ref, f32[16,8,128]{2,1,0:T(8,128)S(1)} %all-to-all-done.1.totals_ref, f32[1,640]{1,0:T(1,128)S(1)} %broadcast_in_dim.6.scale_ref, f32[1,640]{1,0:T(1,128)S(1)} %broadcast_in_dim.7.shift_ref, bf16[384,640]{1,0:T(8,128)(2,1)S(1)} %shard_map.75.w_ref, ...), custom_call_target="tpu_custom_call" | custom-call | flops 2000000000 | bytes 4000000 | tf_op jit(solution)/shard_map/pallas_call | solution.py:399
  83.0 0.0 collective-permute-done.8.above_ref
  83.1 0.3 collective-permute-done.9.below_ref
  83.3 0.0 copy-done.4
  83.3 1.2 shard_map.78
  84.5 10.5 %all_to_all.30.x_ref = bf16[16,32,128]{2,1,0:T(8,128)(2,1)S(1)} all-to-all(bf16[16,32,128]{2,1,0:T(8,128)(2,1)S(1)} %shard_map.78), channel_id=1, replica_groups=mesh['x'=4,'z_lo'=2,'core'=2,'z_hi'=4,'y'=8] {'x','z_lo','core'}, dimensions={0} | all-to-all | bytes 262144 | tf_op jit(solution)/shard_map/all_to_all | solution.py:359
  95.0 0.7 shard_map.79
  95.7 24.5 %all_to_all.31.totals_ref = f32[32,8,128]{2,1,0:T(8,128)S(1)} all-to-all(f32[32,8,128]{2,1,0:T(8,128)S(1)} %get-tuple-element.11), channel_id=1, replica_groups=mesh['x'=4,'z_lo'=2,'core'=2,'z_hi'=4,'y'=8] {'z_hi','y'}, dimensions={0} | all-to-all | bytes 262144 | tf_op jit(solution)/shard_map/all_to_all | solution.py:359
  120.2 0.0 copy-done
  120.2 1.1 shard_map.80
  121.4 26.5 %all_to_all.32.x_ref = bf16[32,112,128]{2,1,0:T(8,128)(2,1)S(1)} all-to-all(bf16[32,112,128]{2,1,0:T(8,128)(2,1)S(1)} %shard_map.80), channel_id=1, replica_groups=mesh['x'=4,'z_lo'=2,'core'=2,'z_hi'=4,'y'=8] {'z_hi','y'}, dimensions={0} | all-to-all | bytes 1835008 | tf_op jit(solution)/shard_map/all_to_all | solution.py:359
  147.8 4.5 %shard_map.81 = bf16[32,16,128]{2,1,0:T(8,128)(2,1)S(1)} custom-call(bf16[32,112,128]{2,1,0:T(8,128)(2,1)S(1)} %all_to_all.32.x_ref), custom_call_target="tpu_custom_call" | custom-call | flops 2000000000 | bytes 2000000 | tf_op jit(solution)/shard_map/pallas_call | solution.py:431
  152.4 20.5 %all_to_all.33.x_ref = bf16[32,16,128]{2,1,0:T(8,128)(2,1)S(1)} all-to-all(bf16[32,16,128]{2,1,0:T(8,128)(2,1)S(1)} %shard_map.81), channel_id=1, replica_groups=mesh['x'=4,'z_lo'=2,'core'=2,'z_hi'=4,'y'=8] {'z_hi','y'}, dimensions={0} | all-to-all | bytes 262144 | tf_op jit(solution)/shard_map/all_to_all | solution.py:359
  172.9 1.0 shard_map.82
  (8 shorter events, 0.0 us)
Async XLA Ops:
  0.0 67.9 %copy-start.5 = (f32[640]{0:T(1024)S(1)}, f32[640]{0:T(1024)}, u32[]{:S(2)}) copy-start(f32[640]{0:T(1024)} %param.8) | copy-start | bytes 7684
  0.0 67.9 %copy-start.6 = (f32[640]{0:T(1024)S(1)}, f32[640]{0:T(1024)}, u32[]{:S(2)}) copy-start(f32[640]{0:T(1024)} %param.9) | copy-start | bytes 7684
  0.1 0.9 copy-start.2
  1.0 0.9 copy-start.3
  3.9 59.5 %all-to-all-start = ((bf16[32,64,128]{2,1,0:T(8,128)(2,1)}), bf16[32,64,128]{2,1,0:T(8,128)(2,1)S(1)}, u32[]{:S(2)}, u32[]{:S(2)}) async-start(bf16[32,64,128]{2,1,0:T(8,128)(2,1)} %shard_map.73), calls=%async_computation | async-start | bytes 1048576 | tf_op jit(solution)/shard_map/all_to_all | solution.py:359
  20.5 17.1 %collective-permute-start = (bf16[96,640]{1,0:T(8,128)(2,1)}, bf16[96,640]{1,0:T(8,128)(2,1)S(1)}, u32[]{:S(2)}, u32[]{:S(2)}) collective-permute-start(bf16[96,640]{1,0:T(8,128)(2,1)} %bitcast.8), channel_id=1, source_target_pairs={{0,64},{64,0},{1,65},{65,1},{2,66},{66,2},{3,67},{67,3},{4,68},{68... | collective-permute-start | bytes 368648 | tf_op jit(solution)/shard_map/ppermute | solution.py:368
  38.5 13.7 %collective-permute-start.1 = (bf16[2,96,640]{2,1,0:T(8,128)(2,1)S(1)}, bf16[2,96,640]{2,1,0:T(8,128)(2,1)S(1)}, u32[]{:S(2)}, u32[]{:S(2)}) collective-permute-start(bf16[2,96,640]{2,1,0:T(8,128)(2,1)S(1)} %pad_maximum_fusion.refs_0_), channel_id=1, source_target_pairs={{128,0},{256,128},{384,256},{0,384},{129,1},{257,129},{385,257},{1... | collective-permute-start | bytes 737288 | tf_op jit(solution)/shard_map/ppermute | solution.py:370
  42.9 11.2 %collective-permute-start.2 = (bf16[2,96,640]{2,1,0:T(8,128)(2,1)S(1)}, bf16[2,96,640]{2,1,0:T(8,128)(2,1)S(1)}, u32[]{:S(2)}, u32[]{:S(2)}) collective-permute-start(bf16[2,96,640]{2,1,0:T(8,128)(2,1)S(1)} %pad_maximum_fusion.refs_0_), channel_id=1, source_target_pairs={{384,0},{0,128},{128,256},{256,384},{385,1},{1,129},{129,257},{257... | collective-permute-start | bytes 737288 | tf_op jit(solution)/shard_map/ppermute | solution.py:370
  44.8 16.7 %collective-permute-start.3 = (bf16[2,96,640]{2,1,0:T(8,128)(2,1)S(1)}, bf16[2,96,640]{2,1,0:T(8,128)(2,1)S(1)}, u32[]{:S(2)}, u32[]{:S(2)}) collective-permute-start(bf16[2,96,640]{2,1,0:T(8,128)(2,1)S(1)} %pad_maximum_fusion.refs_0_), channel_id=1, source_target_pairs={{256,0},{384,128},{0,256},{128,384},{257,1},{385,129},{1,257},{129... | collective-permute-start | bytes 737288 | tf_op jit(solution)/shard_map/ppermute | solution.py:370
  48.4 21.1 %collective-permute-start.4 = (bf16[2,96,640]{2,1,0:T(8,128)(2,1)S(1)}, bf16[2,96,640]{2,1,0:T(8,128)(2,1)S(1)}, u32[]{:S(2)}, u32[]{:S(2)}) collective-permute-start(bf16[2,96,640]{2,1,0:T(8,128)(2,1)S(1)} %pad_maximum_fusion.refs_0_), channel_id=1, source_target_pairs={{0,32},{32,0},{1,33},{33,1},{2,34},{34,2},{3,35},{35,3},{4,36},{36... | collective-permute-start | bytes 737288 | tf_op jit(solution)/shard_map/ppermute | solution.py:372
  52.1 17.4 %collective-permute-start.5 = (bf16[2,96,640]{2,1,0:T(8,128)(2,1)S(1)}, bf16[2,96,640]{2,1,0:T(8,128)(2,1)S(1)}, u32[]{:S(2)}, u32[]{:S(2)}) collective-permute-start(bf16[2,96,640]{2,1,0:T(8,128)(2,1)S(1)} %collective-permute-done.1.refs_1_), channel_id=1, source_target_pairs={{0,32},{32,0},{1,33},{33,1},{2,34},{34,2},{3,35},{35,3},{4,36},{36... | collective-permute-start | bytes 737288 | tf_op jit(solution)/shard_map/ppermute | solution.py:372
  54.1 15.4 %collective-permute-start.6 = (bf16[2,96,640]{2,1,0:T(8,128)(2,1)S(1)}, bf16[2,96,640]{2,1,0:T(8,128)(2,1)S(1)}, u32[]{:S(2)}, u32[]{:S(2)}) collective-permute-start(bf16[2,96,640]{2,1,0:T(8,128)(2,1)S(1)} %collective-permute-done.2.refs_2_), channel_id=1, source_target_pairs={{0,32},{32,0},{1,33},{33,1},{2,34},{34,2},{3,35},{35,3},{4,36},{36... | collective-permute-start | bytes 737288 | tf_op jit(solution)/shard_map/ppermute | solution.py:372
  61.5 8.0 %collective-permute-start.7 = (bf16[2,96,640]{2,1,0:T(8,128)(2,1)S(1)}, bf16[2,96,640]{2,1,0:T(8,128)(2,1)S(1)}, u32[]{:S(2)}, u32[]{:S(2)}) collective-permute-start(bf16[2,96,640]{2,1,0:T(8,128)(2,1)S(1)} %collective-permute-done.3.refs_3_), channel_id=1, source_target_pairs={{0,32},{32,0},{1,33},{33,1},{2,34},{34,2},{3,35},{35,3},{4,36},{36... | collective-permute-start | bytes 737288 | tf_op jit(solution)/shard_map/ppermute | solution.py:372
  64.1 9.7 %all-to-all-start.1 = ((f32[16,8,128]{2,1,0:T(8,128)}), f32[16,8,128]{2,1,0:T(8,128)S(1)}, u32[]{:S(2)}, u32[]{:S(2)}) async-start(f32[16,8,128]{2,1,0:T(8,128)} %shard_map.74), calls=%async_computation.1 | async-start | bytes 131072 | tf_op jit(solution)/shard_map/all_to_all | solution.py:359
  75.9 7.2 %collective-permute-start.8 = (f32[16,8,128]{2,1,0:T(8,128)S(1)}, f32[16,8,128]{2,1,0:T(8,128)S(1)}, u32[]{:S(2)}, u32[]{:S(2)}) collective-permute-start(f32[16,8,128]{2,1,0:T(8,128)S(1)} %get-tuple-element.9), channel_id=1, source_target_pairs={{0,1},{1,2},{2,3},{3,4},{4,5},{5,6},{6,7},{7,8},{8,9},{9,10},{10,1... | collective-permute-start | bytes 196616 | tf_op jit(solution)/shard_map/ppermute | solution.py:397
  78.3 5.0 %copy-start.4 = (s32[16]{0:T(128)S(1)}, s32[16]{0:T(128)}, u32[]{:S(2)}) copy-start(s32[16]{0:T(128)} %anc_ref.1) | copy-start | bytes 196
  78.3 5.0 %collective-permute-start.9 = (f32[16,8,128]{2,1,0:T(8,128)S(1)}, f32[16,8,128]{2,1,0:T(8,128)S(1)}, u32[]{:S(2)}, u32[]{:S(2)}) collective-permute-start(f32[16,8,128]{2,1,0:T(8,128)S(1)} %get-tuple-element.10), channel_id=1, source_target_pairs={{1,0},{2,1},{3,2},{4,3},{5,4},{6,5},{7,6},{8,7},{9,8},{10,9},{11,1... | collective-permute-start | bytes 196616 | tf_op jit(solution)/shard_map/ppermute | solution.py:398
  79.6 40.6 %copy-start = (bf16[640,1920]{1,0:T(8,128)(2,1)S(1)}, bf16[640,1920]{1,0:T(8,128)(2,1)}, u32[]{:S(2)}) copy-start(bf16[640,1920]{1,0:T(8,128)(2,1)} %w_ref.4) | copy-start | bytes 7372804
  147.8 25.0 %copy-start.1 = (bf16[640,640]{1,0:T(8,128)(2,1)S(1)}, bf16[640,640]{1,0:T(8,128)(2,1)}, u32[]{:S(2)}) copy-start(bf16[640,640]{1,0:T(8,128)(2,1)} %w_ref.5) | copy-start | bytes 2457604

commit v4 on v3

--- a/solution.py
+++ b/solution.py
@@ -150,8 +150,8 @@
     return [
         lax.rem(x + dx, 4) * 4 + lax.rem(z + dz, 2) * 2 + lax.rem(core + dc, 2)
         for dc in range(2)
+        for dz in range(2)
         for dx in STEPS
-        for dz in range(2)
     ]
 
 
@@ -160,7 +160,7 @@
     dz = lax.rem(lax.rem(q // 2, 2) + place_ref[2], 2)
     dc = lax.rem(lax.rem(q, 2) + place_ref[3], 2)
     step = jnp.where(dx == 2, 3, jnp.where(dx == 3, 2, dx))
-    return dc * 8 + step * 2 + dz
+    return dc * 8 + dz * 4 + step
 
 
 def gain_and_bias(place_ref, totals_ref, scale_ref, shift_ref):
@@ -199,7 +199,7 @@
 
 
 def edge_kernel(place_ref, totals_ref, scale_ref, shift_ref, w_ref, *refs):
-    slabs, (up_ref, down_ref) = refs[:8], refs[8:]
+    slabs, (up_ref, down_ref) = refs[:4], refs[4:]
     gain, bias = gain_and_bias(place_ref, totals_ref, scale_ref, shift_ref)
     for rows, tap, ref in (
         (slice(0, WIDTH), 2, up_ref),
@@ -207,7 +207,7 @@
     ):
         active = []
         for q in range(PARTICLES):
-            x = slabs[q // 2][q % 2].astype(F32)[rows]
+            x = slabs[q // 4][q % 4].astype(F32)[rows]
             active.append(silu(x * gain[q : q + 1] + bias[q : q + 1]))
         active = jnp.concatenate(active, axis=0)
         weights = w_ref[tap * LANES : (tap + 1) * LANES, :]
@@ -218,7 +218,7 @@
 
 
 def conv_kernel(place_ref, totals_ref, scale_ref, shift_ref, w_ref, *refs):
-    slabs, part_ref = refs[:8], refs[8]
+    slabs, part_ref = refs[:4], refs[4]
     gain, bias = gain_and_bias(place_ref, totals_ref, scale_ref, shift_ref)
     row, col = iota((LANES, CHANS), 0), iota((LANES, CHANS), 1)
     chosen = ((col == row + place_ref[0] * SLICE) & (row < SLICE)).astype(F32).astype(BF16)
@@ -228,7 +228,7 @@
     for step in range(PARTICLES // each):
         active, raw = [], []
         for q in range(step * each, (step + 1) * each):
-            x = slabs[q // 2][q % 2]
+            x = slabs[q // 4][q % 4]
             raw.append(x)
             active.append(silu(x.astype(F32) * gain[q : q + 1] + bias[q : q + 1]))
         active = jnp.concatenate(active, axis=0)
@@ -365,11 +365,12 @@
     place = jnp.stack([particle] + [lax.axis_index(a).astype(jnp.int32) for a in PART])
 
     swap = [(0, 1), (1, 0)]
-    pair = jnp.stack([slab, lax.ppermute(slab, "z_lo", swap)])
-    near = [pair] + [
-        lax.ppermute(pair, "x", [((i + d) % 4, i) for i in range(4)]) for d in (1, 3, 2)
+    along = [slab] + [
+        lax.ppermute(slab, "x", [((i + d) % 4, i) for i in range(4)]) for d in STEPS[1:]
     ]
-    slabs = near + [lax.ppermute(values, "core", swap) for values in near]
+    four = jnp.stack(along)
+    eight = [four, lax.ppermute(four, "z_lo", swap)]
+    slabs = eight + [lax.ppermute(values, "core", swap) for values in eight]
 
     picked = call(pick_kernel, shaped(ROW_DEVS, 64, LANES), [SMEM, VMEM, VMEM], 10**7, 10**6)(
         place, slab, conv_weight
@@ -391,7 +392,7 @@
 
     scale, shift = ada_scale[None], ada_shift[None]
     edge = shaped(PARTICLES, WIDTH // 3, LANES, dtype=F32)
-    up, down = call(edge_kernel, [edge, edge], [SMEM] + [VMEM] * 12, 10**8, 10**6)(
+    up, down = call(edge_kernel, [edge, edge], [SMEM] + [VMEM] * 8, 10**8, 10**6)(
         place, totals, scale, shift, weights, *slabs
     )
     above = lax.ppermute(down, ROWS, [(i, i + 1) for i in range(ROW_DEVS - 1)])
@@ -399,7 +400,7 @@
     part = call(
         conv_kernel,
         shaped(PARTICLES, TOKENS, LANES, dtype=F32),
-        [SMEM] + [VMEM] * 12,
+        [SMEM] + [VMEM] * 8,
         2 * 10**9,
         4 * 10**6,
         vmem=32,

time: 177 us -> 172 us (0.972)
  starting transfers between devices: 52 us -> 44.3 us
  waiting for transfers between devices: 18.5 us -> 21.9 us
    ppermute x8 -> x6, starting transfers between devices: 28 us -> 20.9 us  [the longest x3 10.9 us: per_device(): lax.ppermute(slab, 'x', [((i + d) % 4, i) for i in range(4)])]
    ppermute x8 -> x6, waiting for transfers between devices: 14 us -> 17 us  [the longest x1 17 us: per_device(): eight = [four, lax.ppermute(four, 'z_lo', swap)]]
  transfers between devices with their start and end apart: 12 -> 10, of which waited for: 3 -> 3; matrix products, arithmetic and copies ran while one was open for 1% -> 1% of each run, Pallas kernels for 3% -> 5%
where the time goes in v4:
time: 172 us; the launch traced here: 169 us
  blocking collectives  81.2 us (47%)
  starting transfers between devices  44.3 us (26%)
  waiting for transfers between devices  21.9 us (13%)
  Pallas kernels  18.2 us (11%)
  local copies, waits for them, and re-layouts  1.87 us (1%)
    all_to_all x4, blocking collectives, exchange(): return lax.all_to_all(values, axes, split_axis=0, concat_axis=0, tiled=True)  81.2 us
    all_to_all x2, starting transfers between devices, exchange(): return lax.all_to_all(values, axes, split_axis=0, concat_axis=0, tiled=True)  19.5 us
    ppermute x1, waiting for transfers between devices, per_device(): eight = [four, lax.ppermute(four, 'z_lo', swap)]  17 us
    ppermute x3, starting transfers between devices, per_device(): lax.ppermute(slab, 'x', [((i + d) % 4, i) for i in range(4)])  10.9 us
    ppermute x2, starting transfers between devices, per_device(): slabs = eight + [lax.ppermute(values, 'core', swap) for values in eight]  6.92 us
    pallas_call x1, Pallas kernels, per_device(): call(attend_kernel, shaped(ROW_DEVS, 16, LANES), [VMEM], 2 * 10 ** 9, 2 *...  4.54 us
    all_to_all x2, waiting for transfers between devices, exchange(): return lax.all_to_all(values, axes, split_axis=0, concat_axis=0, tiled=True)  4.23 us
  transfers between devices with their start and end apart: 10, of which 3 were waited for; matrix products, arithmetic and copies ran while one was open for 1% of the time, Pallas kernels for 5%

profile of v4, /device:TPU:1, one launch (start us, length us, event | category | flops | bytes accessed | tf_op | source)
XLA Modules:
  0.0 168.8 jit_solution(16496480113662320063)
XLA Ops:
  0.0 0.0 copy-start.5
  0.0 0.0 copy-start.6
  0.0 5.3 %collective-permute-start = (bf16[96,640]{1,0:T(8,128)(2,1)}, bf16[96,640]{1,0:T(8,128)(2,1)S(1)}, u32[]{:S(2)}, u32[]{:S(2)}) collective-permute-start(bf16[96,640]{1,0:T(8,128)(2,1)} %bitcast.10), channel_id=1, source_target_pairs={{128,0},{256,128},{384,256},{0,384},{129,1},{257,129},{385,257},{1... | collective-permute-start | bytes 368648 | tf_op jit(solution)/shard_map/ppermute | solution.py:369
  5.4 1.9 %collective-permute-start.1 = (bf16[96,640]{1,0:T(8,128)(2,1)}, bf16[96,640]{1,0:T(8,128)(2,1)S(1)}, u32[]{:S(2)}, u32[]{:S(2)}) collective-permute-start(bf16[96,640]{1,0:T(8,128)(2,1)} %bitcast.11), channel_id=1, source_target_pairs={{384,0},{0,128},{128,256},{256,384},{385,1},{1,129},{129,257},{257... | collective-permute-start | bytes 368648 | tf_op jit(solution)/shard_map/ppermute | solution.py:369
  7.3 3.6 %collective-permute-start.2 = (bf16[96,640]{1,0:T(8,128)(2,1)}, bf16[96,640]{1,0:T(8,128)(2,1)S(1)}, u32[]{:S(2)}, u32[]{:S(2)}) collective-permute-start(bf16[96,640]{1,0:T(8,128)(2,1)} %bitcast.12), channel_id=1, source_target_pairs={{256,0},{384,128},{0,256},{128,384},{257,1},{385,129},{1,257},{129... | collective-permute-start | bytes 368648 | tf_op jit(solution)/shard_map/ppermute | solution.py:369
  10.9 0.1 pad_add_fusion.place_ref
  11.0 0.0 copy-start.2
  11.0 0.9 copy-done.2
  11.9 0.9 copy-done.3
  12.9 2.0 %shard_map.73 = bf16[32,64,128]{2,1,0:T(8,128)(2,1)} custom-call(s32[4]{0:T(128)S(1)} %pad_add_fusion.place_ref, bf16[96,640]{1,0:T(8,128)(2,1)S(1)} %bitcast.14, bf16[180,640]{1,0:T(8,128)(2,1)S(1)} %copy-done.3), custom_call_target="tpu_custom_call" | custom-call | flops 10000000 | bytes 1000000 | tf_op jit(solution)/shard_map/pallas_call | solution.py:375
  14.9 15.7 %all-to-all-start = ((bf16[32,64,128]{2,1,0:T(8,128)(2,1)}), bf16[32,64,128]{2,1,0:T(8,128)(2,1)S(1)}, u32[]{:S(2)}, u32[]{:S(2)}) async-start(bf16[32,64,128]{2,1,0:T(8,128)(2,1)} %shard_map.73), calls=%async_computation | async-start | bytes 1048576 | tf_op jit(solution)/shard_map/all_to_all | solution.py:359
  30.5 0.0 collective-permute-done
  30.5 0.0 collective-permute-done.1
  30.6 0.0 collective-permute-done.2
  30.6 1.0 pad_maximum_fusion.refs_0_
  31.6 3.1 %collective-permute-start.3 = (bf16[4,96,640]{2,1,0:T(8,128)(2,1)S(1)}, bf16[4,96,640]{2,1,0:T(8,128)(2,1)S(1)}, u32[]{:S(2)}, u32[]{:S(2)}) collective-permute-start(bf16[4,96,640]{2,1,0:T(8,128)(2,1)S(1)} %pad_maximum_fusion.refs_0_), channel_id=1, source_target_pairs={{0,64},{64,0},{1,65},{65,1},{2,66},{66,2},{3,67},{67,3},{4,68},{68... | collective-permute-start | bytes 1474568 | tf_op jit(solution)/shard_map/ppermute | solution.py:372
  34.7 4.0 %collective-permute-start.4 = (bf16[4,96,640]{2,1,0:T(8,128)(2,1)S(1)}, bf16[4,96,640]{2,1,0:T(8,128)(2,1)S(1)}, u32[]{:S(2)}, u32[]{:S(2)}) collective-permute-start(bf16[4,96,640]{2,1,0:T(8,128)(2,1)S(1)} %pad_maximum_fusion.refs_0_), channel_id=1, source_target_pairs={{0,32},{32,0},{1,33},{33,1},{2,34},{34,2},{3,35},{35,3},{4,36},{36... | collective-permute-start | bytes 1474568 | tf_op jit(solution)/shard_map/ppermute | solution.py:373
  38.7 17.0 %collective-permute-done.3.refs_1_ = bf16[4,96,640]{2,1,0:T(8,128)(2,1)S(1)} collective-permute-done((bf16[4,96,640]{2,1,0:T(8,128)(2,1)S(1)}, bf16[4,96,640]{2,1,0:T(8,128)(2,1)S(1)}, u32[]{:S(2)}, u32[]{:S(2)}) %collective-permute-start.3) | collective-permute-done | bytes 491552 | tf_op jit(solution)/shard_map/ppermute | solution.py:372
  55.7 2.9 %collective-permute-start.5 = (bf16[4,96,640]{2,1,0:T(8,128)(2,1)S(1)}, bf16[4,96,640]{2,1,0:T(8,128)(2,1)S(1)}, u32[]{:S(2)}, u32[]{:S(2)}) collective-permute-start(bf16[4,96,640]{2,1,0:T(8,128)(2,1)S(1)} %collective-permute-done.3.refs_1_), channel_id=1, source_target_pairs={{0,32},{32,0},{1,33},{33,1},{2,34},{34,2},{3,35},{35,3},{4,36},{36... | collective-permute-start | bytes 1474568 | tf_op jit(solution)/shard_map/ppermute | solution.py:373
  58.6 0.0 all-to-all-done.x_ref
  58.6 0.7 shard_map.74
  59.3 3.8 %all-to-all-start.1 = ((f32[16,8,128]{2,1,0:T(8,128)}), f32[16,8,128]{2,1,0:T(8,128)S(1)}, u32[]{:S(2)}, u32[]{:S(2)}) async-start(f32[16,8,128]{2,1,0:T(8,128)} %shard_map.74), calls=%async_computation.1 | async-start | bytes 131072 | tf_op jit(solution)/shard_map/all_to_all | solution.py:359
  63.1 0.0 copy-done.5
  63.1 0.0 copy-done.6
  63.1 1.5 shard_map.75.w_ref
  64.7 0.0 collective-permute-done.4.refs_2_
  64.7 0.0 collective-permute-done.5.refs_3_
  64.7 4.2 %all-to-all-done.1.totals_ref = f32[16,8,128]{2,1,0:T(8,128)S(1)} async-done(((f32[16,8,128]{2,1,0:T(8,128)}), f32[16,8,128]{2,1,0:T(8,128)S(1)}, u32[]{:S(2)}, u32[]{:S(2)}) %all-to-all-start.1) | async-done | bytes 65568 | tf_op jit(solution)/shard_map/all_to_all | solution.py:359
  68.9 2.0 %shard_map.77 = (f32[16,8,128]{2,1,0:T(8,128)S(1)}, f32[16,8,128]{2,1,0:T(8,128)S(1)}) custom-call(s32[4]{0:T(128)S(1)} %pad_add_fusion.place_ref, f32[16,8,128]{2,1,0:T(8,128)S(1)} %all-to-all-done.1.totals_ref, f32[1,640]{1,0:T(1,128)S(1)} %broadcast_in_dim.6.scale_ref, f32[1,640]{1,0:T(1,128)S(1)} %broadcast_in_dim.7.shift_ref, ...), custom_call_target="tpu_custom_call" | custom-call | flops 100000000 | bytes 1000000 | tf_op jit(solution)/shard_map/pallas_call | solution.py:395
  71.0 2.7 %collective-permute-start.6 = (f32[16,8,128]{2,1,0:T(8,128)S(1)}, f32[16,8,128]{2,1,0:T(8,128)S(1)}, u32[]{:S(2)}, u32[]{:S(2)}) collective-permute-start(f32[16,8,128]{2,1,0:T(8,128)S(1)} %get-tuple-element.9), channel_id=1, source_target_pairs={{0,1},{1,2},{2,3},{3,4},{4,5},{5,6},{6,7},{7,8},{8,9},{9,10},{10,1... | collective-permute-start | bytes 196616 | tf_op jit(solution)/shard_map/ppermute | solution.py:398
  73.6 0.0 copy-start.4
  73.6 1.3 collective-permute-start.7
  74.9 0.0 copy-start
  74.9 3.4 %shard_map.76.part_ref = f32[16,96,128]{2,1,0:T(8,128)S(1)} custom-call(s32[4]{0:T(128)S(1)} %pad_add_fusion.place_ref, f32[16,8,128]{2,1,0:T(8,128)S(1)} %all-to-all-done.1.totals_ref, f32[1,640]{1,0:T(1,128)S(1)} %broadcast_in_dim.6.scale_ref, f32[1,640]{1,0:T(1,128)S(1)} %broadcast_in_dim.7.shift_ref, bf16[384,640]{1,0:T(8,128)(2,1)S(1)} %shard_map.75.w_ref, ...), custom_call_target="tpu_custom_call" | custom-call | flops 2000000000 | bytes 4000000 | tf_op jit(solution)/shard_map/pallas_call | solution.py:400
  78.4 0.0 collective-permute-done.6.above_ref
  78.4 0.6 collective-permute-done.7.below_ref
  79.0 0.0 copy-done.4
  79.0 1.2 shard_map.78
  80.2 10.2 %all_to_all.30.x_ref = bf16[16,32,128]{2,1,0:T(8,128)(2,1)S(1)} all-to-all(bf16[16,32,128]{2,1,0:T(8,128)(2,1)S(1)} %shard_map.78), channel_id=1, replica_groups=mesh['x'=4,'z_lo'=2,'core'=2,'z_hi'=4,'y'=8] {'x','z_lo','core'}, dimensions={0} | all-to-all | bytes 262144 | tf_op jit(solution)/shard_map/all_to_all | solution.py:359
  90.4 0.7 shard_map.79
  91.1 24.1 %all_to_all.31.totals_ref = f32[32,8,128]{2,1,0:T(8,128)S(1)} all-to-all(f32[32,8,128]{2,1,0:T(8,128)S(1)} %get-tuple-element.11), channel_id=1, replica_groups=mesh['x'=4,'z_lo'=2,'core'=2,'z_hi'=4,'y'=8] {'z_hi','y'}, dimensions={0} | all-to-all | bytes 262144 | tf_op jit(solution)/shard_map/all_to_all | solution.py:359
  115.2 0.0 copy-done
  115.2 1.1 shard_map.80
  116.3 26.5 %all_to_all.32.x_ref = bf16[32,112,128]{2,1,0:T(8,128)(2,1)S(1)} all-to-all(bf16[32,112,128]{2,1,0:T(8,128)(2,1)S(1)} %shard_map.80), channel_id=1, replica_groups=mesh['x'=4,'z_lo'=2,'core'=2,'z_hi'=4,'y'=8] {'z_hi','y'}, dimensions={0} | all-to-all | bytes 1835008 | tf_op jit(solution)/shard_map/all_to_all | solution.py:359
  142.8 4.5 %shard_map.81 = bf16[32,16,128]{2,1,0:T(8,128)(2,1)S(1)} custom-call(bf16[32,112,128]{2,1,0:T(8,128)(2,1)S(1)} %all_to_all.32.x_ref), custom_call_target="tpu_custom_call" | custom-call | flops 2000000000 | bytes 2000000 | tf_op jit(solution)/shard_map/pallas_call | solution.py:432
  147.3 20.5 %all_to_all.33.x_ref = bf16[32,16,128]{2,1,0:T(8,128)(2,1)S(1)} all-to-all(bf16[32,16,128]{2,1,0:T(8,128)(2,1)S(1)} %shard_map.81), channel_id=1, replica_groups=mesh['x'=4,'z_lo'=2,'core'=2,'z_hi'=4,'y'=8] {'z_hi','y'}, dimensions={0} | all-to-all | bytes 262144 | tf_op jit(solution)/shard_map/all_to_all | solution.py:359
  167.8 0.0 copy-done.1
  167.8 1.0 shard_map.82
  (4 shorter events, 0.0 us)
Async XLA Ops:
  0.0 63.1 %copy-start.5 = (f32[640]{0:T(1024)S(1)}, f32[640]{0:T(1024)}, u32[]{:S(2)}) copy-start(f32[640]{0:T(1024)} %param.8) | copy-start | bytes 7684
  0.0 63.1 %copy-start.6 = (f32[640]{0:T(1024)S(1)}, f32[640]{0:T(1024)}, u32[]{:S(2)}) copy-start(f32[640]{0:T(1024)} %param.9) | copy-start | bytes 7684
  0.0 30.5 %collective-permute-start = (bf16[96,640]{1,0:T(8,128)(2,1)}, bf16[96,640]{1,0:T(8,128)(2,1)S(1)}, u32[]{:S(2)}, u32[]{:S(2)}) collective-permute-start(bf16[96,640]{1,0:T(8,128)(2,1)} %bitcast.10), channel_id=1, source_target_pairs={{128,0},{256,128},{384,256},{0,384},{129,1},{257,129},{385,257},{1... | collective-permute-start | bytes 368648 | tf_op jit(solution)/shard_map/ppermute | solution.py:369
  5.4 25.2 %collective-permute-start.1 = (bf16[96,640]{1,0:T(8,128)(2,1)}, bf16[96,640]{1,0:T(8,128)(2,1)S(1)}, u32[]{:S(2)}, u32[]{:S(2)}) collective-permute-start(bf16[96,640]{1,0:T(8,128)(2,1)} %bitcast.11), channel_id=1, source_target_pairs={{384,0},{0,128},{128,256},{256,384},{385,1},{1,129},{129,257},{257... | collective-permute-start | bytes 368648 | tf_op jit(solution)/shard_map/ppermute | solution.py:369
  7.3 23.3 %collective-permute-start.2 = (bf16[96,640]{1,0:T(8,128)(2,1)}, bf16[96,640]{1,0:T(8,128)(2,1)S(1)}, u32[]{:S(2)}, u32[]{:S(2)}) collective-permute-start(bf16[96,640]{1,0:T(8,128)(2,1)} %bitcast.12), channel_id=1, source_target_pairs={{256,0},{384,128},{0,256},{128,384},{257,1},{385,129},{1,257},{129... | collective-permute-start | bytes 368648 | tf_op jit(solution)/shard_map/ppermute | solution.py:369
  11.0 0.9 copy-start.2
  11.9 0.9 copy-start.3
  14.9 43.8 %all-to-all-start = ((bf16[32,64,128]{2,1,0:T(8,128)(2,1)}), bf16[32,64,128]{2,1,0:T(8,128)(2,1)S(1)}, u32[]{:S(2)}, u32[]{:S(2)}) async-start(bf16[32,64,128]{2,1,0:T(8,128)(2,1)} %shard_map.73), calls=%async_computation | async-start | bytes 1048576 | tf_op jit(solution)/shard_map/all_to_all | solution.py:359
  31.6 24.1 %collective-permute-start.3 = (bf16[4,96,640]{2,1,0:T(8,128)(2,1)S(1)}, bf16[4,96,640]{2,1,0:T(8,128)(2,1)S(1)}, u32[]{:S(2)}, u32[]{:S(2)}) collective-permute-start(bf16[4,96,640]{2,1,0:T(8,128)(2,1)S(1)} %pad_maximum_fusion.refs_0_), channel_id=1, source_target_pairs={{0,64},{64,0},{1,65},{65,1},{2,66},{66,2},{3,67},{67,3},{4,68},{68... | collective-permute-start | bytes 1474568 | tf_op jit(solution)/shard_map/ppermute | solution.py:372
  34.7 30.0 %collective-permute-start.4 = (bf16[4,96,640]{2,1,0:T(8,128)(2,1)S(1)}, bf16[4,96,640]{2,1,0:T(8,128)(2,1)S(1)}, u32[]{:S(2)}, u32[]{:S(2)}) collective-permute-start(bf16[4,96,640]{2,1,0:T(8,128)(2,1)S(1)} %pad_maximum_fusion.refs_0_), channel_id=1, source_target_pairs={{0,32},{32,0},{1,33},{33,1},{2,34},{34,2},{3,35},{35,3},{4,36},{36... | collective-permute-start | bytes 1474568 | tf_op jit(solution)/shard_map/ppermute | solution.py:373
  55.7 9.0 %collective-permute-start.5 = (bf16[4,96,640]{2,1,0:T(8,128)(2,1)S(1)}, bf16[4,96,640]{2,1,0:T(8,128)(2,1)S(1)}, u32[]{:S(2)}, u32[]{:S(2)}) collective-permute-start(bf16[4,96,640]{2,1,0:T(8,128)(2,1)S(1)} %collective-permute-done.3.refs_1_), channel_id=1, source_target_pairs={{0,32},{32,0},{1,33},{33,1},{2,34},{34,2},{3,35},{35,3},{4,36},{36... | collective-permute-start | bytes 1474568 | tf_op jit(solution)/shard_map/ppermute | solution.py:373
  59.3 9.6 %all-to-all-start.1 = ((f32[16,8,128]{2,1,0:T(8,128)}), f32[16,8,128]{2,1,0:T(8,128)S(1)}, u32[]{:S(2)}, u32[]{:S(2)}) async-start(f32[16,8,128]{2,1,0:T(8,128)} %shard_map.74), calls=%async_computation.1 | async-start | bytes 131072 | tf_op jit(solution)/shard_map/all_to_all | solution.py:359
  71.0 7.4 %collective-permute-start.6 = (f32[16,8,128]{2,1,0:T(8,128)S(1)}, f32[16,8,128]{2,1,0:T(8,128)S(1)}, u32[]{:S(2)}, u32[]{:S(2)}) collective-permute-start(f32[16,8,128]{2,1,0:T(8,128)S(1)} %get-tuple-element.9), channel_id=1, source_target_pairs={{0,1},{1,2},{2,3},{3,4},{4,5},{5,6},{6,7},{7,8},{8,9},{9,10},{10,1... | collective-permute-start | bytes 196616 | tf_op jit(solution)/shard_map/ppermute | solution.py:398
  73.6 5.4 %copy-start.4 = (s32[16]{0:T(128)S(1)}, s32[16]{0:T(128)}, u32[]{:S(2)}) copy-start(s32[16]{0:T(128)} %anc_ref.1) | copy-start | bytes 196
  73.6 5.4 %collective-permute-start.7 = (f32[16,8,128]{2,1,0:T(8,128)S(1)}, f32[16,8,128]{2,1,0:T(8,128)S(1)}, u32[]{:S(2)}, u32[]{:S(2)}) collective-permute-start(f32[16,8,128]{2,1,0:T(8,128)S(1)} %get-tuple-element.10), channel_id=1, source_target_pairs={{1,0},{2,1},{3,2},{4,3},{5,4},{6,5},{7,6},{8,7},{9,8},{10,9},{11,1... | collective-permute-start | bytes 196616 | tf_op jit(solution)/shard_map/ppermute | solution.py:399
  74.9 40.3 %copy-start = (bf16[640,1920]{1,0:T(8,128)(2,1)S(1)}, bf16[640,1920]{1,0:T(8,128)(2,1)}, u32[]{:S(2)}) copy-start(bf16[640,1920]{1,0:T(8,128)(2,1)} %w_ref.4) | copy-start | bytes 7372804
  142.8 25.0 %copy-start.1 = (bf16[640,640]{1,0:T(8,128)(2,1)S(1)}, bf16[640,640]{1,0:T(8,128)(2,1)}, u32[]{:S(2)}) copy-start(bf16[640,640]{1,0:T(8,128)(2,1)} %w_ref.5) | copy-start | bytes 2457604

commit v5 on v4

--- a/solution.py
+++ b/solution.py
@@ -33,6 +33,7 @@
 BF16 = jnp.bfloat16
 SMEM = pl.BlockSpec(memory_space=pltpu.SMEM)
 VMEM = pl.BlockSpec(memory_space=pltpu.VMEM)
+ANY = pl.BlockSpec(memory_space=pl.ANY)
 
 
 def call(kernel, out_shape, in_specs, flops, size, vmem=16, scratch=()):
@@ -90,7 +91,7 @@
     return parts
 
 
-def pick_kernel(place_ref, x_ref, w_ref, out_ref):
+def pick_kernel(place_ref, x_ref, w_ref, _, out_ref):
     row, col = iota((48, CHANS), 0), iota((48, CHANS), 1)
     chosen = ((col == row + place_ref[0] * SLICE) & (row < SLICE)).astype(F32).astype(BF16)
     picked = lax.dot_general(chosen, w_ref[...], NT, preferred_element_type=F32)
@@ -365,15 +366,17 @@
     place = jnp.stack([particle] + [lax.axis_index(a).astype(jnp.int32) for a in PART])
 
     swap = [(0, 1), (1, 0)]
-    along = [slab] + [
-        lax.ppermute(slab, "x", [((i + d) % 4, i) for i in range(4)]) for d in STEPS[1:]
-    ]
-    four = jnp.stack(along)
-    eight = [four, lax.ppermute(four, "z_lo", swap)]
+    opposite = lax.ppermute(slab, "z_lo", swap)
+
+    def along(values):
+        turns = [[((i + d) % 4, i) for i in range(4)] for d in STEPS[1:]]
+        return jnp.stack([values] + [lax.ppermute(values, "x", turn) for turn in turns])
+
+    eight = [along(slab), along(opposite)]
     slabs = eight + [lax.ppermute(values, "core", swap) for values in eight]
 
-    picked = call(pick_kernel, shaped(ROW_DEVS, 64, LANES), [SMEM, VMEM, VMEM], 10**7, 10**6)(
-        place, slab, conv_weight
+    picked = call(pick_kernel, shaped(ROW_DEVS, 64, LANES), [SMEM, VMEM, VMEM, ANY], 10**7, 10**6)(
+        place, slab, conv_weight, opposite
     )
     picked = exchange(picked, ROWS)
     totals = call(total_kernel, shaped(PARTICLES, 8, LANES, dtype=F32), [VMEM], 10**5, 10**5)(picked)

time: 172 us -> 170 us (0.988)
  waiting for transfers between devices: 21.9 us -> 6.63 us
  starting transfers between devices: 44.3 us -> 58 us
    ppermute x4 -> x7, waiting for transfers between devices: 17 us -> 2.39 us  [the longest x1 2.38 us: per_device(): opposite = lax.ppermute(slab, 'z_lo', swap)]
    ppermute x4 -> x7, starting transfers between devices: 14 us -> 23.9 us  [the longest x6 19 us: along(): lax.ppermute(values, 'x', turn)]
  transfers between devices with their start and end apart: 10 -> 13, of which waited for: 3 -> 2; matrix products, arithmetic and copies ran while one was open for 1% -> 1% of each run, Pallas kernels for 5% -> 3%
where the time goes in v5:
time: 170 us; the launch traced here: 167 us
  blocking collectives  81.1 us (48%)
  starting transfers between devices  58 us (34%)
  Pallas kernels  18.2 us (11%)
  waiting for transfers between devices  6.63 us (4%)
  local copies, waits for them, and re-layouts  1.87 us (1%)
    all_to_all x4, blocking collectives, exchange(): return lax.all_to_all(values, axes, split_axis=0, concat_axis=0, tiled=True)  81.1 us
    all_to_all x2, starting transfers between devices, exchange(): return lax.all_to_all(values, axes, split_axis=0, concat_axis=0, tiled=True)  20.2 us
    ppermute x6, starting transfers between devices, along(): lax.ppermute(values, 'x', turn)  19 us
    ppermute x2, starting transfers between devices, per_device(): slabs = eight + [lax.ppermute(values, 'core', swap) for values in eight]  8.59 us
    ppermute x1, starting transfers between devices, per_device(): opposite = lax.ppermute(slab, 'z_lo', swap)  4.95 us
    pallas_call x1, Pallas kernels, per_device(): call(attend_kernel, shaped(ROW_DEVS, 16, LANES), [VMEM], 2 * 10 ** 9, 2 *...  4.55 us
    all_to_all x2, waiting for transfers between devices, exchange(): return lax.all_to_all(values, axes, split_axis=0, concat_axis=0, tiled=True)  4.23 us
    ppermute x1, starting transfers between devices, per_device(): above = lax.ppermute(down, ROWS, [(i, i + 1) for i in range(ROW_DEVS - 1)])  4.05 us
  transfers between devices with their start and end apart: 13, of which 2 were waited for; matrix products, arithmetic and copies ran while one was open for 1% of the time, Pallas kernels for 3%

profile of v5, /device:TPU:1, one launch (start us, length us, event | category | flops | bytes accessed | tf_op | source)
XLA Modules:
  0.0 167.3 jit_solution(1578976049019803736)
XLA Ops:
  0.0 5.0 %collective-permute-start = (bf16[96,640]{1,0:T(8,128)(2,1)}, bf16[96,640]{1,0:T(8,128)(2,1)S(1)}, u32[]{:S(2)}, u32[]{:S(2)}) collective-permute-start(bf16[96,640]{1,0:T(8,128)(2,1)} %bitcast.14), channel_id=1, source_target_pairs={{0,64},{64,0},{1,65},{65,1},{2,66},{66,2},{3,67},{67,3},{4,68},{68... | collective-permute-start | bytes 368648 | tf_op jit(solution)/shard_map/ppermute | solution.py:369
  5.0 0.1 pad_add_fusion.place_ref
  5.1 2.4 %collective-permute-done._ = bf16[96,640]{1,0:T(8,128)(2,1)S(1)} collective-permute-done((bf16[96,640]{1,0:T(8,128)(2,1)}, bf16[96,640]{1,0:T(8,128)(2,1)S(1)}, u32[]{:S(2)}, u32[]{:S(2)}) %collective-permute-start) | collective-permute-done | bytes 122912 | tf_op jit(solution)/shard_map/ppermute | solution.py:369
  7.4 0.9 copy-done.2
  8.3 0.9 copy-done.3
  9.3 2.0 %shard_map.73 = bf16[32,64,128]{2,1,0:T(8,128)(2,1)} custom-call(s32[4]{0:T(128)S(1)} %pad_add_fusion.place_ref, bf16[96,640]{1,0:T(8,128)(2,1)S(1)} %bitcast.19, bf16[180,640]{1,0:T(8,128)(2,1)S(1)} %copy-done.3, bf16[96,640]{1,0:T(8,128)(2,1)S(1)} %collective-permute-done._), custom_call_target="tpu_custom_call" | custom-call | flops 10000000 | bytes 1000000 | tf_op jit(solution)/shard_map/pallas_call | solution.py:378
  11.3 15.5 %all-to-all-start = ((bf16[32,64,128]{2,1,0:T(8,128)(2,1)}), bf16[32,64,128]{2,1,0:T(8,128)(2,1)S(1)}, u32[]{:S(2)}, u32[]{:S(2)}) async-start(bf16[32,64,128]{2,1,0:T(8,128)(2,1)} %shard_map.73), calls=%async_computation | async-start | bytes 1048576 | tf_op jit(solution)/shard_map/all_to_all | solution.py:360
  26.8 4.4 %collective-permute-start.1 = (bf16[96,640]{1,0:T(8,128)(2,1)}, bf16[96,640]{1,0:T(8,128)(2,1)S(1)}, u32[]{:S(2)}, u32[]{:S(2)}) collective-permute-start(bf16[96,640]{1,0:T(8,128)(2,1)} %bitcast.15), channel_id=1, source_target_pairs={{128,0},{256,128},{384,256},{0,384},{129,1},{257,129},{385,257},{1... | collective-permute-start | bytes 368648 | tf_op jit(solution)/shard_map/ppermute | solution.py:373
  31.2 1.9 %collective-permute-start.2 = (bf16[96,640]{1,0:T(8,128)(2,1)}, bf16[96,640]{1,0:T(8,128)(2,1)S(1)}, u32[]{:S(2)}, u32[]{:S(2)}) collective-permute-start(bf16[96,640]{1,0:T(8,128)(2,1)} %bitcast.16), channel_id=1, source_target_pairs={{384,0},{0,128},{128,256},{256,384},{385,1},{1,129},{129,257},{257... | collective-permute-start | bytes 368648 | tf_op jit(solution)/shard_map/ppermute | solution.py:373
  33.1 3.6 %collective-permute-start.3 = (bf16[96,640]{1,0:T(8,128)(2,1)}, bf16[96,640]{1,0:T(8,128)(2,1)S(1)}, u32[]{:S(2)}, u32[]{:S(2)}) collective-permute-start(bf16[96,640]{1,0:T(8,128)(2,1)} %bitcast.17), channel_id=1, source_target_pairs={{256,0},{384,128},{0,256},{128,384},{257,1},{385,129},{1,257},{129... | collective-permute-start | bytes 368648 | tf_op jit(solution)/shard_map/ppermute | solution.py:373
  36.8 2.9 %collective-permute-start.4 = (bf16[96,640]{1,0:T(8,128)(2,1)S(1)}, bf16[96,640]{1,0:T(8,128)(2,1)S(1)}, u32[]{:S(2)}, u32[]{:S(2)}) collective-permute-start(bf16[96,640]{1,0:T(8,128)(2,1)S(1)} %collective-permute-done._), channel_id=1, source_target_pairs={{128,0},{256,128},{384,256},{0,384},{129,1},{257,129},{385,257},{1... | collective-permute-start | bytes 368648 | tf_op jit(solution)/shard_map/ppermute | solution.py:373
  39.6 2.5 %collective-permute-start.5 = (bf16[96,640]{1,0:T(8,128)(2,1)S(1)}, bf16[96,640]{1,0:T(8,128)(2,1)S(1)}, u32[]{:S(2)}, u32[]{:S(2)}) collective-permute-start(bf16[96,640]{1,0:T(8,128)(2,1)S(1)} %collective-permute-done._), channel_id=1, source_target_pairs={{384,0},{0,128},{128,256},{256,384},{385,1},{1,129},{129,257},{257... | collective-permute-start | bytes 368648 | tf_op jit(solution)/shard_map/ppermute | solution.py:373
  42.1 0.0 collective-permute-done.1
  42.1 3.7 %collective-permute-start.6 = (bf16[96,640]{1,0:T(8,128)(2,1)S(1)}, bf16[96,640]{1,0:T(8,128)(2,1)S(1)}, u32[]{:S(2)}, u32[]{:S(2)}) collective-permute-start(bf16[96,640]{1,0:T(8,128)(2,1)S(1)} %collective-permute-done._), channel_id=1, source_target_pairs={{256,0},{384,128},{0,256},{128,384},{257,1},{385,129},{1,257},{129... | collective-permute-start | bytes 368648 | tf_op jit(solution)/shard_map/ppermute | solution.py:373
  45.8 0.0 collective-permute-done.2
  45.8 0.0 collective-permute-done.3
  45.9 1.0 pad_maximum_fusion.refs_0_
  46.8 5.1 %collective-permute-start.7 = (bf16[4,96,640]{2,1,0:T(8,128)(2,1)S(1)}, bf16[4,96,640]{2,1,0:T(8,128)(2,1)S(1)}, u32[]{:S(2)}, u32[]{:S(2)}) collective-permute-start(bf16[4,96,640]{2,1,0:T(8,128)(2,1)S(1)} %pad_maximum_fusion.refs_0_), channel_id=1, source_target_pairs={{0,32},{32,0},{1,33},{33,1},{2,34},{34,2},{3,35},{35,3},{4,36},{36... | collective-permute-start | bytes 1474568 | tf_op jit(solution)/shard_map/ppermute | solution.py:376
  52.0 0.0 collective-permute-done.4
  52.0 0.0 collective-permute-done.5
  52.0 0.0 collective-permute-done.6
  52.0 0.1 pad_maximum_fusion.1.refs_1_
  52.1 3.5 %collective-permute-start.8 = (bf16[4,96,640]{2,1,0:T(8,128)(2,1)S(1)}, bf16[4,96,640]{2,1,0:T(8,128)(2,1)S(1)}, u32[]{:S(2)}, u32[]{:S(2)}) collective-permute-start(bf16[4,96,640]{2,1,0:T(8,128)(2,1)S(1)} %pad_maximum_fusion.1.refs_1_), channel_id=1, source_target_pairs={{0,32},{32,0},{1,33},{33,1},{2,34},{34,2},{3,35},{35,3},{4,36},{36... | collective-permute-start | bytes 1474568 | tf_op jit(solution)/shard_map/ppermute | solution.py:376
  55.6 0.0 all-to-all-done.x_ref
  55.6 0.7 shard_map.74
  56.2 4.7 %all-to-all-start.1 = ((f32[16,8,128]{2,1,0:T(8,128)}), f32[16,8,128]{2,1,0:T(8,128)S(1)}, u32[]{:S(2)}, u32[]{:S(2)}) async-start(f32[16,8,128]{2,1,0:T(8,128)} %shard_map.74), calls=%async_computation.1 | async-start | bytes 131072 | tf_op jit(solution)/shard_map/all_to_all | solution.py:360
  60.9 0.0 copy-done.5
  61.0 1.5 shard_map.75.w_ref
  62.5 0.0 collective-permute-done.7.refs_2_
  62.5 0.0 collective-permute-done.8.refs_3_
  62.5 4.2 %all-to-all-done.1.totals_ref = f32[16,8,128]{2,1,0:T(8,128)S(1)} async-done(((f32[16,8,128]{2,1,0:T(8,128)}), f32[16,8,128]{2,1,0:T(8,128)S(1)}, u32[]{:S(2)}, u32[]{:S(2)}) %all-to-all-start.1) | async-done | bytes 65568 | tf_op jit(solution)/shard_map/all_to_all | solution.py:360
  66.7 2.0 %shard_map.77 = (f32[16,8,128]{2,1,0:T(8,128)S(1)}, f32[16,8,128]{2,1,0:T(8,128)S(1)}) custom-call(s32[4]{0:T(128)S(1)} %pad_add_fusion.place_ref, f32[16,8,128]{2,1,0:T(8,128)S(1)} %all-to-all-done.1.totals_ref, f32[1,640]{1,0:T(1,128)S(1)} %broadcast_in_dim.6.scale_ref, f32[1,640]{1,0:T(1,128)S(1)} %broadcast_in_dim.7.shift_ref, ...), custom_call_target="tpu_custom_call" | custom-call | flops 100000000 | bytes 1000000 | tf_op jit(solution)/shard_map/pallas_call | solution.py:398
  68.8 1.3 collective-permute-start.10
  70.1 0.0 copy-start.4
  70.1 4.0 %collective-permute-start.9 = (f32[16,8,128]{2,1,0:T(8,128)S(1)}, f32[16,8,128]{2,1,0:T(8,128)S(1)}, u32[]{:S(2)}, u32[]{:S(2)}) collective-permute-start(f32[16,8,128]{2,1,0:T(8,128)S(1)} %get-tuple-element.9), channel_id=1, source_target_pairs={{0,1},{1,2},{2,3},{3,4},{4,5},{5,6},{6,7},{7,8},{8,9},{9,10},{10,1... | collective-permute-start | bytes 196616 | tf_op jit(solution)/shard_map/ppermute | solution.py:401
  74.1 0.0 copy-start
  74.2 3.4 %shard_map.76.part_ref = f32[16,96,128]{2,1,0:T(8,128)S(1)} custom-call(s32[4]{0:T(128)S(1)} %pad_add_fusion.place_ref, f32[16,8,128]{2,1,0:T(8,128)S(1)} %all-to-all-done.1.totals_ref, f32[1,640]{1,0:T(1,128)S(1)} %broadcast_in_dim.6.scale_ref, f32[1,640]{1,0:T(1,128)S(1)} %broadcast_in_dim.7.shift_ref, bf16[384,640]{1,0:T(8,128)(2,1)S(1)} %shard_map.75.w_ref, ...), custom_call_target="tpu_custom_call" | custom-call | flops 2000000000 | bytes 4000000 | tf_op jit(solution)/shard_map/pallas_call | solution.py:403
  77.6 0.0 collective-permute-done.10.below_ref
  77.6 0.0 collective-permute-done.9.above_ref
  77.6 1.2 shard_map.78
  78.8 9.6 %all_to_all.30.x_ref = bf16[16,32,128]{2,1,0:T(8,128)(2,1)S(1)} all-to-all(bf16[16,32,128]{2,1,0:T(8,128)(2,1)S(1)} %shard_map.78), channel_id=1, replica_groups=mesh['x'=4,'z_lo'=2,'core'=2,'z_hi'=4,'y'=8] {'x','z_lo','core'}, dimensions={0} | all-to-all | bytes 262144 | tf_op jit(solution)/shard_map/all_to_all | solution.py:360
  88.3 0.7 shard_map.79
  89.1 24.6 %all_to_all.31.totals_ref = f32[32,8,128]{2,1,0:T(8,128)S(1)} all-to-all(f32[32,8,128]{2,1,0:T(8,128)S(1)} %get-tuple-element.11), channel_id=1, replica_groups=mesh['x'=4,'z_lo'=2,'core'=2,'z_hi'=4,'y'=8] {'z_hi','y'}, dimensions={0} | all-to-all | bytes 262144 | tf_op jit(solution)/shard_map/all_to_all | solution.py:360
  113.7 1.1 shard_map.80
  114.8 26.5 %all_to_all.32.x_ref = bf16[32,112,128]{2,1,0:T(8,128)(2,1)S(1)} all-to-all(bf16[32,112,128]{2,1,0:T(8,128)(2,1)S(1)} %shard_map.80), channel_id=1, replica_groups=mesh['x'=4,'z_lo'=2,'core'=2,'z_hi'=4,'y'=8] {'z_hi','y'}, dimensions={0} | all-to-all | bytes 1835008 | tf_op jit(solution)/shard_map/all_to_all | solution.py:360
  141.3 4.5 %shard_map.81 = bf16[32,16,128]{2,1,0:T(8,128)(2,1)S(1)} custom-call(bf16[32,112,128]{2,1,0:T(8,128)(2,1)S(1)} %all_to_all.32.x_ref), custom_call_target="tpu_custom_call" | custom-call | flops 2000000000 | bytes 2000000 | tf_op jit(solution)/shard_map/pallas_call | solution.py:435
  145.8 20.5 %all_to_all.33.x_ref = bf16[32,16,128]{2,1,0:T(8,128)(2,1)S(1)} all-to-all(bf16[32,16,128]{2,1,0:T(8,128)(2,1)S(1)} %shard_map.81), channel_id=1, replica_groups=mesh['x'=4,'z_lo'=2,'core'=2,'z_hi'=4,'y'=8] {'z_hi','y'}, dimensions={0} | all-to-all | bytes 262144 | tf_op jit(solution)/shard_map/all_to_all | solution.py:360
  166.3 1.0 shard_map.82
  (11 shorter events, 0.0 us)
Async XLA Ops:
  0.0 60.9 %copy-start.5 = (f32[640]{0:T(1024)S(1)}, f32[640]{0:T(1024)}, u32[]{:S(2)}) copy-start(f32[640]{0:T(1024)} %param.8) | copy-start | bytes 7684
  0.0 60.9 %copy-start.6 = (f32[640]{0:T(1024)S(1)}, f32[640]{0:T(1024)}, u32[]{:S(2)}) copy-start(f32[640]{0:T(1024)} %param.9) | copy-start | bytes 7684
  0.0 7.4 %collective-permute-start = (bf16[96,640]{1,0:T(8,128)(2,1)}, bf16[96,640]{1,0:T(8,128)(2,1)S(1)}, u32[]{:S(2)}, u32[]{:S(2)}) collective-permute-start(bf16[96,640]{1,0:T(8,128)(2,1)} %bitcast.14), channel_id=1, source_target_pairs={{0,64},{64,0},{1,65},{65,1},{2,66},{66,2},{3,67},{67,3},{4,68},{68... | collective-permute-start | bytes 368648 | tf_op jit(solution)/shard_map/ppermute | solution.py:369
  7.4 0.9 copy-start.2
  8.3 0.9 copy-start.3
  11.3 44.3 %all-to-all-start = ((bf16[32,64,128]{2,1,0:T(8,128)(2,1)}), bf16[32,64,128]{2,1,0:T(8,128)(2,1)S(1)}, u32[]{:S(2)}, u32[]{:S(2)}) async-start(bf16[32,64,128]{2,1,0:T(8,128)(2,1)} %shard_map.73), calls=%async_computation | async-start | bytes 1048576 | tf_op jit(solution)/shard_map/all_to_all | solution.py:360
  26.8 15.3 %collective-permute-start.1 = (bf16[96,640]{1,0:T(8,128)(2,1)}, bf16[96,640]{1,0:T(8,128)(2,1)S(1)}, u32[]{:S(2)}, u32[]{:S(2)}) collective-permute-start(bf16[96,640]{1,0:T(8,128)(2,1)} %bitcast.15), channel_id=1, source_target_pairs={{128,0},{256,128},{384,256},{0,384},{129,1},{257,129},{385,257},{1... | collective-permute-start | bytes 368648 | tf_op jit(solution)/shard_map/ppermute | solution.py:373
  31.2 14.7 %collective-permute-start.2 = (bf16[96,640]{1,0:T(8,128)(2,1)}, bf16[96,640]{1,0:T(8,128)(2,1)S(1)}, u32[]{:S(2)}, u32[]{:S(2)}) collective-permute-start(bf16[96,640]{1,0:T(8,128)(2,1)} %bitcast.16), channel_id=1, source_target_pairs={{384,0},{0,128},{128,256},{256,384},{385,1},{1,129},{129,257},{257... | collective-permute-start | bytes 368648 | tf_op jit(solution)/shard_map/ppermute | solution.py:373
  33.1 12.7 %collective-permute-start.3 = (bf16[96,640]{1,0:T(8,128)(2,1)}, bf16[96,640]{1,0:T(8,128)(2,1)S(1)}, u32[]{:S(2)}, u32[]{:S(2)}) collective-permute-start(bf16[96,640]{1,0:T(8,128)(2,1)} %bitcast.17), channel_id=1, source_target_pairs={{256,0},{384,128},{0,256},{128,384},{257,1},{385,129},{1,257},{129... | collective-permute-start | bytes 368648 | tf_op jit(solution)/shard_map/ppermute | solution.py:373
  36.8 15.2 %collective-permute-start.4 = (bf16[96,640]{1,0:T(8,128)(2,1)S(1)}, bf16[96,640]{1,0:T(8,128)(2,1)S(1)}, u32[]{:S(2)}, u32[]{:S(2)}) collective-permute-start(bf16[96,640]{1,0:T(8,128)(2,1)S(1)} %collective-permute-done._), channel_id=1, source_target_pairs={{128,0},{256,128},{384,256},{0,384},{129,1},{257,129},{385,257},{1... | collective-permute-start | bytes 368648 | tf_op jit(solution)/shard_map/ppermute | solution.py:373
  39.6 12.4 %collective-permute-start.5 = (bf16[96,640]{1,0:T(8,128)(2,1)S(1)}, bf16[96,640]{1,0:T(8,128)(2,1)S(1)}, u32[]{:S(2)}, u32[]{:S(2)}) collective-permute-start(bf16[96,640]{1,0:T(8,128)(2,1)S(1)} %collective-permute-done._), channel_id=1, source_target_pairs={{384,0},{0,128},{128,256},{256,384},{385,1},{1,129},{129,257},{257... | collective-permute-start | bytes 368648 | tf_op jit(solution)/shard_map/ppermute | solution.py:373
  42.1 9.9 %collective-permute-start.6 = (bf16[96,640]{1,0:T(8,128)(2,1)S(1)}, bf16[96,640]{1,0:T(8,128)(2,1)S(1)}, u32[]{:S(2)}, u32[]{:S(2)}) collective-permute-start(bf16[96,640]{1,0:T(8,128)(2,1)S(1)} %collective-permute-done._), channel_id=1, source_target_pairs={{256,0},{384,128},{0,256},{128,384},{257,1},{385,129},{1,257},{129... | collective-permute-start | bytes 368648 | tf_op jit(solution)/shard_map/ppermute | solution.py:373
  46.8 15.7 %collective-permute-start.7 = (bf16[4,96,640]{2,1,0:T(8,128)(2,1)S(1)}, bf16[4,96,640]{2,1,0:T(8,128)(2,1)S(1)}, u32[]{:S(2)}, u32[]{:S(2)}) collective-permute-start(bf16[4,96,640]{2,1,0:T(8,128)(2,1)S(1)} %pad_maximum_fusion.refs_0_), channel_id=1, source_target_pairs={{0,32},{32,0},{1,33},{33,1},{2,34},{34,2},{3,35},{35,3},{4,36},{36... | collective-permute-start | bytes 1474568 | tf_op jit(solution)/shard_map/ppermute | solution.py:376
  52.1 10.4 %collective-permute-start.8 = (bf16[4,96,640]{2,1,0:T(8,128)(2,1)S(1)}, bf16[4,96,640]{2,1,0:T(8,128)(2,1)S(1)}, u32[]{:S(2)}, u32[]{:S(2)}) collective-permute-start(bf16[4,96,640]{2,1,0:T(8,128)(2,1)S(1)} %pad_maximum_fusion.1.refs_1_), channel_id=1, source_target_pairs={{0,32},{32,0},{1,33},{33,1},{2,34},{34,2},{3,35},{35,3},{4,36},{36... | collective-permute-start | bytes 1474568 | tf_op jit(solution)/shard_map/ppermute | solution.py:376
  56.2 10.5 %all-to-all-start.1 = ((f32[16,8,128]{2,1,0:T(8,128)}), f32[16,8,128]{2,1,0:T(8,128)S(1)}, u32[]{:S(2)}, u32[]{:S(2)}) async-start(f32[16,8,128]{2,1,0:T(8,128)} %shard_map.74), calls=%async_computation.1 | async-start | bytes 131072 | tf_op jit(solution)/shard_map/all_to_all | solution.py:360
  68.8 8.8 %collective-permute-start.10 = (f32[16,8,128]{2,1,0:T(8,128)S(1)}, f32[16,8,128]{2,1,0:T(8,128)S(1)}, u32[]{:S(2)}, u32[]{:S(2)}) collective-permute-start(f32[16,8,128]{2,1,0:T(8,128)S(1)} %get-tuple-element.10), channel_id=1, source_target_pairs={{1,0},{2,1},{3,2},{4,3},{5,4},{6,5},{7,6},{8,7},{9,8},{10,9},{11,1... | collective-permute-start | bytes 196616 | tf_op jit(solution)/shard_map/ppermute | solution.py:402
  70.1 7.5 %copy-start.4 = (s32[16]{0:T(128)S(1)}, s32[16]{0:T(128)}, u32[]{:S(2)}) copy-start(s32[16]{0:T(128)} %anc_ref.1) | copy-start | bytes 196
  70.1 7.5 %collective-permute-start.9 = (f32[16,8,128]{2,1,0:T(8,128)S(1)}, f32[16,8,128]{2,1,0:T(8,128)S(1)}, u32[]{:S(2)}, u32[]{:S(2)}) collective-permute-start(f32[16,8,128]{2,1,0:T(8,128)S(1)} %get-tuple-element.9), channel_id=1, source_target_pairs={{0,1},{1,2},{2,3},{3,4},{4,5},{5,6},{6,7},{7,8},{8,9},{9,10},{10,1... | collective-permute-start | bytes 196616 | tf_op jit(solution)/shard_map/ppermute | solution.py:401
  74.1 39.5 %copy-start = (bf16[640,1920]{1,0:T(8,128)(2,1)S(1)}, bf16[640,1920]{1,0:T(8,128)(2,1)}, u32[]{:S(2)}) copy-start(bf16[640,1920]{1,0:T(8,128)(2,1)} %w_ref.4) | copy-start | bytes 7372804
  141.3 25.0 %copy-start.1 = (bf16[640,640]{1,0:T(8,128)(2,1)S(1)}, bf16[640,640]{1,0:T(8,128)(2,1)}, u32[]{:S(2)}) copy-start(bf16[640,640]{1,0:T(8,128)(2,1)} %w_ref.5) | copy-start | bytes 2457604

commit v6 on v2

--- a/solution.py
+++ b/solution.py
@@ -1,5 +1,3 @@
-import functools
-
 import jax
 import jax.numpy as jnp
 from jax import lax
@@ -14,7 +12,9 @@
 WIDTH = 24
 ROWS_HERE = 4
 TOKENS = ROWS_HERE * WIDTH
+LAST = TOKENS - WIDTH
 PARTICLES = 16
+HALF = PARTICLES // 2
 ROW_DEVS = 32
 PER_GROUP = CHANS // GROUPS
 SLICE = CHANS // PARTICLES
@@ -26,6 +26,7 @@
 SLOT = TOKENS + 16
 
 PART = ("x", "z_lo", "core")
+CHIPS = ("x", "z_lo")
 ROWS = ("z_hi", "y")
 
 NT = (((1,), (1,)), ((), ()))
@@ -60,15 +61,16 @@
     return jnp.dot(a, b, precision=lax.Precision.HIGHEST, preferred_element_type=F32)
 
 
-def group_row(values):
-    sums = jnp.sum(values, axis=0, keepdims=True)
-    squares = jnp.sum(values * values, axis=0, keepdims=True)
+def group_rows(values):
+    fill = [jnp.zeros((1, CHANS), F32)] * (8 - len(values))
+    sums = jnp.concatenate([jnp.sum(v, axis=0, keepdims=True) for v in values] + fill, axis=0)
+    squares = [jnp.sum(v * v, axis=0, keepdims=True) for v in values] + fill
+    squares = jnp.concatenate(squares, axis=0)
     chan, lane = iota((CHANS, LANES), 0), iota((CHANS, LANES), 1)
     first = ((chan >= lane * PER_GROUP) & (chan < (lane + 1) * PER_GROUP)).astype(F32)
     other = lane - GROUPS
     second = ((chan >= other * PER_GROUP) & (chan < (other + 1) * PER_GROUP)).astype(F32)
-    eight = lambda row: jnp.broadcast_to(row, (8, CHANS))
-    return exact_dot(eight(sums), first) + exact_dot(eight(squares), second)
+    return exact_dot(sums, first) + exact_dot(squares, second)
 
 
 def mean_and_inverse(totals):
@@ -97,22 +99,20 @@
     head = picked[:, :LANES]
     rest = jnp.concatenate([picked[:, LANES:], jnp.zeros((48, LANES - TAIL), F32)], axis=1)
     turned = pltpu.roll(pltpu.roll(rest, 48 - 20, 0), 64, 1)
-    sums = thirds(group_row(x_ref[...].astype(F32)))
-    row, lane = iota((24, LANES), 0), iota((24, LANES), 1)
-    low = jnp.where(lane < 64, rest[:24], turned[:24])
-    for n in range(3):
-        low = jnp.where(row == 20 + n, sums[n][:1], low)
-    low = jnp.where(row == 23, 0.0, low)
-    slot = jnp.concatenate([head[:SLICE], low], axis=0).astype(BF16)
+    low = jnp.where(iota((24, LANES), 1) < 64, rest[:24], turned[:24])
+    values = [x_ref[j].astype(F32) for j in range(HALF)]
+    first, second, third = thirds(group_rows(values))
+    sums = jnp.concatenate([first + pltpu.roll(second, 64, 1), third], axis=0)
+    slot = jnp.concatenate([head[:SLICE], low, sums], axis=0).astype(BF16)
     out_ref[...] = jnp.broadcast_to(slot[None], out_ref.shape)
 
 
 def total_kernel(x_ref, out_ref):
     total = jnp.zeros((16, LANES), F32)
     for r in range(ROW_DEVS):
-        total = total + x_ref[r, 48:64].astype(F32)
-    row = total[12:13] + total[13:14] + total[14:15]
-    out_ref[...] = jnp.broadcast_to(row[None], out_ref.shape)
+        total = total + x_ref[r, 64:80].astype(F32)
+    total = total[:8] + pltpu.roll(total[:8], 64, 1) + total[8:]
+    out_ref[...] = jnp.where(iota((HALF, LANES), 1) < 64, total, 0.0)
 
 
 PLACE = {1: 0, 0: 1, 2: 2}
@@ -125,7 +125,7 @@
         at = r * KERNEL_ROWS
         block, off = at // LANES, at % LANES
         slot = x_ref[r].astype(F32)
-        low = jnp.concatenate([slot[SLICE:], jnp.zeros((16, LANES), F32)], axis=0)
+        low = jnp.concatenate([slot[SLICE:64], jnp.zeros((16, LANES), F32)], axis=0)
         rest = jnp.where(row < 20, low, pltpu.roll(pltpu.roll(low, 20, 0), 64, 1))
         rest = jnp.where(lane < TAIL, rest, 0.0)
         wide = jnp.concatenate([slot[:SLICE], rest, jnp.zeros((SLICE, LANES), F32)], axis=1)
@@ -142,15 +142,13 @@
     out_ref[...] = tall_ref[...].astype(BF16)
 
 
-def gain_and_bias(totals_ref, scale_ref, shift_ref):
-    mean, inverse = mean_and_inverse(totals_ref[:, 0, :])
-    gain = inverse * (1.0 + scale_ref[...])
-    return gain, shift_ref[...] - mean * gain
+def spot(place_ref, q):
+    return lax.rem(lax.rem(q, 2) + place_ref[1], 2) * HALF + q // 2
 
 
 def silu(v):
     half = 0.5 * v
-    return (half + half * jnp.tanh(half)).astype(BF16)
+    return half + half * jnp.tanh(half)
 
 
 def across(full):
@@ -170,76 +168,38 @@
     return out
 
 
-def unpacked(value):
-    return jnp.concatenate(
-        [value] + [pltpu.roll(value, LANES - SLICE * t, 1) for t in (1, 2)], axis=0
-    )
-
-
-def edge_kernel(x_ref, totals_ref, scale_ref, shift_ref, w_ref, up_ref, down_ref):
-    gain, bias = gain_and_bias(totals_ref, scale_ref, shift_ref)
-    for rows, tap, ref in (
-        (slice(0, WIDTH), 2, up_ref),
-        (slice(TOKENS - WIDTH, TOKENS), 0, down_ref),
-    ):
-        active = []
-        for q in range(PARTICLES):
-            x = x_ref[q].astype(F32)[rows]
-            active.append(silu(x * gain[q : q + 1] + bias[q : q + 1]))
-        active = jnp.concatenate(active, axis=0)
-        weights = w_ref[tap * LANES : (tap + 1) * LANES, :]
-        full = lax.dot_general(active, weights, NT, preferred_element_type=F32)
-        full = across(full)
-        for q in range(PARTICLES):
-            ref[q] = packed(full[q * WIDTH : (q + 1) * WIDTH])
-
-
-def conv_kernel(place_ref, x_ref, totals_ref, scale_ref, shift_ref, w_ref, part_ref):
-    gain, bias = gain_and_bias(totals_ref, scale_ref, shift_ref)
+def conv_kernel(place_ref, anc_ref, scale_ref, shift_ref, w_ref, *refs):
+    totals, slabs, edges, (out_ref, done_ref) = refs[:2], refs[2:4], refs[4:6], refs[6:]
+    mean, inverse = mean_and_inverse(jnp.concatenate([ref[...] for ref in totals], axis=0))
+    gain = inverse * (1.0 + scale_ref[...])
+    bias = shift_ref[...] - mean * gain
     row, col = iota((LANES, CHANS), 0), iota((LANES, CHANS), 1)
     chosen = ((col == row + place_ref[0] * SLICE) & (row < SLICE)).astype(F32).astype(BF16)
     weights = w_ref[...]
+    top, bottom = place_ref[2] == 0, place_ref[2] == ROW_DEVS - 1
     each = 2
-    last = TOKENS - WIDTH
     for step in range(PARTICLES // each):
         active, raw = [], []
-        for q in range(step * each, (step + 1) * each):
-            x = x_ref[q]
+        for n in range(step * each, (step + 1) * each):
+            which, j = n // HALF, n % HALF
+            x = slabs[which][j]
             raw.append(x)
-            active.append(silu(x.astype(F32) * gain[q : q + 1] + bias[q : q + 1]))
-        active = jnp.concatenate(active, axis=0)
+            act = lambda v: silu(v.astype(F32) * gain[n : n + 1] + bias[n : n + 1])
+            above, below = act(edges[which][0, j]), act(edges[which][1, j])
+            active += [jnp.where(top, 0.0, above), act(x), jnp.where(bottom, 0.0, below)]
+        active = jnp.concatenate(active, axis=0).astype(BF16)
         raw = jnp.concatenate(raw, axis=0)
         taps = lax.dot_general(active, weights, NT, preferred_element_type=F32)
         field = lax.dot_general(raw, chosen, NT, preferred_element_type=F32)
         for k in range(each):
-            rows = slice(k * TOKENS, (k + 1) * TOKENS)
-            t0, t1, t2 = (taps[rows, n * LANES : (n + 1) * LANES] for n in range(3))
-            base = t1 + field[rows]
-            full = jnp.concatenate(
-                [
-                    base[:WIDTH] + t2[WIDTH : 2 * WIDTH],
-                    base[WIDTH:last] + t0[: last - WIDTH] + t2[2 * WIDTH :],
-                    base[last:] + t0[last - WIDTH : last],
-                ],
-                axis=0,
-            )
-            part_ref[step * each + k] = across(full)
-
-
-def finish_kernel(anc_ref, part_ref, above_ref, below_ref, out_ref):
-    last = TOKENS - WIDTH
-    lane = iota((TOKENS, LANES), 1)
+            at = k * (TOKENS + 2 * WIDTH)
+            full = field[k * TOKENS : (k + 1) * TOKENS]
+            for a in range(3):
+                rows = slice(at + a * WIDTH, at + a * WIDTH + TOKENS)
+                full = full + taps[rows, a * LANES : (a + 1) * LANES]
+            done_ref[step * each + k] = packed(across(full)).astype(BF16)
     for p in range(PARTICLES):
-        q = anc_ref[p]
-        total = jnp.concatenate(
-            [
-                part_ref[q, :WIDTH] + unpacked(above_ref[q]),
-                part_ref[q, WIDTH:last],
-                part_ref[q, last:] + unpacked(below_ref[q]),
-            ],
-            axis=0,
-        )
-        out_ref[p] = packed(jnp.where(lane < SLICE, total, 0.0)).astype(BF16)
+        out_ref[p] = done_ref[spot(place_ref, anc_ref[p])]
 
 
 def gather_kernel(x_ref, resid_ref, out_ref, wide_ref):
@@ -260,7 +220,7 @@
             wide_ref[32 * t : 32 * (t + 1), n * LANES : (n + 1) * LANES] = value
     wide = wide_ref[...]
     resid_ref[...] = wide.astype(BF16)
-    out_ref[...] = jnp.broadcast_to(group_row(wide)[None], out_ref.shape)
+    out_ref[...] = jnp.broadcast_to(group_rows([wide])[None], out_ref.shape)
 
 
 def project_kernel(totals_ref, resid_ref, w_ref, out_ref, both_ref):
@@ -337,16 +297,25 @@
 
 def per_device(latent, ada_scale, ada_shift, conv_weight, qkv_weight, out_weight, ancestors):
     slab = latent.reshape(TOKENS, CHANS)
-    place = lax.axis_index(PART).astype(jnp.int32)[None]
-
-    slabs = lax.all_gather(slab, PART)
-
-    picked = call(pick_kernel, shaped(ROW_DEVS, 64, LANES), [SMEM, VMEM, VMEM], 10**7, 10**6)(
-        place, slab, conv_weight
+    particle = lax.axis_index(PART).astype(jnp.int32)
+    place = jnp.stack(
+        [particle] + [lax.axis_index(a).astype(jnp.int32) for a in ("core", ROWS)]
+    )
+
+    swap = [(0, 1), (1, 0)]
+    here = exchange(jnp.broadcast_to(slab[None], (HALF, TOKENS, CHANS)), CHIPS)
+    above = lax.ppermute(here[:, LAST:], ROWS, [(i, i + 1) for i in range(ROW_DEVS - 1)])
+    below = lax.ppermute(here[:, :WIDTH], ROWS, [(i + 1, i) for i in range(ROW_DEVS - 1)])
+    edges = jnp.stack([above, below])
+    slabs = [here, lax.ppermute(here, "core", swap)]
+    edges = [edges, lax.ppermute(edges, "core", swap)]
+
+    picked = call(pick_kernel, shaped(ROW_DEVS, 80, LANES), [SMEM, VMEM, VMEM], 10**7, 10**6)(
+        place, here, conv_weight
     )
     picked = exchange(picked, ROWS)
-    totals = call(total_kernel, shaped(PARTICLES, 8, LANES, dtype=F32), [VMEM], 10**5, 10**5)(picked)
-    totals = exchange(totals, PART)
+    totals = call(total_kernel, shaped(HALF, LANES, dtype=F32), [VMEM], 10**5, 10**5)(picked)
+    totals = [totals, lax.ppermute(totals, "core", swap)]
     weights = call(
         weights_kernel,
         shaped(3 * LANES, CHANS),
@@ -358,25 +327,15 @@
             pltpu.VMEM((3 * LANES, CHANS), F32),
         ),
     )(picked)
-
-    scale, shift = ada_scale[None], ada_shift[None]
-    edge = shaped(PARTICLES, WIDTH // 3, LANES, dtype=F32)
-    up, down = call(edge_kernel, [edge, edge], [VMEM] * 5, 10**8, 10**6)(
-        slabs, totals, scale, shift, weights
-    )
-    above = lax.ppermute(down, ROWS, [(i, i + 1) for i in range(ROW_DEVS - 1)])
-    below = lax.ppermute(up, ROWS, [(i + 1, i) for i in range(ROW_DEVS - 1)])
-    part = call(
+    pieces = call(
         conv_kernel,
-        shaped(PARTICLES, TOKENS, LANES, dtype=F32),
-        [SMEM] + [VMEM] * 5,
+        shaped(PARTICLES, 32, LANES),
+        [SMEM, SMEM] + [VMEM] * 9,
         2 * 10**9,
         4 * 10**6,
         vmem=32,
-    )(place, slabs, totals, scale, shift, weights)
-    pieces = call(
-        finish_kernel, shaped(PARTICLES, 32, LANES), [SMEM] + [VMEM] * 3, 10**6, 10**6
-    )(ancestors, part, above, below)
+        scratch=(pltpu.VMEM((PARTICLES, 32, LANES), BF16),),
+    )(place, ancestors, ada_scale[None], ada_shift[None], weights, *totals, *slabs, *edges)
     pieces = exchange(pieces, PART)
 
     resid, sums = call(

time: 174 us -> 166 us (0.954)
  blocking collectives: 115 us -> 82.6 us
  starting transfers between devices: 12.3 us -> 39.5 us
  between operations: 13.5 us -> 0.19 us
  waiting for transfers between devices: 11.1 us -> 22.4 us
    all_to_all x5 -> x4, blocking collectives: 115 us -> 82.6 us  [exchange(): return lax.all_to_all(values, axes, split_axis=0, concat_axis=0, tiled=True)]
    all_to_all x1 -> x2, starting transfers between devices: 8.86 us -> 24 us  [exchange(): return lax.all_to_all(values, axes, split_axis=0, concat_axis=0, tiled=True)]
    ppermute x2 -> x5, starting transfers between devices: 3.4 us -> 15.6 us  [the longest x1 4.35 us: per_device(): slabs = [here, lax.ppermute(here, 'core', swap)]]
    ppermute x2 -> x5, waiting for transfers between devices: 1.71 us -> 11.1 us  [the longest x1 7.92 us: per_device(): lax.ppermute(here[:, LAST:], ROWS, [(i, i + 1) for i in range(ROW_DEVS -...]
    all_to_all x1 -> x2, waiting for transfers between devices: 4.25 us -> 11.3 us  [exchange(): return lax.all_to_all(values, axes, split_axis=0, concat_axis=0, tiled=True)]
    all_gather x1 -> x0, waiting for transfers between devices: 4.44 us -> none  [per_device(): slabs = lax.all_gather(slab, PART)]
    unnamed x18 -> x12, local copies, waits for them, and re-layouts: 3.41 us -> 0.02 us
    broadcast_in_dim x2 -> x3, local copies, waits for them, and re-layouts: 0.01 us -> 1.98 us  [the longest x1 1.97 us: per_device(): here = exchange(jnp.broadcast_to(slab[None], (HALF, TOKENS, CHANS)), CHIPS)]
  transfers between devices with their start and end apart: 4 -> 7, of which waited for: 3 -> 3; matrix products, arithmetic and copies ran while one was open for 0% -> 0% of each run, Pallas kernels for 3% -> 1%
where the time goes in v6:
time: 166 us; the launch traced here: 163 us
  blocking collectives  82.6 us (50%)
  starting transfers between devices  39.5 us (24%)
  waiting for transfers between devices  22.4 us (13%)
  Pallas kernels  16.3 us (10%)
  local copies, waits for them, and re-layouts  2.05 us (1%)
    all_to_all x4, blocking collectives, exchange(): return lax.all_to_all(values, axes, split_axis=0, concat_axis=0, tiled=True)  82.6 us
    all_to_all x2, starting transfers between devices, exchange(): return lax.all_to_all(values, axes, split_axis=0, concat_axis=0, tiled=True)  24 us
    all_to_all x2, waiting for transfers between devices, exchange(): return lax.all_to_all(values, axes, split_axis=0, concat_axis=0, tiled=True)  11.3 us
    ppermute x1, waiting for transfers between devices, per_device(): lax.ppermute(here[:, LAST:], ROWS, [(i, i + 1) for i in range(ROW_DEVS -...  7.92 us
    pallas_call x1, Pallas kernels, per_device(): call(conv_kernel, shaped(PARTICLES, 32, LANES), [SMEM, SMEM] + [VMEM] * 9...  4.92 us
    pallas_call x1, Pallas kernels, per_device(): call(attend_kernel, shaped(ROW_DEVS, 16, LANES), [VMEM], 2 * 10 ** 9, 2 *...  4.54 us
    ppermute x1, starting transfers between devices, per_device(): slabs = [here, lax.ppermute(here, 'core', swap)]  4.35 us
    ppermute x1, starting transfers between devices, per_device(): edges = [edges, lax.ppermute(edges, 'core', swap)]  3.99 us
  transfers between devices with their start and end apart: 7, of which 3 were waited for; matrix products, arithmetic and copies ran while one was open for 0% of the time, Pallas kernels for 1%

profile of v6, /device:TPU:1, one launch (start us, length us, event | category | flops | bytes accessed | tf_op | source)
XLA Modules:
  0.0 163.2 jit_solution(3149454326096930059)
XLA Ops:
  0.0 0.0 copy-start.2
  0.0 2.0 %broadcast_in_dim.16 = bf16[8,96,640]{2,1,0:T(8,128)(2,1)} broadcast(bf16[96,640]{1,0:T(8,128)(2,1)} %bitcast.9), dimensions={1,2} | broadcast | bytes 1105920 | tf_op jit(solution)/shard_map/broadcast_in_dim | solution.py:306
  2.0 6.7 %all-to-all-start = ((bf16[8,96,640]{2,1,0:T(8,128)(2,1)}), bf16[8,96,640]{2,1,0:T(8,128)(2,1)S(1)}, u32[]{:S(2)}, u32[]{:S(2)}) async-start(bf16[8,96,640]{2,1,0:T(8,128)(2,1)} %broadcast_in_dim.16), calls=%async_computation | async-start | bytes 1966080 | tf_op jit(solution)/shard_map/all_to_all | solution.py:295
  8.6 0.1 pad_add_fusion.place_ref
  8.7 0.0 copy-start.4
  8.7 0.0 copy-start.5
  8.7 11.3 %all-to-all-done.x_ref.refs_2_ = bf16[8,96,640]{2,1,0:T(8,128)(2,1)S(1)} async-done(((bf16[8,96,640]{2,1,0:T(8,128)(2,1)}), bf16[8,96,640]{2,1,0:T(8,128)(2,1)S(1)}, u32[]{:S(2)}, u32[]{:S(2)}) %all-to-all-start) | async-done | bytes 983072 | tf_op jit(solution)/shard_map/all_to_all | solution.py:295
  20.0 0.0 copy-done.2
  20.0 2.3 %shard_map.73 = bf16[32,80,128]{2,1,0:T(8,128)(2,1)} custom-call(s32[3]{0:T(128)S(1)} %pad_add_fusion.place_ref, bf16[8,96,640]{2,1,0:T(8,128)(2,1)S(1)} %all-to-all-done.x_ref.refs_2_, bf16[180,640]{1,0:T(8,128)(2,1)S(1)} %copy-done.2), custom_call_target="tpu_custom_call" | custom-call | flops 10000000 | bytes 1000000 | tf_op jit(solution)/shard_map/pallas_call | solution.py:313
  22.4 0.0 copy-start.3
  22.4 17.3 %all-to-all-start.1 = ((bf16[32,80,128]{2,1,0:T(8,128)(2,1)}), bf16[32,80,128]{2,1,0:T(8,128)(2,1)S(1)}, u32[]{:S(2)}, u32[]{:S(2)}) async-start(bf16[32,80,128]{2,1,0:T(8,128)(2,1)} %shard_map.73), calls=%async_computation.1 | async-start | bytes 1310720 | tf_op jit(solution)/shard_map/all_to_all | solution.py:295
  39.7 4.3 %collective-permute-start.1 = (bf16[8,96,640]{2,1,0:T(8,128)(2,1)S(1)}, bf16[8,96,640]{2,1,0:T(8,128)(2,1)S(1)}, u32[]{:S(2)}, u32[]{:S(2)}) collective-permute-start(bf16[8,96,640]{2,1,0:T(8,128)(2,1)S(1)} %all-to-all-done.x_ref.refs_2_), channel_id=1, source_target_pairs={{0,32},{32,0},{1,33},{33,1},{2,34},{34,2},{3,35},{35,3},{4,36},{36... | collective-permute-start | bytes 2949128 | tf_op jit(solution)/shard_map/ppermute | solution.py:310
  44.1 3.4 %collective-permute-start.2 = (bf16[8,24,640]{2,1,0:T(8,128)(2,1)S(1)}, bf16[8,24,640]{2,1,0:T(8,128)(2,1)S(1)}, u32[]{:S(2)}, u32[]{:S(2)}) collective-permute-start(bf16[8,24,640]{2,1,0:T(8,128)(2,1)S(1)} %get-tuple-element.9), channel_id=1, source_target_pairs={{0,1},{1,2},{2,3},{3,4},{4,5},{5,6},{6,7},{7,8},{8,9},{9,10},{10,1... | collective-permute-start | bytes 737288 | tf_op jit(solution)/shard_map/ppermute | solution.py:307
  47.5 1.3 collective-permute-start.3
  48.8 7.9 %collective-permute-done.2 = bf16[8,24,640]{2,1,0:T(8,128)(2,1)S(1)} collective-permute-done((bf16[8,24,640]{2,1,0:T(8,128)(2,1)S(1)}, bf16[8,24,640]{2,1,0:T(8,128)(2,1)S(1)}, u32[]{:S(2)}, u32[]{:S(2)}) %collective-permute-start.2) | collective-permute-done | bytes 245792 | tf_op jit(solution)/shard_map/ppermute | solution.py:307
  56.8 3.2 %collective-permute-done.3 = bf16[8,24,640]{2,1,0:T(8,128)(2,1)S(1)} collective-permute-done((bf16[8,24,640]{2,1,0:T(8,128)(2,1)S(1)}, bf16[8,24,640]{2,1,0:T(8,128)(2,1)S(1)}, u32[]{:S(2)}, u32[]{:S(2)}) %collective-permute-start.3) | collective-permute-done | bytes 245792 | tf_op jit(solution)/shard_map/ppermute | solution.py:308
  59.9 0.1 pad_maximum_fusion.refs_4_
  60.0 4.0 %collective-permute-start.4 = (bf16[2,8,24,640]{3,2,1,0:T(8,128)(2,1)S(1)}, bf16[2,8,24,640]{3,2,1,0:T(8,128)(2,1)}, u32[]{:S(2)}, u32[]{:S(2)}) collective-permute-start(bf16[2,8,24,640]{3,2,1,0:T(8,128)(2,1)S(1)} %pad_maximum_fusion.refs_4_), channel_id=1, source_target_pairs={{0,32},{32,0},{1,33},{33,1},{2,34},{34,2},{3,35},{35,3},{4,36},{36... | collective-permute-start | bytes 1474568 | tf_op jit(solution)/shard_map/ppermute | solution.py:311
  64.0 0.0 all-to-all-done.1.x_ref
  64.0 0.1 shard_map.75.refs_0_
  64.1 2.5 %collective-permute-start = (f32[8,128]{1,0:T(8,128)S(1)}, f32[8,128]{1,0:T(8,128)S(1)}, u32[]{:S(2)}, u32[]{:S(2)}) collective-permute-start(f32[8,128]{1,0:T(8,128)S(1)} %shard_map.75.refs_0_), channel_id=1, source_target_pairs={{0,32},{32,0},{1,33},{33,1},{2,34},{34,2},{3,35},{35,3},{4,36},{36... | collective-permute-start | bytes 12296 | tf_op jit(solution)/shard_map/ppermute | solution.py:318
  66.6 0.0 copy-done.4
  66.6 0.0 copy-done.5
  66.7 1.5 shard_map.74.w_ref
  68.2 0.0 copy-start
  68.2 0.0 collective-permute-done.4.refs_5_
  68.2 0.0 collective-permute-done.1.refs_3_
  68.2 0.0 collective-permute-done.refs_1_
  68.2 0.0 copy-done.3
  68.3 4.9 %shard_map.76 = bf16[16,32,128]{2,1,0:T(8,128)(2,1)S(1)} custom-call(s32[3]{0:T(128)S(1)} %pad_add_fusion.place_ref, s32[16]{0:T(128)S(1)} %copy-done.3, f32[1,640]{1,0:T(1,128)S(1)} %broadcast_in_dim.13.scale_ref, f32[1,640]{1,0:T(1,128)S(1)} %broadcast_in_dim.14.shift_ref, bf16[384,640]{1,0:T(8,128)(2,1)S(1)} %shard_map.74.w_ref, ...), custom_call_target="tpu_custom_call" | custom-call | flops 2000000000 | bytes 4000000 | tf_op jit(solution)/shard_map/pallas_call | solution.py:330
  73.2 10.2 %all_to_all.30.x_ref = bf16[16,32,128]{2,1,0:T(8,128)(2,1)S(1)} all-to-all(bf16[16,32,128]{2,1,0:T(8,128)(2,1)S(1)} %shard_map.76), channel_id=1, replica_groups=mesh['x'=4,'z_lo'=2,'core'=2,'z_hi'=4,'y'=8] {'x','z_lo','core'}, dimensions={0} | all-to-all | bytes 262144 | tf_op jit(solution)/shard_map/all_to_all | solution.py:295
  83.4 0.7 shard_map.77
  84.2 25.4 %all_to_all.31.totals_ref = f32[32,8,128]{2,1,0:T(8,128)S(1)} all-to-all(f32[32,8,128]{2,1,0:T(8,128)S(1)} %get-tuple-element.7), channel_id=1, replica_groups=mesh['x'=4,'z_lo'=2,'core'=2,'z_hi'=4,'y'=8] {'z_hi','y'}, dimensions={0} | all-to-all | bytes 262144 | tf_op jit(solution)/shard_map/all_to_all | solution.py:295
  109.5 0.0 copy-done
  109.5 1.1 shard_map.78
  110.7 26.5 %all_to_all.32.x_ref = bf16[32,112,128]{2,1,0:T(8,128)(2,1)S(1)} all-to-all(bf16[32,112,128]{2,1,0:T(8,128)(2,1)S(1)} %shard_map.78), channel_id=1, replica_groups=mesh['x'=4,'z_lo'=2,'core'=2,'z_hi'=4,'y'=8] {'z_hi','y'}, dimensions={0} | all-to-all | bytes 1835008 | tf_op jit(solution)/shard_map/all_to_all | solution.py:295
  137.2 0.0 copy-start.1
  137.2 4.5 %shard_map.79 = bf16[32,16,128]{2,1,0:T(8,128)(2,1)S(1)} custom-call(bf16[32,112,128]{2,1,0:T(8,128)(2,1)S(1)} %all_to_all.32.x_ref), custom_call_target="tpu_custom_call" | custom-call | flops 2000000000 | bytes 2000000 | tf_op jit(solution)/shard_map/pallas_call | solution.py:360
  141.7 20.5 %all_to_all.33.x_ref = bf16[32,16,128]{2,1,0:T(8,128)(2,1)S(1)} all-to-all(bf16[32,16,128]{2,1,0:T(8,128)(2,1)S(1)} %shard_map.79), channel_id=1, replica_groups=mesh['x'=4,'z_lo'=2,'core'=2,'z_hi'=4,'y'=8] {'z_hi','y'}, dimensions={0} | all-to-all | bytes 262144 | tf_op jit(solution)/shard_map/all_to_all | solution.py:295
  162.2 0.0 copy-done.1
  162.2 1.0 shard_map.80
  (3 shorter events, 0.1 us)
Async XLA Ops:
  0.0 20.0 %copy-start.2 = (bf16[180,640]{1,0:T(8,128)(2,1)S(1)}, bf16[180,640]{1,0:T(8,128)(2,1)}, u32[]{:S(2)}) copy-start(bf16[180,640]{1,0:T(8,128)(2,1)} %w_ref.3) | copy-start | bytes 691204
  2.0 18.1 %all-to-all-start = ((bf16[8,96,640]{2,1,0:T(8,128)(2,1)}), bf16[8,96,640]{2,1,0:T(8,128)(2,1)S(1)}, u32[]{:S(2)}, u32[]{:S(2)}) async-start(bf16[8,96,640]{2,1,0:T(8,128)(2,1)} %broadcast_in_dim.16), calls=%async_computation | async-start | bytes 1966080 | tf_op jit(solution)/shard_map/all_to_all | solution.py:295
  8.7 57.9 %copy-start.4 = (f32[640]{0:T(1024)S(1)}, f32[640]{0:T(1024)}, u32[]{:S(2)}) copy-start(f32[640]{0:T(1024)} %param.8) | copy-start | bytes 7684
  8.7 57.9 %copy-start.5 = (f32[640]{0:T(1024)S(1)}, f32[640]{0:T(1024)}, u32[]{:S(2)}) copy-start(f32[640]{0:T(1024)} %param.9) | copy-start | bytes 7684
  22.4 45.9 %copy-start.3 = (s32[16]{0:T(128)S(1)}, s32[16]{0:T(128)}, u32[]{:S(2)}) copy-start(s32[16]{0:T(128)} %anc_ref.1) | copy-start | bytes 196
  22.4 41.6 %all-to-all-start.1 = ((bf16[32,80,128]{2,1,0:T(8,128)(2,1)}), bf16[32,80,128]{2,1,0:T(8,128)(2,1)S(1)}, u32[]{:S(2)}, u32[]{:S(2)}) async-start(bf16[32,80,128]{2,1,0:T(8,128)(2,1)} %shard_map.73), calls=%async_computation.1 | async-start | bytes 1310720 | tf_op jit(solution)/shard_map/all_to_all | solution.py:295
  39.7 28.5 %collective-permute-start.1 = (bf16[8,96,640]{2,1,0:T(8,128)(2,1)S(1)}, bf16[8,96,640]{2,1,0:T(8,128)(2,1)S(1)}, u32[]{:S(2)}, u32[]{:S(2)}) collective-permute-start(bf16[8,96,640]{2,1,0:T(8,128)(2,1)S(1)} %all-to-all-done.x_ref.refs_2_), channel_id=1, source_target_pairs={{0,32},{32,0},{1,33},{33,1},{2,34},{34,2},{3,35},{35,3},{4,36},{36... | collective-permute-start | bytes 2949128 | tf_op jit(solution)/shard_map/ppermute | solution.py:310
  44.1 12.7 %collective-permute-start.2 = (bf16[8,24,640]{2,1,0:T(8,128)(2,1)S(1)}, bf16[8,24,640]{2,1,0:T(8,128)(2,1)S(1)}, u32[]{:S(2)}, u32[]{:S(2)}) collective-permute-start(bf16[8,24,640]{2,1,0:T(8,128)(2,1)S(1)} %get-tuple-element.9), channel_id=1, source_target_pairs={{0,1},{1,2},{2,3},{3,4},{4,5},{5,6},{6,7},{7,8},{8,9},{9,10},{10,1... | collective-permute-start | bytes 737288 | tf_op jit(solution)/shard_map/ppermute | solution.py:307
  47.5 12.4 %collective-permute-start.3 = (bf16[8,24,640]{2,1,0:T(8,128)(2,1)S(1)}, bf16[8,24,640]{2,1,0:T(8,128)(2,1)S(1)}, u32[]{:S(2)}, u32[]{:S(2)}) collective-permute-start(bf16[8,24,640]{2,1,0:T(8,128)(2,1)S(1)} %get-tuple-element.10), channel_id=1, source_target_pairs={{1,0},{2,1},{3,2},{4,3},{5,4},{6,5},{7,6},{8,7},{9,8},{10,9},{11,1... | collective-permute-start | bytes 737288 | tf_op jit(solution)/shard_map/ppermute | solution.py:308
  60.0 8.2 %collective-permute-start.4 = (bf16[2,8,24,640]{3,2,1,0:T(8,128)(2,1)S(1)}, bf16[2,8,24,640]{3,2,1,0:T(8,128)(2,1)}, u32[]{:S(2)}, u32[]{:S(2)}) collective-permute-start(bf16[2,8,24,640]{3,2,1,0:T(8,128)(2,1)S(1)} %pad_maximum_fusion.refs_4_), channel_id=1, source_target_pairs={{0,32},{32,0},{1,33},{33,1},{2,34},{34,2},{3,35},{35,3},{4,36},{36... | collective-permute-start | bytes 1474568 | tf_op jit(solution)/shard_map/ppermute | solution.py:311
  64.1 4.1 %collective-permute-start = (f32[8,128]{1,0:T(8,128)S(1)}, f32[8,128]{1,0:T(8,128)S(1)}, u32[]{:S(2)}, u32[]{:S(2)}) collective-permute-start(f32[8,128]{1,0:T(8,128)S(1)} %shard_map.75.refs_0_), channel_id=1, source_target_pairs={{0,32},{32,0},{1,33},{33,1},{2,34},{34,2},{3,35},{35,3},{4,36},{36... | collective-permute-start | bytes 12296 | tf_op jit(solution)/shard_map/ppermute | solution.py:318
  68.2 41.3 %copy-start = (bf16[640,1920]{1,0:T(8,128)(2,1)S(1)}, bf16[640,1920]{1,0:T(8,128)(2,1)}, u32[]{:S(2)}) copy-start(bf16[640,1920]{1,0:T(8,128)(2,1)} %w_ref.4) | copy-start | bytes 7372804
  137.2 25.0 %copy-start.1 = (bf16[640,640]{1,0:T(8,128)(2,1)S(1)}, bf16[640,640]{1,0:T(8,128)(2,1)}, u32[]{:S(2)}) copy-start(bf16[640,640]{1,0:T(8,128)(2,1)} %w_ref.5) | copy-start | bytes 2457604

commit v7 on v6

--- a/solution.py
+++ b/solution.py
@@ -90,6 +90,10 @@
         parts.append(top)
         value = value - top
     return parts
+
+
+def spread_kernel(x_ref, out_ref):
+    out_ref[...] = jnp.broadcast_to(x_ref[...][None], out_ref.shape)
 
 
 def pick_kernel(place_ref, x_ref, w_ref, out_ref):
@@ -168,38 +172,76 @@
     return out
 
 
-def conv_kernel(place_ref, anc_ref, scale_ref, shift_ref, w_ref, *refs):
-    totals, slabs, edges, (out_ref, done_ref) = refs[:2], refs[2:4], refs[4:6], refs[6:]
+def unpacked(value):
+    return jnp.concatenate(
+        [value] + [pltpu.roll(value, LANES - SLICE * t, 1) for t in (1, 2)], axis=0
+    )
+
+
+def edge_kernel(scale_ref, shift_ref, w_ref, *refs):
+    totals, slabs, (up_ref, down_ref, gain_ref, bias_ref) = refs[:2], refs[2:4], refs[4:]
     mean, inverse = mean_and_inverse(jnp.concatenate([ref[...] for ref in totals], axis=0))
     gain = inverse * (1.0 + scale_ref[...])
     bias = shift_ref[...] - mean * gain
+    gain_ref[...] = gain
+    bias_ref[...] = bias
+    for rows, tap, ref in ((slice(0, WIDTH), 2, up_ref), (slice(LAST, TOKENS), 0, down_ref)):
+        active = []
+        for n in range(PARTICLES):
+            x = slabs[n // HALF][n % HALF].astype(F32)[rows]
+            active.append(silu(x * gain[n : n + 1] + bias[n : n + 1]))
+        active = jnp.concatenate(active, axis=0).astype(BF16)
+        weights = w_ref[tap * LANES : (tap + 1) * LANES, :]
+        full = across(lax.dot_general(active, weights, NT, preferred_element_type=F32))
+        for n in range(PARTICLES):
+            ref[n] = packed(full[n * WIDTH : (n + 1) * WIDTH])
+
+
+def conv_kernel(place_ref, gain_ref, bias_ref, w_ref, *refs):
+    slabs, part_ref = refs[:2], refs[2]
     row, col = iota((LANES, CHANS), 0), iota((LANES, CHANS), 1)
     chosen = ((col == row + place_ref[0] * SLICE) & (row < SLICE)).astype(F32).astype(BF16)
     weights = w_ref[...]
-    top, bottom = place_ref[2] == 0, place_ref[2] == ROW_DEVS - 1
     each = 2
     for step in range(PARTICLES // each):
         active, raw = [], []
         for n in range(step * each, (step + 1) * each):
-            which, j = n // HALF, n % HALF
-            x = slabs[which][j]
+            x = slabs[n // HALF][n % HALF]
             raw.append(x)
-            act = lambda v: silu(v.astype(F32) * gain[n : n + 1] + bias[n : n + 1])
-            above, below = act(edges[which][0, j]), act(edges[which][1, j])
-            active += [jnp.where(top, 0.0, above), act(x), jnp.where(bottom, 0.0, below)]
-        active = jnp.concatenate(active, axis=0).astype(BF16)
+            v = x.astype(F32) * gain_ref[n : n + 1] + bias_ref[n : n + 1]
+            active.append(silu(v).astype(BF16))
+        active = jnp.concatenate(active, axis=0)
         raw = jnp.concatenate(raw, axis=0)
         taps = lax.dot_general(active, weights, NT, preferred_element_type=F32)
         field = lax.dot_general(raw, chosen, NT, preferred_element_type=F32)
         for k in range(each):
-            at = k * (TOKENS + 2 * WIDTH)
-            full = field[k * TOKENS : (k + 1) * TOKENS]
-            for a in range(3):
-                rows = slice(at + a * WIDTH, at + a * WIDTH + TOKENS)
-                full = full + taps[rows, a * LANES : (a + 1) * LANES]
-            done_ref[step * each + k] = packed(across(full)).astype(BF16)
+            rows = slice(k * TOKENS, (k + 1) * TOKENS)
+            t0, t1, t2 = (taps[rows, n * LANES : (n + 1) * LANES] for n in range(3))
+            base = t1 + field[rows]
+            full = jnp.concatenate(
+                [
+                    base[:WIDTH] + t2[WIDTH : 2 * WIDTH],
+                    base[WIDTH:LAST] + t0[: LAST - WIDTH] + t2[2 * WIDTH :],
+                    base[LAST:] + t0[LAST - WIDTH : LAST],
+                ],
+                axis=0,
+            )
+            part_ref[step * each + k] = across(full)
+
+
+def finish_kernel(place_ref, anc_ref, part_ref, above_ref, below_ref, out_ref):
+    lane = iota((TOKENS, LANES), 1)
     for p in range(PARTICLES):
-        out_ref[p] = done_ref[spot(place_ref, anc_ref[p])]
+        q = spot(place_ref, anc_ref[p])
+        total = jnp.concatenate(
+            [
+                part_ref[q, :WIDTH] + unpacked(above_ref[q]),
+                part_ref[q, WIDTH:LAST],
+                part_ref[q, LAST:] + unpacked(below_ref[q]),
+            ],
+            axis=0,
+        )
+        out_ref[p] = packed(jnp.where(lane < SLICE, total, 0.0)).astype(BF16)
 
 
 def gather_kernel(x_ref, resid_ref, out_ref, wide_ref):
@@ -298,17 +340,12 @@
 def per_device(latent, ada_scale, ada_shift, conv_weight, qkv_weight, out_weight, ancestors):
     slab = latent.reshape(TOKENS, CHANS)
     particle = lax.axis_index(PART).astype(jnp.int32)
-    place = jnp.stack(
-        [particle] + [lax.axis_index(a).astype(jnp.int32) for a in ("core", ROWS)]
-    )
+    place = jnp.stack([particle, lax.axis_index("core").astype(jnp.int32)])
 
     swap = [(0, 1), (1, 0)]
-    here = exchange(jnp.broadcast_to(slab[None], (HALF, TOKENS, CHANS)), CHIPS)
-    above = lax.ppermute(here[:, LAST:], ROWS, [(i, i + 1) for i in range(ROW_DEVS - 1)])
-    below = lax.ppermute(here[:, :WIDTH], ROWS, [(i + 1, i) for i in range(ROW_DEVS - 1)])
-    edges = jnp.stack([above, below])
+    copies = call(spread_kernel, shaped(HALF, TOKENS, CHANS), [VMEM], 10**5, 10**6)(slab)
+    here = exchange(copies, CHIPS)
     slabs = [here, lax.ppermute(here, "core", swap)]
-    edges = [edges, lax.ppermute(edges, "core", swap)]
 
     picked = call(pick_kernel, shaped(ROW_DEVS, 80, LANES), [SMEM, VMEM, VMEM], 10**7, 10**6)(
         place, here, conv_weight
@@ -327,15 +364,25 @@
             pltpu.VMEM((3 * LANES, CHANS), F32),
         ),
     )(picked)
-    pieces = call(
+
+    edge = shaped(PARTICLES, WIDTH // 3, LANES, dtype=F32)
+    each = shaped(PARTICLES, CHANS, dtype=F32)
+    up, down, gain, bias = call(edge_kernel, [edge, edge, each, each], [VMEM] * 7, 10**8, 10**6)(
+        ada_scale[None], ada_shift[None], weights, *totals, *slabs
+    )
+    above = lax.ppermute(down, ROWS, [(i, i + 1) for i in range(ROW_DEVS - 1)])
+    below = lax.ppermute(up, ROWS, [(i + 1, i) for i in range(ROW_DEVS - 1)])
+    part = call(
         conv_kernel,
-        shaped(PARTICLES, 32, LANES),
-        [SMEM, SMEM] + [VMEM] * 9,
+        shaped(PARTICLES, TOKENS, LANES, dtype=F32),
+        [SMEM] + [VMEM] * 5,
         2 * 10**9,
         4 * 10**6,
         vmem=32,
-        scratch=(pltpu.VMEM((PARTICLES, 32, LANES), BF16),),
-    )(place, ancestors, ada_scale[None], ada_shift[None], weights, *totals, *slabs, *edges)
+    )(place, gain, bias, weights, *slabs)
+    pieces = call(
+        finish_kernel, shaped(PARTICLES, 32, LANES), [SMEM, SMEM] + [VMEM] * 3, 10**6, 10**6
+    )(place, ancestors, part, above, below)
     pieces = exchange(pieces, PART)
 
     resid, sums = call(

time: 166 us -> 166 us (level)
  blocking collectives: 82.6 us -> 77.3 us
  waiting for transfers between devices: 22.4 us -> 25.1 us
  starting transfers between devices: 39.5 us -> 41.3 us
  Pallas kernels: 16.3 us -> 18 us
    all_to_all x2, waiting for transfers between devices: 11.3 us -> 24.5 us  [exchange(): return lax.all_to_all(values, axes, split_axis=0, concat_axis=0, tiled=True)]
    ppermute x3 -> x2, waiting for transfers between devices: 11.1 us -> 0.64 us  [the longest x1 0.63 us: per_device(): below = lax.ppermute(up, ROWS, [(i + 1, i) for i in range(ROW_DEVS - 1)])]
    all_to_all x4, blocking collectives: 82.6 us -> 77.3 us  [exchange(): return lax.all_to_all(values, axes, split_axis=0, concat_axis=0, tiled=True)]
    ppermute x1, starting transfers between devices: 2.52 us -> 6.56 us  [per_device(): totals = [totals, lax.ppermute(totals, 'core', swap)]]
    ppermute x3 -> x2, starting transfers between devices: 8.71 us -> 6.42 us  [the longest x1 5.13 us: per_device(): above = lax.ppermute(down, ROWS, [(i, i + 1) for i in range(ROW_DEVS - 1)])]
    broadcast_in_dim x1 -> x0, local copies, waits for them, and re-layouts: 1.97 us -> none  [per_device(): here = exchange(jnp.broadcast_to(slab[None], (HALF, TOKENS, CHANS)), CHIPS)]
    pallas_call x1 -> x4, Pallas kernels: 4.92 us -> 6.63 us  [the longest x1 3.03 us: per_device(): call(conv_kernel, shaped(PARTICLES, TOKENS, LANES, dtype=F32), [SMEM] + [...]
  transfers between devices with their start and end apart: 7 -> 6, of which waited for: 3 -> 3; matrix products, arithmetic and copies ran while one was open for 0% -> 0% of each run, Pallas kernels for 1% -> 3%
where the time goes in v7:
time: 166 us; the launch traced here: 163 us
  blocking collectives  77.3 us (47%)
  starting transfers between devices  41.3 us (25%)
  waiting for transfers between devices  25.1 us (15%)
  Pallas kernels  18 us (11%)
    all_to_all x4, blocking collectives, exchange(): return lax.all_to_all(values, axes, split_axis=0, concat_axis=0, tiled=True)  77.3 us
    all_to_all x2, waiting for transfers between devices, exchange(): return lax.all_to_all(values, axes, split_axis=0, concat_axis=0, tiled=True)  24.5 us
    all_to_all x2, starting transfers between devices, exchange(): return lax.all_to_all(values, axes, split_axis=0, concat_axis=0, tiled=True)  24 us
    ppermute x1, starting transfers between devices, per_device(): totals = [totals, lax.ppermute(totals, 'core', swap)]  6.56 us
    ppermute x1, starting transfers between devices, per_device(): above = lax.ppermute(down, ROWS, [(i, i + 1) for i in range(ROW_DEVS - 1)])  5.13 us
    pallas_call x1, Pallas kernels, per_device(): call(attend_kernel, shaped(ROW_DEVS, 16, LANES), [VMEM], 2 * 10 ** 9, 2 *...  4.54 us
    ppermute x1, starting transfers between devices, per_device(): slabs = [here, lax.ppermute(here, 'core', swap)]  4.35 us
  transfers between devices with their start and end apart: 6, of which 3 were waited for; matrix products, arithmetic and copies ran while one was open for 0% of the time, Pallas kernels for 3%

profile of v7, /device:TPU:1, one launch (start us, length us, event | category | flops | bytes accessed | tf_op | source)
XLA Modules:
  0.0 162.9 jit_solution(8101961672834695389)
XLA Ops:
  0.0 0.0 copy-start.2
  0.0 0.0 copy-start.3
  0.0 0.9 copy-done.3
  0.9 1.0 shard_map.73
  2.0 0.0 copy-start.5
  2.0 0.0 copy-start.6
  2.0 6.8 %all-to-all-start = ((bf16[8,96,640]{2,1,0:T(8,128)(2,1)}), bf16[8,96,640]{2,1,0:T(8,128)(2,1)S(1)}, u32[]{:S(2)}, u32[]{:S(2)}) async-start(bf16[8,96,640]{2,1,0:T(8,128)(2,1)} %shard_map.73), calls=%async_computation | async-start | bytes 1966080 | tf_op jit(solution)/shard_map/all_to_all | solution.py:337
  8.8 0.1 pad_add_fusion.place_ref
  8.8 11.3 %all-to-all-done.x_ref.refs_2_.refs_0_ = bf16[8,96,640]{2,1,0:T(8,128)(2,1)S(1)} async-done(((bf16[8,96,640]{2,1,0:T(8,128)(2,1)}), bf16[8,96,640]{2,1,0:T(8,128)(2,1)S(1)}, u32[]{:S(2)}, u32[]{:S(2)}) %all-to-all-start) | async-done | bytes 983072 | tf_op jit(solution)/shard_map/all_to_all | solution.py:337
  20.2 0.0 copy-done.2
  20.2 2.3 %shard_map.74 = bf16[32,80,128]{2,1,0:T(8,128)(2,1)} custom-call(s32[2]{0:T(128)S(1)} %pad_add_fusion.place_ref, bf16[8,96,640]{2,1,0:T(8,128)(2,1)S(1)} %all-to-all-done.x_ref.refs_2_.refs_0_, bf16[180,640]{1,0:T(8,128)(2,1)S(1)} %copy-done.2), custom_call_target="tpu_custom_call" | custom-call | flops 10000000 | bytes 1000000 | tf_op jit(solution)/shard_map/pallas_call | solution.py:350
  22.5 17.2 %all-to-all-start.1 = ((bf16[32,80,128]{2,1,0:T(8,128)(2,1)}), bf16[32,80,128]{2,1,0:T(8,128)(2,1)S(1)}, u32[]{:S(2)}, u32[]{:S(2)}) async-start(bf16[32,80,128]{2,1,0:T(8,128)(2,1)} %shard_map.74), calls=%async_computation.1 | async-start | bytes 1310720 | tf_op jit(solution)/shard_map/all_to_all | solution.py:337
  39.7 4.3 %collective-permute-start.1 = (bf16[8,96,640]{2,1,0:T(8,128)(2,1)S(1)}, bf16[8,96,640]{2,1,0:T(8,128)(2,1)S(1)}, u32[]{:S(2)}, u32[]{:S(2)}) collective-permute-start(bf16[8,96,640]{2,1,0:T(8,128)(2,1)S(1)} %all-to-all-done.x_ref.refs_2_.refs_0_), channel_id=1, source_target_pairs={{0,32},{32,0},{1,33},{33,1},{2,34},{34,2},{3,35},{35,3},{4,36},{36... | collective-permute-start | bytes 2949128 | tf_op jit(solution)/shard_map/ppermute | solution.py:348
  44.0 13.2 %all-to-all-done.1.x_ref = bf16[32,80,128]{2,1,0:T(8,128)(2,1)S(1)} async-done(((bf16[32,80,128]{2,1,0:T(8,128)(2,1)}), bf16[32,80,128]{2,1,0:T(8,128)(2,1)S(1)}, u32[]{:S(2)}, u32[]{:S(2)}) %all-to-all-start.1) | async-done | bytes 655392 | tf_op jit(solution)/shard_map/all_to_all | solution.py:337
  57.2 0.1 shard_map.76.refs_0_
  57.3 6.6 %collective-permute-start = (f32[8,128]{1,0:T(8,128)S(1)}, f32[8,128]{1,0:T(8,128)S(1)}, u32[]{:S(2)}, u32[]{:S(2)}) collective-permute-start(f32[8,128]{1,0:T(8,128)S(1)} %shard_map.76.refs_0_), channel_id=1, source_target_pairs={{0,32},{32,0},{1,33},{33,1},{2,34},{34,2},{3,35},{35,3},{4,36},{36... | collective-permute-start | bytes 12296 | tf_op jit(solution)/shard_map/ppermute | solution.py:355
  63.9 0.0 copy-done.5
  63.9 0.0 copy-done.6
  63.9 1.5 shard_map.75.w_ref
  65.5 0.0 collective-permute-done.1.refs_3_.refs_1_
  65.5 0.0 collective-permute-done.refs_1_
  65.5 1.5 shard_map.77
  67.0 5.1 %collective-permute-start.2 = (f32[16,8,128]{2,1,0:T(8,128)S(1)}, f32[16,8,128]{2,1,0:T(8,128)S(1)}, u32[]{:S(2)}, u32[]{:S(2)}) collective-permute-start(f32[16,8,128]{2,1,0:T(8,128)S(1)} %get-tuple-element.13), channel_id=1, source_target_pairs={{0,1},{1,2},{2,3},{3,4},{4,5},{5,6},{6,7},{7,8},{8,9},{9,10},{10,1... | collective-permute-start | bytes 196616 | tf_op jit(solution)/shard_map/ppermute | solution.py:373
  72.1 1.3 collective-permute-start.3
  73.4 0.0 copy-start.4
  73.4 0.0 copy-start
  73.4 3.0 %shard_map.78.part_ref = f32[16,96,128]{2,1,0:T(8,128)S(1)} custom-call(s32[2]{0:T(128)S(1)} %pad_add_fusion.place_ref, f32[16,640]{1,0:T(8,128)S(1)} %get-tuple-element.11.gain_ref, f32[16,640]{1,0:T(8,128)S(1)} %get-tuple-element.12.bias_ref, bf16[384,640]{1,0:T(8,128)(2,1)S(1)} %shard_map.75.w_ref, ...), custom_call_target="tpu_custom_call" | custom-call | flops 2000000000 | bytes 4000000 | tf_op jit(solution)/shard_map/pallas_call | solution.py:375
  76.5 0.0 collective-permute-done.2.above_ref
  76.5 0.6 collective-permute-done.3.below_ref
  77.1 0.0 copy-done.4
  77.1 1.1 shard_map.79
  78.2 11.7 %all_to_all.30.x_ref = bf16[16,32,128]{2,1,0:T(8,128)(2,1)S(1)} all-to-all(bf16[16,32,128]{2,1,0:T(8,128)(2,1)S(1)} %shard_map.79), channel_id=1, replica_groups=mesh['x'=4,'z_lo'=2,'core'=2,'z_hi'=4,'y'=8] {'x','z_lo','core'}, dimensions={0} | all-to-all | bytes 262144 | tf_op jit(solution)/shard_map/all_to_all | solution.py:337
  89.9 0.7 shard_map.80
  90.6 18.7 %all_to_all.31.totals_ref = f32[32,8,128]{2,1,0:T(8,128)S(1)} all-to-all(f32[32,8,128]{2,1,0:T(8,128)S(1)} %get-tuple-element.15), channel_id=1, replica_groups=mesh['x'=4,'z_lo'=2,'core'=2,'z_hi'=4,'y'=8] {'z_hi','y'}, dimensions={0} | all-to-all | bytes 262144 | tf_op jit(solution)/shard_map/all_to_all | solution.py:337
  109.3 0.0 copy-done
  109.3 1.1 shard_map.81
  110.5 26.4 %all_to_all.32.x_ref = bf16[32,112,128]{2,1,0:T(8,128)(2,1)S(1)} all-to-all(bf16[32,112,128]{2,1,0:T(8,128)(2,1)S(1)} %shard_map.81), channel_id=1, replica_groups=mesh['x'=4,'z_lo'=2,'core'=2,'z_hi'=4,'y'=8] {'z_hi','y'}, dimensions={0} | all-to-all | bytes 1835008 | tf_op jit(solution)/shard_map/all_to_all | solution.py:337
  136.9 0.0 copy-start.1
  136.9 4.5 %shard_map.82 = bf16[32,16,128]{2,1,0:T(8,128)(2,1)S(1)} custom-call(bf16[32,112,128]{2,1,0:T(8,128)(2,1)S(1)} %all_to_all.32.x_ref), custom_call_target="tpu_custom_call" | custom-call | flops 2000000000 | bytes 2000000 | tf_op jit(solution)/shard_map/pallas_call | solution.py:407
  141.4 20.5 %all_to_all.33.x_ref = bf16[32,16,128]{2,1,0:T(8,128)(2,1)S(1)} all-to-all(bf16[32,16,128]{2,1,0:T(8,128)(2,1)S(1)} %shard_map.82), channel_id=1, replica_groups=mesh['x'=4,'z_lo'=2,'core'=2,'z_hi'=4,'y'=8] {'z_hi','y'}, dimensions={0} | all-to-all | bytes 262144 | tf_op jit(solution)/shard_map/all_to_all | solution.py:337
  161.9 0.0 copy-done.1
  161.9 1.0 shard_map.83
  (2 shorter events, 0.0 us)
Async XLA Ops:
  0.0 20.2 %copy-start.2 = (bf16[180,640]{1,0:T(8,128)(2,1)S(1)}, bf16[180,640]{1,0:T(8,128)(2,1)}, u32[]{:S(2)}) copy-start(bf16[180,640]{1,0:T(8,128)(2,1)} %w_ref.3) | copy-start | bytes 691204
  0.0 0.9 copy-start.3
  2.0 61.9 %copy-start.5 = (f32[640]{0:T(1024)S(1)}, f32[640]{0:T(1024)}, u32[]{:S(2)}) copy-start(f32[640]{0:T(1024)} %param.8) | copy-start | bytes 7684
  2.0 61.9 %copy-start.6 = (f32[640]{0:T(1024)S(1)}, f32[640]{0:T(1024)}, u32[]{:S(2)}) copy-start(f32[640]{0:T(1024)} %param.9) | copy-start | bytes 7684
  2.0 18.2 %all-to-all-start = ((bf16[8,96,640]{2,1,0:T(8,128)(2,1)}), bf16[8,96,640]{2,1,0:T(8,128)(2,1)S(1)}, u32[]{:S(2)}, u32[]{:S(2)}) async-start(bf16[8,96,640]{2,1,0:T(8,128)(2,1)} %shard_map.73), calls=%async_computation | async-start | bytes 1966080 | tf_op jit(solution)/shard_map/all_to_all | solution.py:337
  22.5 34.7 %all-to-all-start.1 = ((bf16[32,80,128]{2,1,0:T(8,128)(2,1)}), bf16[32,80,128]{2,1,0:T(8,128)(2,1)S(1)}, u32[]{:S(2)}, u32[]{:S(2)}) async-start(bf16[32,80,128]{2,1,0:T(8,128)(2,1)} %shard_map.74), calls=%async_computation.1 | async-start | bytes 1310720 | tf_op jit(solution)/shard_map/all_to_all | solution.py:337
  39.7 25.8 %collective-permute-start.1 = (bf16[8,96,640]{2,1,0:T(8,128)(2,1)S(1)}, bf16[8,96,640]{2,1,0:T(8,128)(2,1)S(1)}, u32[]{:S(2)}, u32[]{:S(2)}) collective-permute-start(bf16[8,96,640]{2,1,0:T(8,128)(2,1)S(1)} %all-to-all-done.x_ref.refs_2_.refs_0_), channel_id=1, source_target_pairs={{0,32},{32,0},{1,33},{33,1},{2,34},{34,2},{3,35},{35,3},{4,36},{36... | collective-permute-start | bytes 2949128 | tf_op jit(solution)/shard_map/ppermute | solution.py:348
  57.3 8.2 %collective-permute-start = (f32[8,128]{1,0:T(8,128)S(1)}, f32[8,128]{1,0:T(8,128)S(1)}, u32[]{:S(2)}, u32[]{:S(2)}) collective-permute-start(f32[8,128]{1,0:T(8,128)S(1)} %shard_map.76.refs_0_), channel_id=1, source_target_pairs={{0,32},{32,0},{1,33},{33,1},{2,34},{34,2},{3,35},{35,3},{4,36},{36... | collective-permute-start | bytes 12296 | tf_op jit(solution)/shard_map/ppermute | solution.py:355
  67.0 9.5 %collective-permute-start.2 = (f32[16,8,128]{2,1,0:T(8,128)S(1)}, f32[16,8,128]{2,1,0:T(8,128)S(1)}, u32[]{:S(2)}, u32[]{:S(2)}) collective-permute-start(f32[16,8,128]{2,1,0:T(8,128)S(1)} %get-tuple-element.13), channel_id=1, source_target_pairs={{0,1},{1,2},{2,3},{3,4},{4,5},{5,6},{6,7},{7,8},{8,9},{9,10},{10,1... | collective-permute-start | bytes 196616 | tf_op jit(solution)/shard_map/ppermute | solution.py:373
  72.1 5.0 %collective-permute-start.3 = (f32[16,8,128]{2,1,0:T(8,128)S(1)}, f32[16,8,128]{2,1,0:T(8,128)S(1)}, u32[]{:S(2)}, u32[]{:S(2)}) collective-permute-start(f32[16,8,128]{2,1,0:T(8,128)S(1)} %get-tuple-element.14), channel_id=1, source_target_pairs={{1,0},{2,1},{3,2},{4,3},{5,4},{6,5},{7,6},{8,7},{9,8},{10,9},{11,1... | collective-permute-start | bytes 196616 | tf_op jit(solution)/shard_map/ppermute | solution.py:374
  73.4 3.7 %copy-start.4 = (s32[16]{0:T(128)S(1)}, s32[16]{0:T(128)}, u32[]{:S(2)}) copy-start(s32[16]{0:T(128)} %anc_ref.1) | copy-start | bytes 196
  73.4 35.9 %copy-start = (bf16[640,1920]{1,0:T(8,128)(2,1)S(1)}, bf16[640,1920]{1,0:T(8,128)(2,1)}, u32[]{:S(2)}) copy-start(bf16[640,1920]{1,0:T(8,128)(2,1)} %w_ref.4) | copy-start | bytes 7372804
  136.9 25.0 %copy-start.1 = (bf16[640,640]{1,0:T(8,128)(2,1)S(1)}, bf16[640,640]{1,0:T(8,128)(2,1)}, u32[]{:S(2)}) copy-start(bf16[640,640]{1,0:T(8,128)(2,1)} %w_ref.5) | copy-start | bytes 2457604

commit v8 on v6

--- a/solution.py
+++ b/solution.py
@@ -13,6 +13,7 @@
 ROWS_HERE = 4
 TOKENS = ROWS_HERE * WIDTH
 LAST = TOKENS - WIDTH
+ALL = TOKENS + 2 * WIDTH
 PARTICLES = 16
 HALF = PARTICLES // 2
 ROW_DEVS = 32
@@ -34,6 +35,7 @@
 BF16 = jnp.bfloat16
 SMEM = pl.BlockSpec(memory_space=pltpu.SMEM)
 VMEM = pl.BlockSpec(memory_space=pltpu.VMEM)
+ANY = pl.BlockSpec(memory_space=pl.ANY)
 
 
 def call(kernel, out_shape, in_specs, flops, size, vmem=16, scratch=()):
@@ -92,7 +94,19 @@
     return parts
 
 
-def pick_kernel(place_ref, x_ref, w_ref, out_ref):
+def spread_kernel(x_ref, out_ref, first_ref, last_ref):
+    out_ref[...] = jnp.broadcast_to(x_ref[...][None], out_ref.shape)
+    wide = x_ref[...].astype(F32)
+    first_ref[...] = wide[:WIDTH].astype(BF16)
+    last_ref[...] = wide[LAST:].astype(BF16)
+
+
+def join_kernel(mine_ref, opposite_ref, _, out_ref):
+    out_ref[0] = mine_ref[...]
+    out_ref[1] = opposite_ref[...]
+
+
+def pick_kernel(place_ref, x_ref, w_ref, _, out_ref):
     row, col = iota((48, CHANS), 0), iota((48, CHANS), 1)
     chosen = ((col == row + place_ref[0] * SLICE) & (row < SLICE)).astype(F32).astype(BF16)
     picked = lax.dot_general(chosen, w_ref[...], NT, preferred_element_type=F32)
@@ -168,35 +182,50 @@
     return out
 
 
+STEPS = (0, 1, 3, 2)
+
+
+def beside(place_ref, j):
+    dx = lax.rem(j // 2 + 4 - place_ref[2], 4)
+    dz = lax.rem(j % 2 + place_ref[3], 2)
+    return 2 * jnp.where(dx == 2, 3, jnp.where(dx == 3, 2, dx)) + dz
+
+
+def merge_kernel(place_ref, x_ref, edge_ref, out_ref):
+    for j in range(HALF):
+        at = beside(place_ref, j)
+        parts = [x_ref[j], edge_ref[at, 0], edge_ref[at, 1]]
+        out_ref[j] = jnp.concatenate([v.astype(F32) for v in parts], axis=0).astype(BF16)
+
+
 def conv_kernel(place_ref, anc_ref, scale_ref, shift_ref, w_ref, *refs):
-    totals, slabs, edges, (out_ref, done_ref) = refs[:2], refs[2:4], refs[4:6], refs[6:]
+    totals, slabs, (out_ref, done_ref) = refs[:2], refs[2:4], refs[4:]
     mean, inverse = mean_and_inverse(jnp.concatenate([ref[...] for ref in totals], axis=0))
     gain = inverse * (1.0 + scale_ref[...])
     bias = shift_ref[...] - mean * gain
     row, col = iota((LANES, CHANS), 0), iota((LANES, CHANS), 1)
     chosen = ((col == row + place_ref[0] * SLICE) & (row < SLICE)).astype(F32).astype(BF16)
     weights = w_ref[...]
-    top, bottom = place_ref[2] == 0, place_ref[2] == ROW_DEVS - 1
+    top, bottom = place_ref[4] == 0, place_ref[4] == ROW_DEVS - 1
     each = 2
     for step in range(PARTICLES // each):
         active, raw = [], []
         for n in range(step * each, (step + 1) * each):
-            which, j = n // HALF, n % HALF
-            x = slabs[which][j]
-            raw.append(x)
-            act = lambda v: silu(v.astype(F32) * gain[n : n + 1] + bias[n : n + 1])
-            above, below = act(edges[which][0, j]), act(edges[which][1, j])
-            active += [jnp.where(top, 0.0, above), act(x), jnp.where(bottom, 0.0, below)]
-        active = jnp.concatenate(active, axis=0).astype(BF16)
+            x = slabs[n // HALF][n % HALF]
+            raw.append(x[:TOKENS])
+            active.append(silu(x.astype(F32) * gain[n : n + 1] + bias[n : n + 1]).astype(BF16))
+        active = jnp.concatenate(active, axis=0)
         raw = jnp.concatenate(raw, axis=0)
         taps = lax.dot_general(active, weights, NT, preferred_element_type=F32)
         field = lax.dot_general(raw, chosen, NT, preferred_element_type=F32)
         for k in range(each):
-            at = k * (TOKENS + 2 * WIDTH)
-            full = field[k * TOKENS : (k + 1) * TOKENS]
-            for a in range(3):
-                rows = slice(at + a * WIDTH, at + a * WIDTH + TOKENS)
-                full = full + taps[rows, a * LANES : (a + 1) * LANES]
+            here = taps[k * ALL : (k + 1) * ALL]
+            t0, t1, t2 = (here[:, a * LANES : (a + 1) * LANES] for a in range(3))
+            above = jnp.where(top, 0.0, t0[TOKENS : TOKENS + WIDTH])
+            below = jnp.where(bottom, 0.0, t2[TOKENS + WIDTH :])
+            full = field[k * TOKENS : (k + 1) * TOKENS] + t1[:TOKENS]
+            full = full + jnp.concatenate([above, t0[:LAST]], axis=0)
+            full = full + jnp.concatenate([t2[WIDTH:TOKENS], below], axis=0)
             done_ref[step * each + k] = packed(across(full)).astype(BF16)
     for p in range(PARTICLES):
         out_ref[p] = done_ref[spot(place_ref, anc_ref[p])]
@@ -299,20 +328,32 @@
     slab = latent.reshape(TOKENS, CHANS)
     particle = lax.axis_index(PART).astype(jnp.int32)
     place = jnp.stack(
-        [particle] + [lax.axis_index(a).astype(jnp.int32) for a in ("core", ROWS)]
+        [particle] + [lax.axis_index(a).astype(jnp.int32) for a in ("core", "x", "z_lo", ROWS)]
     )
 
     swap = [(0, 1), (1, 0)]
-    here = exchange(jnp.broadcast_to(slab[None], (HALF, TOKENS, CHANS)), CHIPS)
-    above = lax.ppermute(here[:, LAST:], ROWS, [(i, i + 1) for i in range(ROW_DEVS - 1)])
-    below = lax.ppermute(here[:, :WIDTH], ROWS, [(i + 1, i) for i in range(ROW_DEVS - 1)])
-    edges = jnp.stack([above, below])
-    slabs = [here, lax.ppermute(here, "core", swap)]
-    edges = [edges, lax.ppermute(edges, "core", swap)]
-
-    picked = call(pick_kernel, shaped(ROW_DEVS, 80, LANES), [SMEM, VMEM, VMEM], 10**7, 10**6)(
-        place, here, conv_weight
-    )
+    row = shaped(WIDTH, CHANS)
+    copies, first, last = call(
+        spread_kernel, [shaped(HALF, TOKENS, CHANS), row, row], [VMEM], 10**5, 10**6
+    )(slab)
+    here = exchange(copies, CHIPS)
+    above = lax.ppermute(last, ROWS, [(i, i + 1) for i in range(ROW_DEVS - 1)])
+    below = lax.ppermute(first, ROWS, [(i + 1, i) for i in range(ROW_DEVS - 1)])
+    mine = jnp.stack([above, below])
+    opposite = lax.ppermute(mine, "z_lo", swap)
+
+    picked = call(pick_kernel, shaped(ROW_DEVS, 80, LANES), [SMEM, VMEM, VMEM, ANY], 10**7, 10**6)(
+        place, here, conv_weight, opposite
+    )
+    pair = call(join_kernel, shaped(2, 2, WIDTH, CHANS), [VMEM, VMEM, ANY], 10**5, 10**6)(
+        mine, opposite, picked
+    )
+    turns = [[((i + d) % 4, i) for i in range(4)] for d in STEPS[1:]]
+    edges = jnp.concatenate([pair] + [lax.ppermute(pair, "x", turn) for turn in turns])
+    merged = call(merge_kernel, shaped(HALF, ALL, CHANS), [SMEM, VMEM, VMEM], 10**6, 10**6)(
+        place, here, edges
+    )
+    slabs = [merged, lax.ppermute(merged, "core", swap)]
     picked = exchange(picked, ROWS)
     totals = call(total_kernel, shaped(HALF, LANES, dtype=F32), [VMEM], 10**5, 10**5)(picked)
     totals = [totals, lax.ppermute(totals, "core", swap)]
@@ -330,12 +371,12 @@
     pieces = call(
         conv_kernel,
         shaped(PARTICLES, 32, LANES),
-        [SMEM, SMEM] + [VMEM] * 9,
+        [SMEM, SMEM] + [VMEM] * 7,
         2 * 10**9,
         4 * 10**6,
         vmem=32,
         scratch=(pltpu.VMEM((PARTICLES, 32, LANES), BF16),),
-    )(place, ancestors, ada_scale[None], ada_shift[None], weights, *totals, *slabs, *edges)
+    )(place, ancestors, ada_scale[None], ada_shift[None], weights, *totals, *slabs)
     pieces = exchange(pieces, PART)
 
     resid, sums = call(

time: 166 us -> 176 us (1.060)
  blocking collectives: 82.6 us -> 111 us
  waiting for transfers between devices: 22.4 us -> 7.75 us
  starting transfers between devices: 39.5 us -> 37.2 us
    all_to_all x4 -> x5, blocking collectives: 82.6 us -> 111 us  [exchange(): return lax.all_to_all(values, axes, split_axis=0, concat_axis=0, tiled=True)]
    all_to_all x2 -> x1, starting transfers between devices: 24 us -> 6.66 us  [exchange(): return lax.all_to_all(values, axes, split_axis=0, concat_axis=0, tiled=True)]
    ppermute x4 -> x7, starting transfers between devices: 13.1 us -> 26 us  [the longest x3 11.3 us: per_device(): lax.ppermute(pair, 'x', turn)]
    all_to_all x2 -> x1, waiting for transfers between devices: 11.3 us -> 0.01 us  [exchange(): return lax.all_to_all(values, axes, split_axis=0, concat_axis=0, tiled=True)]
    ppermute x4 -> x7, waiting for transfers between devices: 11.1 us -> 7.74 us  [the longest x1 3.62 us: per_device(): below = lax.ppermute(first, ROWS, [(i + 1, i) for i in range(ROW_DEVS - 1)])]
    ppermute x1, starting transfers between devices: 2.52 us -> 4.6 us  [per_device(): totals = [totals, lax.ppermute(totals, 'core', swap)]]
    broadcast_in_dim x1 -> x0, local copies, waits for them, and re-layouts: 1.97 us -> none  [per_device(): here = exchange(jnp.broadcast_to(slab[None], (HALF, TOKENS, CHANS)), CHIPS)]
    pallas_call x2 -> x5, Pallas kernels: 7.26 us -> 7.56 us  [the longest x1 4.35 us: per_device(): call(conv_kernel, shaped(PARTICLES, 32, LANES), [SMEM, SMEM] + [VMEM] * 7...]
  transfers between devices with their start and end apart: 7 -> 9, of which waited for: 3 -> 4; matrix products, arithmetic and copies ran while one was open for 0% -> 0% of each run, Pallas kernels for 1% -> 1%
where the time goes in v8:
time: 176 us; the launch traced here: 174 us
  blocking collectives  111 us (63%)
  starting transfers between devices  37.2 us (21%)
  Pallas kernels  16.6 us (9%)
  waiting for transfers between devices  7.75 us (4%)
    all_to_all x5, blocking collectives, exchange(): return lax.all_to_all(values, axes, split_axis=0, concat_axis=0, tiled=True)  111 us
    ppermute x3, starting transfers between devices, per_device(): lax.ppermute(pair, 'x', turn)  11.3 us
    ppermute x1, starting transfers between devices, per_device(): slabs = [merged, lax.ppermute(merged, 'core', swap)]  6.81 us
    all_to_all x1, starting transfers between devices, exchange(): return lax.all_to_all(values, axes, split_axis=0, concat_axis=0, tiled=True)  6.66 us
    ppermute x1, starting transfers between devices, per_device(): totals = [totals, lax.ppermute(totals, 'core', swap)]  4.6 us
    pallas_call x1, Pallas kernels, per_device(): call(attend_kernel, shaped(ROW_DEVS, 16, LANES), [VMEM], 2 * 10 ** 9, 2 *...  4.53 us
    pallas_call x1, Pallas kernels, per_device(): call(conv_kernel, shaped(PARTICLES, 32, LANES), [SMEM, SMEM] + [VMEM] * 7...  4.35 us
    ppermute x1, waiting for transfers between devices, per_device(): below = lax.ppermute(first, ROWS, [(i + 1, i) for i in range(ROW_DEVS - 1)])  3.62 us
  transfers between devices with their start and end apart: 9, of which 4 were waited for; matrix products, arithmetic and copies ran while one was open for 0% of the time, Pallas kernels for 1%

profile of v8, /device:TPU:1, one launch (start us, length us, event | category | flops | bytes accessed | tf_op | source)
XLA Modules:
  0.0 173.8 jit_solution(12601863555861533045)
XLA Ops:
  0.0 0.0 copy-start.2
  0.0 0.0 copy-start.3
  0.0 0.9 copy-done.3
  0.9 1.0 shard_map.73
  2.0 6.7 %all-to-all-start = ((bf16[8,96,640]{2,1,0:T(8,128)(2,1)}), bf16[8,96,640]{2,1,0:T(8,128)(2,1)S(1)}, u32[]{:S(2)}, u32[]{:S(2)}) async-start(bf16[8,96,640]{2,1,0:T(8,128)(2,1)} %get-tuple-element.10), calls=%async_computation | async-start | bytes 1966080 | tf_op jit(solution)/shard_map/all_to_all | solution.py:324
  8.6 3.2 %collective-permute-start = (bf16[24,640]{1,0:T(8,128)(2,1)S(1)}, bf16[24,640]{1,0:T(8,128)(2,1)S(1)}, u32[]{:S(2)}, u32[]{:S(2)}) collective-permute-start(bf16[24,640]{1,0:T(8,128)(2,1)S(1)} %get-tuple-element.11), channel_id=1, source_target_pairs={{0,1},{1,2},{2,3},{3,4},{4,5},{5,6},{6,7},{7,8},{8,9},{9,10},{10,1... | collective-permute-start | bytes 92168 | tf_op jit(solution)/shard_map/ppermute | solution.py:340
  11.8 1.3 collective-permute-start.1
  13.1 0.0 collective-permute-done
  13.2 3.6 %collective-permute-done.1 = bf16[24,640]{1,0:T(8,128)(2,1)S(1)} collective-permute-done((bf16[24,640]{1,0:T(8,128)(2,1)S(1)}, bf16[24,640]{1,0:T(8,128)(2,1)S(1)}, u32[]{:S(2)}, u32[]{:S(2)}) %collective-permute-start.1) | collective-permute-done | bytes 30752 | tf_op jit(solution)/shard_map/ppermute | solution.py:341
  16.8 3.4 %collective-permute-start.2 = (bf16[2,24,640]{2,1,0:T(8,128)(2,1)S(1)}, bf16[2,24,640]{2,1,0:T(8,128)(2,1)S(1)}, u32[]{:S(2)}, u32[]{:S(2)}) collective-permute-start(bf16[2,24,640]{2,1,0:T(8,128)(2,1)S(1)} %pad_maximum_fusion.1.mine_ref), channel_id=1, source_target_pairs={{0,64},{64,0},{1,65},{65,1},{2,66},{66,2},{3,67},{67,3},{4,68},{68... | collective-permute-start | bytes 184328 | tf_op jit(solution)/shard_map/ppermute | solution.py:343
  20.2 0.1 stack.32.place_ref
  20.3 2.3 %collective-permute-done.2._.opposite_ref = bf16[2,24,640]{2,1,0:T(8,128)(2,1)S(1)} collective-permute-done((bf16[2,24,640]{2,1,0:T(8,128)(2,1)S(1)}, bf16[2,24,640]{2,1,0:T(8,128)(2,1)S(1)}, u32[]{:S(2)}, u32[]{:S(2)}) %collective-permute-start.2) | collective-permute-done | bytes 61472 | tf_op jit(solution)/shard_map/ppermute | solution.py:343
  22.5 0.0 all-to-all-done.x_ref
  22.5 0.0 copy-done.2
  22.6 1.5 shard_map.74._
  24.1 4.8 %collective-permute-start.6 = (bf16[2,2,24,640]{3,2,1,0:T(8,128)(2,1)S(1)}, bf16[2,2,24,640]{3,2,1,0:T(8,128)(2,1)S(1)}, u32[]{:S(2)}, u32[]{:S(2)}) collective-permute-start(bf16[2,2,24,640]{3,2,1,0:T(8,128)(2,1)S(1)} %shard_map.77), channel_id=1, source_target_pairs={{256,0},{384,128},{0,256},{128,384},{257,1},{385,129},{1,257},{129... | collective-permute-start | bytes 368648 | tf_op jit(solution)/shard_map/ppermute | solution.py:352
  28.9 2.3 %collective-permute-start.5 = (bf16[2,2,24,640]{3,2,1,0:T(8,128)(2,1)S(1)}, bf16[2,2,24,640]{3,2,1,0:T(8,128)(2,1)S(1)}, u32[]{:S(2)}, u32[]{:S(2)}) collective-permute-start(bf16[2,2,24,640]{3,2,1,0:T(8,128)(2,1)S(1)} %shard_map.77), channel_id=1, source_target_pairs={{384,0},{0,128},{128,256},{256,384},{385,1},{1,129},{129,257},{257... | collective-permute-start | bytes 368648 | tf_op jit(solution)/shard_map/ppermute | solution.py:352
  31.2 4.2 %collective-permute-start.4 = (bf16[2,2,24,640]{3,2,1,0:T(8,128)(2,1)S(1)}, bf16[2,2,24,640]{3,2,1,0:T(8,128)(2,1)S(1)}, u32[]{:S(2)}, u32[]{:S(2)}) collective-permute-start(bf16[2,2,24,640]{3,2,1,0:T(8,128)(2,1)S(1)} %shard_map.77), channel_id=1, source_target_pairs={{128,0},{256,128},{384,256},{0,384},{129,1},{257,129},{385,257},{1... | collective-permute-start | bytes 368648 | tf_op jit(solution)/shard_map/ppermute | solution.py:352
  35.4 0.0 collective-permute-done.6
  35.4 1.0 collective-permute-done.5
  36.4 0.9 collective-permute-done.4
  37.2 0.1 pad_maximum_fusion.edge_ref
  37.3 0.7 shard_map.78.refs_2_
  38.0 0.0 copy-start.5
  38.0 0.0 copy-start.6
  38.0 0.0 copy-start.4
  38.0 6.8 %collective-permute-start.7 = (bf16[8,144,640]{2,1,0:T(8,128)(2,1)S(1)}, bf16[8,144,640]{2,1,0:T(8,128)(2,1)S(1)}, u32[]{:S(2)}, u32[]{:S(2)}) collective-permute-start(bf16[8,144,640]{2,1,0:T(8,128)(2,1)S(1)} %shard_map.78.refs_2_), channel_id=1, source_target_pairs={{0,32},{32,0},{1,33},{33,1},{2,34},{34,2},{3,35},{35,3},{4,36},{36... | collective-permute-start | bytes 4423688 | tf_op jit(solution)/shard_map/ppermute | solution.py:356
  44.8 34.8 %all_to_all.30.x_ref = bf16[32,80,128]{2,1,0:T(8,128)(2,1)S(1)} all-to-all(bf16[32,80,128]{2,1,0:T(8,128)(2,1)S(1)} %shard_map.74._), channel_id=1, replica_groups=mesh['x'=4,'z_lo'=2,'core'=2,'z_hi'=4,'y'=8] {'z_hi','y'}, dimensions={0} | all-to-all | bytes 1310720 | tf_op jit(solution)/shard_map/all_to_all | solution.py:324
  79.7 0.1 shard_map.76.refs_0_
  79.8 4.6 %collective-permute-start.3 = (f32[8,128]{1,0:T(8,128)S(1)}, f32[8,128]{1,0:T(8,128)S(1)}, u32[]{:S(2)}, u32[]{:S(2)}) collective-permute-start(f32[8,128]{1,0:T(8,128)S(1)} %shard_map.76.refs_0_), channel_id=1, source_target_pairs={{0,32},{32,0},{1,33},{33,1},{2,34},{34,2},{3,35},{35,3},{4,36},{36... | collective-permute-start | bytes 12296 | tf_op jit(solution)/shard_map/ppermute | solution.py:359
  84.4 0.0 copy-done.5
  84.4 0.0 copy-done.6
  84.4 1.5 shard_map.75.w_ref
  85.9 0.0 collective-permute-done.3.refs_1_
  86.0 0.0 collective-permute-done.7.refs_3_
  86.0 0.0 copy-done.4
  86.0 0.0 copy-start
  86.0 4.3 %shard_map.79 = bf16[16,32,128]{2,1,0:T(8,128)(2,1)S(1)} custom-call(s32[5]{0:T(128)S(1)} %stack.32.place_ref, s32[16]{0:T(128)S(1)} %copy-done.4, f32[1,640]{1,0:T(1,128)S(1)} %broadcast_in_dim.6.scale_ref, f32[1,640]{1,0:T(1,128)S(1)} %broadcast_in_dim.7.shift_ref, bf16[384,640]{1,0:T(8,128)(2,1)S(1)} %shard_map.75.w_ref, f32[8,128]{1,0:T(8,128)S(1)} %shard_map.76.refs_0_, ...), custom_call_target="tpu_custom_call" | custom-call | flops 2000000000 | bytes 4000000 | tf_op jit(solution)/shard_map/pallas_call | solution.py:371
  90.3 12.1 %all_to_all.31.x_ref = bf16[16,32,128]{2,1,0:T(8,128)(2,1)S(1)} all-to-all(bf16[16,32,128]{2,1,0:T(8,128)(2,1)S(1)} %shard_map.79), channel_id=1, replica_groups=mesh['x'=4,'z_lo'=2,'core'=2,'z_hi'=4,'y'=8] {'x','z_lo','core'}, dimensions={0} | all-to-all | bytes 262144 | tf_op jit(solution)/shard_map/all_to_all | solution.py:324
  102.4 0.7 shard_map.80
  103.2 17.0 %all_to_all.32.totals_ref = f32[32,8,128]{2,1,0:T(8,128)S(1)} all-to-all(f32[32,8,128]{2,1,0:T(8,128)S(1)} %get-tuple-element.13), channel_id=1, replica_groups=mesh['x'=4,'z_lo'=2,'core'=2,'z_hi'=4,'y'=8] {'z_hi','y'}, dimensions={0} | all-to-all | bytes 262144 | tf_op jit(solution)/shard_map/all_to_all | solution.py:324
  120.2 0.0 copy-done
  120.2 1.1 shard_map.81
  121.3 26.5 %all_to_all.33.x_ref = bf16[32,112,128]{2,1,0:T(8,128)(2,1)S(1)} all-to-all(bf16[32,112,128]{2,1,0:T(8,128)(2,1)S(1)} %shard_map.81), channel_id=1, replica_groups=mesh['x'=4,'z_lo'=2,'core'=2,'z_hi'=4,'y'=8] {'z_hi','y'}, dimensions={0} | all-to-all | bytes 1835008 | tf_op jit(solution)/shard_map/all_to_all | solution.py:324
  147.8 4.5 %shard_map.82 = bf16[32,16,128]{2,1,0:T(8,128)(2,1)S(1)} custom-call(bf16[32,112,128]{2,1,0:T(8,128)(2,1)S(1)} %all_to_all.33.x_ref), custom_call_target="tpu_custom_call" | custom-call | flops 2000000000 | bytes 2000000 | tf_op jit(solution)/shard_map/pallas_call | solution.py:401
  152.3 20.5 %all_to_all.34.x_ref = bf16[32,16,128]{2,1,0:T(8,128)(2,1)S(1)} all-to-all(bf16[32,16,128]{2,1,0:T(8,128)(2,1)S(1)} %shard_map.82), channel_id=1, replica_groups=mesh['x'=4,'z_lo'=2,'core'=2,'z_hi'=4,'y'=8] {'z_hi','y'}, dimensions={0} | all-to-all | bytes 262144 | tf_op jit(solution)/shard_map/all_to_all | solution.py:324
  172.8 0.0 copy-done.1
  172.8 1.0 shard_map.83
  (5 shorter events, 0.0 us)
Async XLA Ops:
  0.0 22.6 %copy-start.2 = (bf16[180,640]{1,0:T(8,128)(2,1)S(1)}, bf16[180,640]{1,0:T(8,128)(2,1)}, u32[]{:S(2)}) copy-start(bf16[180,640]{1,0:T(8,128)(2,1)} %w_ref.3) | copy-start | bytes 691204
  0.0 0.9 copy-start.3
  2.0 20.6 %all-to-all-start = ((bf16[8,96,640]{2,1,0:T(8,128)(2,1)}), bf16[8,96,640]{2,1,0:T(8,128)(2,1)S(1)}, u32[]{:S(2)}, u32[]{:S(2)}) async-start(bf16[8,96,640]{2,1,0:T(8,128)(2,1)} %get-tuple-element.10), calls=%async_computation | async-start | bytes 1966080 | tf_op jit(solution)/shard_map/all_to_all | solution.py:324
  8.6 4.5 %collective-permute-start = (bf16[24,640]{1,0:T(8,128)(2,1)S(1)}, bf16[24,640]{1,0:T(8,128)(2,1)S(1)}, u32[]{:S(2)}, u32[]{:S(2)}) collective-permute-start(bf16[24,640]{1,0:T(8,128)(2,1)S(1)} %get-tuple-element.11), channel_id=1, source_target_pairs={{0,1},{1,2},{2,3},{3,4},{4,5},{5,6},{6,7},{7,8},{8,9},{9,10},{10,1... | collective-permute-start | bytes 92168 | tf_op jit(solution)/shard_map/ppermute | solution.py:340
  11.8 4.9 %collective-permute-start.1 = (bf16[24,640]{1,0:T(8,128)(2,1)S(1)}, bf16[24,640]{1,0:T(8,128)(2,1)S(1)}, u32[]{:S(2)}, u32[]{:S(2)}) collective-permute-start(bf16[24,640]{1,0:T(8,128)(2,1)S(1)} %get-tuple-element.12), channel_id=1, source_target_pairs={{1,0},{2,1},{3,2},{4,3},{5,4},{6,5},{7,6},{8,7},{9,8},{10,9},{11,1... | collective-permute-start | bytes 92168 | tf_op jit(solution)/shard_map/ppermute | solution.py:341
  16.8 5.8 %collective-permute-start.2 = (bf16[2,24,640]{2,1,0:T(8,128)(2,1)S(1)}, bf16[2,24,640]{2,1,0:T(8,128)(2,1)S(1)}, u32[]{:S(2)}, u32[]{:S(2)}) collective-permute-start(bf16[2,24,640]{2,1,0:T(8,128)(2,1)S(1)} %pad_maximum_fusion.1.mine_ref), channel_id=1, source_target_pairs={{0,64},{64,0},{1,65},{65,1},{2,66},{66,2},{3,67},{67,3},{4,68},{68... | collective-permute-start | bytes 184328 | tf_op jit(solution)/shard_map/ppermute | solution.py:343
  24.1 11.3 %collective-permute-start.6 = (bf16[2,2,24,640]{3,2,1,0:T(8,128)(2,1)S(1)}, bf16[2,2,24,640]{3,2,1,0:T(8,128)(2,1)S(1)}, u32[]{:S(2)}, u32[]{:S(2)}) collective-permute-start(bf16[2,2,24,640]{3,2,1,0:T(8,128)(2,1)S(1)} %shard_map.77), channel_id=1, source_target_pairs={{256,0},{384,128},{0,256},{128,384},{257,1},{385,129},{1,257},{129... | collective-permute-start | bytes 368648 | tf_op jit(solution)/shard_map/ppermute | solution.py:352
  28.9 7.5 %collective-permute-start.5 = (bf16[2,2,24,640]{3,2,1,0:T(8,128)(2,1)S(1)}, bf16[2,2,24,640]{3,2,1,0:T(8,128)(2,1)S(1)}, u32[]{:S(2)}, u32[]{:S(2)}) collective-permute-start(bf16[2,2,24,640]{3,2,1,0:T(8,128)(2,1)S(1)} %shard_map.77), channel_id=1, source_target_pairs={{384,0},{0,128},{128,256},{256,384},{385,1},{1,129},{129,257},{257... | collective-permute-start | bytes 368648 | tf_op jit(solution)/shard_map/ppermute | solution.py:352
  31.2 6.1 %collective-permute-start.4 = (bf16[2,2,24,640]{3,2,1,0:T(8,128)(2,1)S(1)}, bf16[2,2,24,640]{3,2,1,0:T(8,128)(2,1)S(1)}, u32[]{:S(2)}, u32[]{:S(2)}) collective-permute-start(bf16[2,2,24,640]{3,2,1,0:T(8,128)(2,1)S(1)} %shard_map.77), channel_id=1, source_target_pairs={{128,0},{256,128},{384,256},{0,384},{129,1},{257,129},{385,257},{1... | collective-permute-start | bytes 368648 | tf_op jit(solution)/shard_map/ppermute | solution.py:352
  38.0 46.4 %copy-start.5 = (f32[640]{0:T(1024)S(1)}, f32[640]{0:T(1024)}, u32[]{:S(2)}) copy-start(f32[640]{0:T(1024)} %param.8) | copy-start | bytes 7684
  38.0 46.4 %copy-start.6 = (f32[640]{0:T(1024)S(1)}, f32[640]{0:T(1024)}, u32[]{:S(2)}) copy-start(f32[640]{0:T(1024)} %param.9) | copy-start | bytes 7684
  38.0 48.0 %copy-start.4 = (s32[16]{0:T(128)S(1)}, s32[16]{0:T(128)}, u32[]{:S(2)}) copy-start(s32[16]{0:T(128)} %anc_ref.1) | copy-start | bytes 196
  38.0 47.9 %collective-permute-start.7 = (bf16[8,144,640]{2,1,0:T(8,128)(2,1)S(1)}, bf16[8,144,640]{2,1,0:T(8,128)(2,1)S(1)}, u32[]{:S(2)}, u32[]{:S(2)}) collective-permute-start(bf16[8,144,640]{2,1,0:T(8,128)(2,1)S(1)} %shard_map.78.refs_2_), channel_id=1, source_target_pairs={{0,32},{32,0},{1,33},{33,1},{2,34},{34,2},{3,35},{35,3},{4,36},{36... | collective-permute-start | bytes 4423688 | tf_op jit(solution)/shard_map/ppermute | solution.py:356
  79.8 6.2 %collective-permute-start.3 = (f32[8,128]{1,0:T(8,128)S(1)}, f32[8,128]{1,0:T(8,128)S(1)}, u32[]{:S(2)}, u32[]{:S(2)}) collective-permute-start(f32[8,128]{1,0:T(8,128)S(1)} %shard_map.76.refs_0_), channel_id=1, source_target_pairs={{0,32},{32,0},{1,33},{33,1},{2,34},{34,2},{3,35},{35,3},{4,36},{36... | collective-permute-start | bytes 12296 | tf_op jit(solution)/shard_map/ppermute | solution.py:359
  86.0 34.2 %copy-start = (bf16[640,1920]{1,0:T(8,128)(2,1)S(1)}, bf16[640,1920]{1,0:T(8,128)(2,1)}, u32[]{:S(2)}) copy-start(bf16[640,1920]{1,0:T(8,128)(2,1)} %w_ref.4) | copy-start | bytes 7372804
  147.8 25.0 %copy-start.1 = (bf16[640,640]{1,0:T(8,128)(2,1)S(1)}, bf16[640,640]{1,0:T(8,128)(2,1)}, u32[]{:S(2)}) copy-start(bf16[640,640]{1,0:T(8,128)(2,1)} %w_ref.5) | copy-start | bytes 2457604

commit v9 on v6

--- a/solution.py
+++ b/solution.py
@@ -34,6 +34,7 @@
 BF16 = jnp.bfloat16
 SMEM = pl.BlockSpec(memory_space=pltpu.SMEM)
 VMEM = pl.BlockSpec(memory_space=pltpu.VMEM)
+ANY = pl.BlockSpec(memory_space=pl.ANY)
 
 
 def call(kernel, out_shape, in_specs, flops, size, vmem=16, scratch=()):
@@ -92,27 +93,51 @@
     return parts
 
 
-def pick_kernel(place_ref, x_ref, w_ref, out_ref):
+def spread_kernel(x_ref, out_ref, first_ref, last_ref):
+    out_ref[...] = jnp.broadcast_to(x_ref[...][None], out_ref.shape)
+    wide = x_ref[...].astype(F32)
+    first_ref[...] = wide[:WIDTH].astype(BF16)
+    last_ref[...] = wide[LAST:].astype(BF16)
+
+
+def join_kernel(mine_ref, opposite_ref, _, out_ref):
+    out_ref[0] = mine_ref[...]
+    out_ref[1] = opposite_ref[...]
+
+
+def pick_kernel(place_ref, w_ref, out_ref):
     row, col = iota((48, CHANS), 0), iota((48, CHANS), 1)
     chosen = ((col == row + place_ref[0] * SLICE) & (row < SLICE)).astype(F32).astype(BF16)
     picked = lax.dot_general(chosen, w_ref[...], NT, preferred_element_type=F32)
-    head = picked[:, :LANES]
     rest = jnp.concatenate([picked[:, LANES:], jnp.zeros((48, LANES - TAIL), F32)], axis=1)
     turned = pltpu.roll(pltpu.roll(rest, 48 - 20, 0), 64, 1)
-    low = jnp.where(iota((24, LANES), 1) < 64, rest[:24], turned[:24])
+    row, lane = iota((32, LANES), 0), iota((32, LANES), 1)
+    low = jnp.where(lane < 64, rest[:32], turned[:32])
+    out_ref[:SLICE] = picked[:SLICE, :LANES]
+    out_ref[SLICE:] = jnp.where(row < 20, low, 0.0)
+
+
+def slots_kernel(x_ref, part_ref, _, out_ref):
     values = [x_ref[j].astype(F32) for j in range(HALF)]
     first, second, third = thirds(group_rows(values))
-    sums = jnp.concatenate([first + pltpu.roll(second, 64, 1), third], axis=0)
-    slot = jnp.concatenate([head[:SLICE], low, sums], axis=0).astype(BF16)
+    row, lane = iota((8, LANES), 0), iota((8, LANES), 1)
+    third = jnp.where(lane < 64, third, pltpu.roll(pltpu.roll(third, 4, 0), 64, 1))
+    third = jnp.where(row < 4, third, 0.0)
+    rest = jnp.zeros((24, LANES), F32)
+    sums = pltpu.roll(jnp.concatenate([first + pltpu.roll(second, 64, 1), rest], axis=0), 20, 0)
+    sums = sums + pltpu.roll(jnp.concatenate([third, rest], axis=0), 28, 0)
+    slot = jnp.concatenate([part_ref[:SLICE], part_ref[SLICE:] + sums], axis=0).astype(BF16)
     out_ref[...] = jnp.broadcast_to(slot[None], out_ref.shape)
 
 
 def total_kernel(x_ref, out_ref):
-    total = jnp.zeros((16, LANES), F32)
+    total = jnp.zeros((32, LANES), F32)
     for r in range(ROW_DEVS):
-        total = total + x_ref[r, 64:80].astype(F32)
-    total = total[:8] + pltpu.roll(total[:8], 64, 1) + total[8:]
-    out_ref[...] = jnp.where(iota((HALF, LANES), 1) < 64, total, 0.0)
+        total = total + x_ref[r].astype(F32)[SLICE:]
+    two, third = pltpu.roll(total, 12, 0)[:8], pltpu.roll(total, 4, 0)[:8]
+    row, lane = iota((8, LANES), 0), iota((8, LANES), 1)
+    third = jnp.where(row < 4, third, pltpu.roll(pltpu.roll(third, 4, 0), 64, 1))
+    out_ref[...] = jnp.where(lane < 64, two + pltpu.roll(two, 64, 1) + third, 0.0)
 
 
 PLACE = {1: 0, 0: 1, 2: 2}
@@ -125,7 +150,7 @@
         at = r * KERNEL_ROWS
         block, off = at // LANES, at % LANES
         slot = x_ref[r].astype(F32)
-        low = jnp.concatenate([slot[SLICE:64], jnp.zeros((16, LANES), F32)], axis=0)
+        low = jnp.concatenate([slot[SLICE:], jnp.zeros((8, LANES), F32)], axis=0)
         rest = jnp.where(row < 20, low, pltpu.roll(pltpu.roll(low, 20, 0), 64, 1))
         rest = jnp.where(lane < TAIL, rest, 0.0)
         wide = jnp.concatenate([slot[:SLICE], rest, jnp.zeros((SLICE, LANES), F32)], axis=1)
@@ -168,6 +193,15 @@
     return out
 
 
+STEPS = (0, 1, 3, 2)
+
+
+def beside(place_ref, j):
+    dx = lax.rem(j // 2 + 4 - place_ref[2], 4)
+    dz = lax.rem(j % 2 + place_ref[3], 2)
+    return 2 * jnp.where(dx == 2, 3, jnp.where(dx == 3, 2, dx)) + dz
+
+
 def conv_kernel(place_ref, anc_ref, scale_ref, shift_ref, w_ref, *refs):
     totals, slabs, edges, (out_ref, done_ref) = refs[:2], refs[2:4], refs[4:6], refs[6:]
     mean, inverse = mean_and_inverse(jnp.concatenate([ref[...] for ref in totals], axis=0))
@@ -176,7 +210,7 @@
     row, col = iota((LANES, CHANS), 0), iota((LANES, CHANS), 1)
     chosen = ((col == row + place_ref[0] * SLICE) & (row < SLICE)).astype(F32).astype(BF16)
     weights = w_ref[...]
-    top, bottom = place_ref[2] == 0, place_ref[2] == ROW_DEVS - 1
+    top, bottom = place_ref[4] == 0, place_ref[4] == ROW_DEVS - 1
     each = 2
     for step in range(PARTICLES // each):
         active, raw = [], []
@@ -185,7 +219,8 @@
             x = slabs[which][j]
             raw.append(x)
             act = lambda v: silu(v.astype(F32) * gain[n : n + 1] + bias[n : n + 1])
-            above, below = act(edges[which][0, j]), act(edges[which][1, j])
+            at = beside(place_ref, j)
+            above, below = act(edges[which][at, 0]), act(edges[which][at, 1])
             active += [jnp.where(top, 0.0, above), act(x), jnp.where(bottom, 0.0, below)]
         active = jnp.concatenate(active, axis=0).astype(BF16)
         raw = jnp.concatenate(raw, axis=0)
@@ -248,32 +283,37 @@
         out_ref[slot] = jnp.zeros((SLOT, LANES), BF16)
 
 
-def attend_kernel(x_ref, out_ref, keys_ref, ones_ref, query_ref, half_ref):
+def attend_kernel(x_ref, out_ref, keys_ref, ones_ref, query_ref):
     low = iota((TOKENS, LANES), 1) < 64
     for r in range(ROW_DEVS):
         block = x_ref[r, :TOKENS]
         keys_ref[r * TOKENS : (r + 1) * TOKENS] = block
         ones_ref[r * TOKENS : (r + 1) * TOKENS] = jnp.where(low, jnp.ones_like(block), block)
         query_ref[r * 16 : (r + 1) * 16] = x_ref[r, TOKENS:].astype(F32)
-    size = 256
+    size, chunk = 512, 1024
     low_q = iota((size, LANES), 1) < 64
     factor = 0.125 * 1.4426950408889634
-    for n in range(2):
-        here = query_ref[n * size : (n + 1) * size]
-        for side in range(2):
-            turned = here if side == 0 else pltpu.roll(here, 64, 1)
-            query = jnp.where(low_q, turned, 0.0).astype(BF16)
-            scores = lax.dot_general(query, keys_ref[...], NT, preferred_element_type=F32)
-            top = jnp.max(scores, axis=1, keepdims=True)
-            weights = jnp.exp2((scores - top) * factor).astype(BF16)
-            result = jnp.dot(weights, ones_ref[...], preferred_element_type=F32)
-            other = pltpu.roll(result, 64, 1)
-            if side == 0:
-                half_ref[...] = other / result
-            else:
-                both = jnp.where(low_q, half_ref[...], result / other).astype(BF16)
-                for r in range(size // 16):
-                    out_ref[n * (size // 16) + r] = both[r * 16 : (r + 1) * 16]
+    done = []
+    for side in range(2):
+        here = query_ref[...]
+        turned = here if side == 0 else pltpu.roll(here, 64, 1)
+        query = jnp.where(low_q, turned, 0.0).astype(BF16)
+        top = result = None
+        for c in range(0, ROW_DEVS * TOKENS, chunk):
+            span = slice(c, c + chunk)
+            scores = lax.dot_general(query, keys_ref[span], NT, preferred_element_type=F32)
+            higher = jnp.max(scores, axis=1, keepdims=True)
+            if c:
+                higher = jnp.maximum(higher, top)
+            weights = jnp.exp2((scores - higher) * factor).astype(BF16)
+            new = jnp.dot(weights, ones_ref[span], preferred_element_type=F32)
+            result = result * jnp.exp2((top - higher) * factor) + new if c else new
+            top = higher
+        done.append((result, pltpu.roll(result, 64, 1)))
+    (first, first_turned), (second, second_turned) = done
+    both = jnp.where(low_q, first_turned / first, second / second_turned).astype(BF16)
+    for r in range(ROW_DEVS):
+        out_ref[r] = both[r * 16 : (r + 1) * 16]
 
 
 def output_kernel(x_ref, resid_ref, w_ref, out_ref, wide_ref):
@@ -299,20 +339,33 @@
     slab = latent.reshape(TOKENS, CHANS)
     particle = lax.axis_index(PART).astype(jnp.int32)
     place = jnp.stack(
-        [particle] + [lax.axis_index(a).astype(jnp.int32) for a in ("core", ROWS)]
+        [particle] + [lax.axis_index(a).astype(jnp.int32) for a in ("core", "x", "z_lo", ROWS)]
     )
 
     swap = [(0, 1), (1, 0)]
-    here = exchange(jnp.broadcast_to(slab[None], (HALF, TOKENS, CHANS)), CHIPS)
-    above = lax.ppermute(here[:, LAST:], ROWS, [(i, i + 1) for i in range(ROW_DEVS - 1)])
-    below = lax.ppermute(here[:, :WIDTH], ROWS, [(i + 1, i) for i in range(ROW_DEVS - 1)])
-    edges = jnp.stack([above, below])
+    row = shaped(WIDTH, CHANS)
+    copies, first, last = call(
+        spread_kernel, [shaped(HALF, TOKENS, CHANS), row, row], [VMEM], 10**5, 10**6
+    )(slab)
+    here = exchange(copies, CHIPS)
     slabs = [here, lax.ppermute(here, "core", swap)]
+    above = lax.ppermute(last, ROWS, [(i, i + 1) for i in range(ROW_DEVS - 1)])
+    below = lax.ppermute(first, ROWS, [(i + 1, i) for i in range(ROW_DEVS - 1)])
+    mine = jnp.stack([above, below])
+    opposite = lax.ppermute(mine, "z_lo", swap)
+
+    columns = call(pick_kernel, shaped(72, LANES, dtype=F32), [SMEM, VMEM], 10**7, 10**6, vmem=8)(
+        place, conv_weight
+    )
+    picked = call(slots_kernel, shaped(ROW_DEVS, 72, LANES), [VMEM, VMEM, ANY], 10**7, 10**6)(
+        here, columns, opposite
+    )
+    pair = call(join_kernel, shaped(2, 2, WIDTH, CHANS), [VMEM, VMEM, ANY], 10**5, 10**6)(
+        mine, opposite, picked
+    )
+    turns = [[((i + d) % 4, i) for i in range(4)] for d in STEPS[1:]]
+    edges = jnp.concatenate([pair] + [lax.ppermute(pair, "x", turn) for turn in turns])
     edges = [edges, lax.ppermute(edges, "core", swap)]
-
-    picked = call(pick_kernel, shaped(ROW_DEVS, 80, LANES), [SMEM, VMEM, VMEM], 10**7, 10**6)(
-        place, here, conv_weight
-    )
     picked = exchange(picked, ROWS)
     totals = call(total_kernel, shaped(HALF, LANES, dtype=F32), [VMEM], 10**5, 10**5)(picked)
     totals = [totals, lax.ppermute(totals, "core", swap)]
@@ -333,7 +386,7 @@
         [SMEM, SMEM] + [VMEM] * 9,
         2 * 10**9,
         4 * 10**6,
-        vmem=32,
+        vmem=20,
         scratch=(pltpu.VMEM((PARTICLES, 32, LANES), BF16),),
     )(place, ancestors, ada_scale[None], ada_shift[None], weights, *totals, *slabs, *edges)
     pieces = exchange(pieces, PART)
@@ -363,12 +416,11 @@
         [VMEM],
         2 * 10**9,
         2 * 10**6,
-        vmem=40,
+        vmem=32,
         scratch=(
             pltpu.VMEM((rows, LANES), BF16),
             pltpu.VMEM((rows, LANES), BF16),
             pltpu.VMEM((ROW_DEVS * 16, LANES), F32),
-            pltpu.VMEM((256, LANES), F32),
         ),
     )(slots)
     mixed = exchange(mixed, ROWS)

time: 166 us -> 162 us (0.976)
  waiting for transfers between devices: 22.4 us -> 6.2 us
  starting transfers between devices: 39.5 us -> 51.7 us
    ppermute x2 -> x6, starting transfers between devices: 4.72 us -> 19.5 us  [the longest x3 11.7 us: per_device(): lax.ppermute(pair, 'x', turn)]
    all_to_all x2, waiting for transfers between devices: 11.3 us -> 0.01 us  [exchange(): return lax.all_to_all(values, axes, split_axis=0, concat_axis=0, tiled=True)]
    ppermute x2 -> x6, waiting for transfers between devices: 11.1 us -> 6.19 us  [the longest x1 3.62 us: per_device(): below = lax.ppermute(first, ROWS, [(i + 1, i) for i in range(ROW_DEVS - 1)])]
    all_to_all x2, starting transfers between devices: 24 us -> 21.7 us  [exchange(): return lax.all_to_all(values, axes, split_axis=0, concat_axis=0, tiled=True)]
    broadcast_in_dim x1 -> x0, local copies, waits for them, and re-layouts: 1.97 us -> none  [per_device(): here = exchange(jnp.broadcast_to(slab[None], (HALF, TOKENS, CHANS)), CHIPS)]
    unnamed x12 -> x14, local copies, waits for them, and re-layouts: 0.02 us -> 1.86 us
    pallas_call x1 -> x4, Pallas kernels: 2.34 us -> 3.63 us  [the longest x1 1.73 us: per_device(): call(slots_kernel, shaped(ROW_DEVS, 72, LANES), [VMEM, VMEM, ANY], 10 **...]
  transfers between devices with their start and end apart: 7 -> 11, of which waited for: 3 -> 4; matrix products, arithmetic and copies ran while one was open for 0% -> 0% of each run, Pallas kernels for 1% -> 2%
where the time goes in v9:
time: 162 us; the launch traced here: 159 us
  blocking collectives  82.6 us (51%)
  starting transfers between devices  51.7 us (32%)
  Pallas kernels  16.7 us (10%)
  waiting for transfers between devices  6.2 us (4%)
  local copies, waits for them, and re-layouts  1.96 us (1%)
    all_to_all x4, blocking collectives, exchange(): return lax.all_to_all(values, axes, split_axis=0, concat_axis=0, tiled=True)  82.6 us
    all_to_all x2, starting transfers between devices, exchange(): return lax.all_to_all(values, axes, split_axis=0, concat_axis=0, tiled=True)  21.7 us
    ppermute x3, starting transfers between devices, per_device(): lax.ppermute(pair, 'x', turn)  11.7 us
    ppermute x1, starting transfers between devices, per_device(): slabs = [here, lax.ppermute(here, 'core', swap)]  5.23 us
    pallas_call x1, Pallas kernels, per_device(): call(conv_kernel, shaped(PARTICLES, 32, LANES), [SMEM, SMEM] + [VMEM] * 9...  4.3 us
    pallas_call x1, Pallas kernels, per_device(): call(attend_kernel, shaped(ROW_DEVS, 16, LANES), [VMEM], 2 * 10 ** 9, 2 *...  4.23 us
    ppermute x1, waiting for transfers between devices, per_device(): below = lax.ppermute(first, ROWS, [(i + 1, i) for i in range(ROW_DEVS - 1)])  3.62 us
    ppermute x1, starting transfers between devices, per_device(): opposite = lax.ppermute(mine, 'z_lo', swap)  3.37 us
  transfers between devices with their start and end apart: 11, of which 4 were waited for; matrix products, arithmetic and copies ran while one was open for 0% of the time, Pallas kernels for 2%

profile of v9, /device:TPU:1, one launch (start us, length us, event | category | flops | bytes accessed | tf_op | source)
XLA Modules:
  0.0 159.4 jit_solution(1666884467879866736)
XLA Ops:
  0.0 0.0 copy-start.3
  0.0 0.9 copy-done.3
  0.9 1.0 shard_map.73
  1.9 6.7 %all-to-all-start = ((bf16[8,96,640]{2,1,0:T(8,128)(2,1)}), bf16[8,96,640]{2,1,0:T(8,128)(2,1)S(1)}, u32[]{:S(2)}, u32[]{:S(2)}) async-start(bf16[8,96,640]{2,1,0:T(8,128)(2,1)} %get-tuple-element.10), calls=%async_computation | async-start | bytes 1966080 | tf_op jit(solution)/shard_map/all_to_all | solution.py:335
  8.6 3.2 %collective-permute-start = (bf16[24,640]{1,0:T(8,128)(2,1)S(1)}, bf16[24,640]{1,0:T(8,128)(2,1)S(1)}, u32[]{:S(2)}, u32[]{:S(2)}) collective-permute-start(bf16[24,640]{1,0:T(8,128)(2,1)S(1)} %get-tuple-element.11), channel_id=1, source_target_pairs={{0,1},{1,2},{2,3},{3,4},{4,5},{5,6},{6,7},{7,8},{8,9},{9,10},{10,1... | collective-permute-start | bytes 92168 | tf_op jit(solution)/shard_map/ppermute | solution.py:352
  11.8 1.3 collective-permute-start.1
  13.1 0.0 collective-permute-done
  13.1 3.6 %collective-permute-done.1 = bf16[24,640]{1,0:T(8,128)(2,1)S(1)} collective-permute-done((bf16[24,640]{1,0:T(8,128)(2,1)S(1)}, bf16[24,640]{1,0:T(8,128)(2,1)S(1)}, u32[]{:S(2)}, u32[]{:S(2)}) %collective-permute-start.1) | collective-permute-done | bytes 30752 | tf_op jit(solution)/shard_map/ppermute | solution.py:353
  16.8 3.4 %collective-permute-start.2 = (bf16[2,24,640]{2,1,0:T(8,128)(2,1)S(1)}, bf16[2,24,640]{2,1,0:T(8,128)(2,1)S(1)}, u32[]{:S(2)}, u32[]{:S(2)}) collective-permute-start(bf16[2,24,640]{2,1,0:T(8,128)(2,1)S(1)} %pad_maximum_fusion.1.mine_ref), channel_id=1, source_target_pairs={{0,64},{64,0},{1,65},{65,1},{2,66},{66,2},{3,67},{67,3},{4,68},{68... | collective-permute-start | bytes 184328 | tf_op jit(solution)/shard_map/ppermute | solution.py:355
  20.1 0.1 stack.32.place_ref
  20.2 0.0 copy-start.2
  20.2 0.9 copy-done.2
  21.2 0.8 shard_map.74.part_ref
  22.0 0.5 collective-permute-done.2._.opposite_ref
  22.5 0.0 all-to-all-done.x_ref.refs_2_
  22.5 1.7 %shard_map.75._ = bf16[32,72,128]{2,1,0:T(8,128)(2,1)} custom-call(bf16[8,96,640]{2,1,0:T(8,128)(2,1)S(1)} %all-to-all-done.x_ref.refs_2_, f32[72,128]{1,0:T(8,128)S(1)} %shard_map.74.part_ref, bf16[2,24,640]{2,1,0:T(8,128)(2,1)S(1)} %collective-permute-done.2._.opposite_ref), custom_call_target="tpu_custom_call" | custom-call | flops 10000000 | bytes 1000000 | tf_op jit(solution)/shard_map/pallas_call | solution.py:360
  24.2 15.1 %all-to-all-start.1 = ((bf16[32,72,128]{2,1,0:T(8,128)(2,1)}), bf16[32,72,128]{2,1,0:T(8,128)(2,1)S(1)}, u32[]{:S(2)}, u32[]{:S(2)}) async-start(bf16[32,72,128]{2,1,0:T(8,128)(2,1)} %shard_map.75._), calls=%async_computation.1 | async-start | bytes 1179648 | tf_op jit(solution)/shard_map/all_to_all | solution.py:335
  39.3 5.2 %collective-permute-start.4 = (bf16[8,96,640]{2,1,0:T(8,128)(2,1)S(1)}, bf16[8,96,640]{2,1,0:T(8,128)(2,1)S(1)}, u32[]{:S(2)}, u32[]{:S(2)}) collective-permute-start(bf16[8,96,640]{2,1,0:T(8,128)(2,1)S(1)} %all-to-all-done.x_ref.refs_2_), channel_id=1, source_target_pairs={{0,32},{32,0},{1,33},{33,1},{2,34},{34,2},{3,35},{35,3},{4,36},{36... | collective-permute-start | bytes 2949128 | tf_op jit(solution)/shard_map/ppermute | solution.py:351
  44.6 5.2 %collective-permute-start.7 = (bf16[2,2,24,640]{3,2,1,0:T(8,128)(2,1)S(1)}, bf16[2,2,24,640]{3,2,1,0:T(8,128)(2,1)S(1)}, u32[]{:S(2)}, u32[]{:S(2)}) collective-permute-start(bf16[2,2,24,640]{3,2,1,0:T(8,128)(2,1)S(1)} %shard_map.78), channel_id=1, source_target_pairs={{256,0},{384,128},{0,256},{128,384},{257,1},{385,129},{1,257},{129... | collective-permute-start | bytes 368648 | tf_op jit(solution)/shard_map/ppermute | solution.py:367
  49.8 2.2 %collective-permute-start.6 = (bf16[2,2,24,640]{3,2,1,0:T(8,128)(2,1)S(1)}, bf16[2,2,24,640]{3,2,1,0:T(8,128)(2,1)S(1)}, u32[]{:S(2)}, u32[]{:S(2)}) collective-permute-start(bf16[2,2,24,640]{3,2,1,0:T(8,128)(2,1)S(1)} %shard_map.78), channel_id=1, source_target_pairs={{384,0},{0,128},{128,256},{256,384},{385,1},{1,129},{129,257},{257... | collective-permute-start | bytes 368648 | tf_op jit(solution)/shard_map/ppermute | solution.py:367
  52.0 4.3 %collective-permute-start.5 = (bf16[2,2,24,640]{3,2,1,0:T(8,128)(2,1)S(1)}, bf16[2,2,24,640]{3,2,1,0:T(8,128)(2,1)S(1)}, u32[]{:S(2)}, u32[]{:S(2)}) collective-permute-start(bf16[2,2,24,640]{3,2,1,0:T(8,128)(2,1)S(1)} %shard_map.78), channel_id=1, source_target_pairs={{128,0},{256,128},{384,256},{0,384},{129,1},{257,129},{385,257},{1... | collective-permute-start | bytes 368648 | tf_op jit(solution)/shard_map/ppermute | solution.py:367
  56.3 0.0 collective-permute-done.7
  56.3 1.2 collective-permute-done.6
  57.5 0.9 collective-permute-done.5
  58.4 0.1 pad_maximum_fusion.refs_4_
  58.4 3.3 %collective-permute-start.8 = (bf16[8,2,24,640]{3,2,1,0:T(8,128)(2,1)S(1)}, bf16[8,2,24,640]{3,2,1,0:T(8,128)(2,1)S(1)}, u32[]{:S(2)}, u32[]{:S(2)}) collective-permute-start(bf16[8,2,24,640]{3,2,1,0:T(8,128)(2,1)S(1)} %pad_maximum_fusion.refs_4_), channel_id=1, source_target_pairs={{0,32},{32,0},{1,33},{33,1},{2,34},{34,2},{3,35},{35,3},{4,36},{36... | collective-permute-start | bytes 1474568 | tf_op jit(solution)/shard_map/ppermute | solution.py:368
  61.8 0.0 all-to-all-done.1.x_ref
  61.8 0.1 shard_map.77.refs_0_
  61.9 1.9 %collective-permute-start.3 = (f32[8,128]{1,0:T(8,128)S(1)}, f32[8,128]{1,0:T(8,128)S(1)}, u32[]{:S(2)}, u32[]{:S(2)}) collective-permute-start(f32[8,128]{1,0:T(8,128)S(1)} %shard_map.77.refs_0_), channel_id=1, source_target_pairs={{0,32},{32,0},{1,33},{33,1},{2,34},{34,2},{3,35},{35,3},{4,36},{36... | collective-permute-start | bytes 12296 | tf_op jit(solution)/shard_map/ppermute | solution.py:371
  63.8 0.0 copy-done.5
  63.9 0.0 copy-done.6
  63.9 1.5 shard_map.76.w_ref
  65.4 0.0 copy-start
  65.4 0.0 collective-permute-done.8.refs_5_
  65.4 0.0 collective-permute-done.4.refs_3_
  65.4 0.0 collective-permute-done.3.refs_1_
  65.5 0.0 copy-done.4
  65.5 4.3 %shard_map.79 = bf16[16,32,128]{2,1,0:T(8,128)(2,1)S(1)} custom-call(s32[5]{0:T(128)S(1)} %stack.32.place_ref, s32[16]{0:T(128)S(1)} %copy-done.4, f32[1,640]{1,0:T(1,128)S(1)} %broadcast_in_dim.6.scale_ref, f32[1,640]{1,0:T(1,128)S(1)} %broadcast_in_dim.7.shift_ref, bf16[384,640]{1,0:T(8,128)(2,1)S(1)} %shard_map.76.w_ref, f32[8,128]{1,0:T(8,128)S(1)} %shard_map.77.refs_0_, ...), custom_call_target="tpu_custom_call" | custom-call | flops 2000000000 | bytes 4000000 | tf_op jit(solution)/shard_map/pallas_call | solution.py:383
  69.8 12.3 %all_to_all.30.x_ref = bf16[16,32,128]{2,1,0:T(8,128)(2,1)S(1)} all-to-all(bf16[16,32,128]{2,1,0:T(8,128)(2,1)S(1)} %shard_map.79), channel_id=1, replica_groups=mesh['x'=4,'z_lo'=2,'core'=2,'z_hi'=4,'y'=8] {'x','z_lo','core'}, dimensions={0} | all-to-all | bytes 262144 | tf_op jit(solution)/shard_map/all_to_all | solution.py:335
  82.1 0.7 shard_map.80
  82.8 23.3 %all_to_all.31.totals_ref = f32[32,8,128]{2,1,0:T(8,128)S(1)} all-to-all(f32[32,8,128]{2,1,0:T(8,128)S(1)} %get-tuple-element.13), channel_id=1, replica_groups=mesh['x'=4,'z_lo'=2,'core'=2,'z_hi'=4,'y'=8] {'z_hi','y'}, dimensions={0} | all-to-all | bytes 262144 | tf_op jit(solution)/shard_map/all_to_all | solution.py:335
  106.1 0.0 copy-done
  106.1 1.1 shard_map.81
  107.2 26.5 %all_to_all.32.x_ref = bf16[32,112,128]{2,1,0:T(8,128)(2,1)S(1)} all-to-all(bf16[32,112,128]{2,1,0:T(8,128)(2,1)S(1)} %shard_map.81), channel_id=1, replica_groups=mesh['x'=4,'z_lo'=2,'core'=2,'z_hi'=4,'y'=8] {'z_hi','y'}, dimensions={0} | all-to-all | bytes 1835008 | tf_op jit(solution)/shard_map/all_to_all | solution.py:335
  133.7 4.2 %shard_map.82 = bf16[32,16,128]{2,1,0:T(8,128)(2,1)S(1)} custom-call(bf16[32,112,128]{2,1,0:T(8,128)(2,1)S(1)} %all_to_all.32.x_ref), custom_call_target="tpu_custom_call" | custom-call | flops 2000000000 | bytes 2000000 | tf_op jit(solution)/shard_map/pallas_call | solution.py:413
  138.0 20.5 %all_to_all.33.x_ref = bf16[32,16,128]{2,1,0:T(8,128)(2,1)S(1)} all-to-all(bf16[32,16,128]{2,1,0:T(8,128)(2,1)S(1)} %shard_map.82), channel_id=1, replica_groups=mesh['x'=4,'z_lo'=2,'core'=2,'z_hi'=4,'y'=8] {'z_hi','y'}, dimensions={0} | all-to-all | bytes 262144 | tf_op jit(solution)/shard_map/all_to_all | solution.py:335
  158.5 0.0 copy-done.1
  158.5 1.0 shard_map.83
  (8 shorter events, 0.0 us)
Async XLA Ops:
  0.0 0.9 copy-start.3
  1.9 20.6 %all-to-all-start = ((bf16[8,96,640]{2,1,0:T(8,128)(2,1)}), bf16[8,96,640]{2,1,0:T(8,128)(2,1)S(1)}, u32[]{:S(2)}, u32[]{:S(2)}) async-start(bf16[8,96,640]{2,1,0:T(8,128)(2,1)} %get-tuple-element.10), calls=%async_computation | async-start | bytes 1966080 | tf_op jit(solution)/shard_map/all_to_all | solution.py:335
  8.6 4.5 %collective-permute-start = (bf16[24,640]{1,0:T(8,128)(2,1)S(1)}, bf16[24,640]{1,0:T(8,128)(2,1)S(1)}, u32[]{:S(2)}, u32[]{:S(2)}) collective-permute-start(bf16[24,640]{1,0:T(8,128)(2,1)S(1)} %get-tuple-element.11), channel_id=1, source_target_pairs={{0,1},{1,2},{2,3},{3,4},{4,5},{5,6},{6,7},{7,8},{8,9},{9,10},{10,1... | collective-permute-start | bytes 92168 | tf_op jit(solution)/shard_map/ppermute | solution.py:352
  11.8 4.9 %collective-permute-start.1 = (bf16[24,640]{1,0:T(8,128)(2,1)S(1)}, bf16[24,640]{1,0:T(8,128)(2,1)S(1)}, u32[]{:S(2)}, u32[]{:S(2)}) collective-permute-start(bf16[24,640]{1,0:T(8,128)(2,1)S(1)} %get-tuple-element.12), channel_id=1, source_target_pairs={{1,0},{2,1},{3,2},{4,3},{5,4},{6,5},{7,6},{8,7},{9,8},{10,9},{11,1... | collective-permute-start | bytes 92168 | tf_op jit(solution)/shard_map/ppermute | solution.py:353
  16.8 5.8 %collective-permute-start.2 = (bf16[2,24,640]{2,1,0:T(8,128)(2,1)S(1)}, bf16[2,24,640]{2,1,0:T(8,128)(2,1)S(1)}, u32[]{:S(2)}, u32[]{:S(2)}) collective-permute-start(bf16[2,24,640]{2,1,0:T(8,128)(2,1)S(1)} %pad_maximum_fusion.1.mine_ref), channel_id=1, source_target_pairs={{0,64},{64,0},{1,65},{65,1},{2,66},{66,2},{3,67},{67,3},{4,68},{68... | collective-permute-start | bytes 184328 | tf_op jit(solution)/shard_map/ppermute | solution.py:355
  20.2 0.9 copy-start.2
  22.0 41.8 %copy-start.5 = (f32[640]{0:T(1024)S(1)}, f32[640]{0:T(1024)}, u32[]{:S(2)}) copy-start(f32[640]{0:T(1024)} %param.8) | copy-start | bytes 7684
  22.0 41.9 %copy-start.6 = (f32[640]{0:T(1024)S(1)}, f32[640]{0:T(1024)}, u32[]{:S(2)}) copy-start(f32[640]{0:T(1024)} %param.9) | copy-start | bytes 7684
  24.2 41.2 %copy-start.4 = (s32[16]{0:T(128)S(1)}, s32[16]{0:T(128)}, u32[]{:S(2)}) copy-start(s32[16]{0:T(128)} %anc_ref.1) | copy-start | bytes 196
  24.2 37.6 %all-to-all-start.1 = ((bf16[32,72,128]{2,1,0:T(8,128)(2,1)}), bf16[32,72,128]{2,1,0:T(8,128)(2,1)S(1)}, u32[]{:S(2)}, u32[]{:S(2)}) async-start(bf16[32,72,128]{2,1,0:T(8,128)(2,1)} %shard_map.75._), calls=%async_computation.1 | async-start | bytes 1179648 | tf_op jit(solution)/shard_map/all_to_all | solution.py:335
  39.3 26.1 %collective-permute-start.4 = (bf16[8,96,640]{2,1,0:T(8,128)(2,1)S(1)}, bf16[8,96,640]{2,1,0:T(8,128)(2,1)S(1)}, u32[]{:S(2)}, u32[]{:S(2)}) collective-permute-start(bf16[8,96,640]{2,1,0:T(8,128)(2,1)S(1)} %all-to-all-done.x_ref.refs_2_), channel_id=1, source_target_pairs={{0,32},{32,0},{1,33},{33,1},{2,34},{34,2},{3,35},{35,3},{4,36},{36... | collective-permute-start | bytes 2949128 | tf_op jit(solution)/shard_map/ppermute | solution.py:351
  44.6 11.7 %collective-permute-start.7 = (bf16[2,2,24,640]{3,2,1,0:T(8,128)(2,1)S(1)}, bf16[2,2,24,640]{3,2,1,0:T(8,128)(2,1)S(1)}, u32[]{:S(2)}, u32[]{:S(2)}) collective-permute-start(bf16[2,2,24,640]{3,2,1,0:T(8,128)(2,1)S(1)} %shard_map.78), channel_id=1, source_target_pairs={{256,0},{384,128},{0,256},{128,384},{257,1},{385,129},{1,257},{129... | collective-permute-start | bytes 368648 | tf_op jit(solution)/shard_map/ppermute | solution.py:367
  49.8 7.7 %collective-permute-start.6 = (bf16[2,2,24,640]{3,2,1,0:T(8,128)(2,1)S(1)}, bf16[2,2,24,640]{3,2,1,0:T(8,128)(2,1)S(1)}, u32[]{:S(2)}, u32[]{:S(2)}) collective-permute-start(bf16[2,2,24,640]{3,2,1,0:T(8,128)(2,1)S(1)} %shard_map.78), channel_id=1, source_target_pairs={{384,0},{0,128},{128,256},{256,384},{385,1},{1,129},{129,257},{257... | collective-permute-start | bytes 368648 | tf_op jit(solution)/shard_map/ppermute | solution.py:367
  52.0 6.4 %collective-permute-start.5 = (bf16[2,2,24,640]{3,2,1,0:T(8,128)(2,1)S(1)}, bf16[2,2,24,640]{3,2,1,0:T(8,128)(2,1)S(1)}, u32[]{:S(2)}, u32[]{:S(2)}) collective-permute-start(bf16[2,2,24,640]{3,2,1,0:T(8,128)(2,1)S(1)} %shard_map.78), channel_id=1, source_target_pairs={{128,0},{256,128},{384,256},{0,384},{129,1},{257,129},{385,257},{1... | collective-permute-start | bytes 368648 | tf_op jit(solution)/shard_map/ppermute | solution.py:367
  58.4 7.0 %collective-permute-start.8 = (bf16[8,2,24,640]{3,2,1,0:T(8,128)(2,1)S(1)}, bf16[8,2,24,640]{3,2,1,0:T(8,128)(2,1)S(1)}, u32[]{:S(2)}, u32[]{:S(2)}) collective-permute-start(bf16[8,2,24,640]{3,2,1,0:T(8,128)(2,1)S(1)} %pad_maximum_fusion.refs_4_), channel_id=1, source_target_pairs={{0,32},{32,0},{1,33},{33,1},{2,34},{34,2},{3,35},{35,3},{4,36},{36... | collective-permute-start | bytes 1474568 | tf_op jit(solution)/shard_map/ppermute | solution.py:368
  61.9 3.5 %collective-permute-start.3 = (f32[8,128]{1,0:T(8,128)S(1)}, f32[8,128]{1,0:T(8,128)S(1)}, u32[]{:S(2)}, u32[]{:S(2)}) collective-permute-start(f32[8,128]{1,0:T(8,128)S(1)} %shard_map.77.refs_0_), channel_id=1, source_target_pairs={{0,32},{32,0},{1,33},{33,1},{2,34},{34,2},{3,35},{35,3},{4,36},{36... | collective-permute-start | bytes 12296 | tf_op jit(solution)/shard_map/ppermute | solution.py:371
  65.4 40.7 %copy-start = (bf16[640,1920]{1,0:T(8,128)(2,1)S(1)}, bf16[640,1920]{1,0:T(8,128)(2,1)}, u32[]{:S(2)}) copy-start(bf16[640,1920]{1,0:T(8,128)(2,1)} %w_ref.4) | copy-start | bytes 7372804
  133.7 24.7 %copy-start.1 = (bf16[640,640]{1,0:T(8,128)(2,1)S(1)}, bf16[640,640]{1,0:T(8,128)(2,1)}, u32[]{:S(2)}) copy-start(bf16[640,640]{1,0:T(8,128)(2,1)} %w_ref.5) | copy-start | bytes 2457604

commit v10 on v9

--- a/solution.py
+++ b/solution.py
@@ -13,6 +13,7 @@
 ROWS_HERE = 4
 TOKENS = ROWS_HERE * WIDTH
 LAST = TOKENS - WIDTH
+ALL = TOKENS + 2 * WIDTH
 PARTICLES = 16
 HALF = PARTICLES // 2
 ROW_DEVS = 32
@@ -202,8 +203,15 @@
     return 2 * jnp.where(dx == 2, 3, jnp.where(dx == 3, 2, dx)) + dz
 
 
+def merge_kernel(place_ref, x_ref, edge_ref, out_ref):
+    for j in range(HALF):
+        at = beside(place_ref, j)
+        parts = [x_ref[j], edge_ref[at, 0], edge_ref[at, 1]]
+        out_ref[j] = jnp.concatenate([v.astype(F32) for v in parts], axis=0).astype(BF16)
+
+
 def conv_kernel(place_ref, anc_ref, scale_ref, shift_ref, w_ref, *refs):
-    totals, slabs, edges, (out_ref, done_ref) = refs[:2], refs[2:4], refs[4:6], refs[6:]
+    totals, slabs, (out_ref, done_ref) = refs[:2], refs[2:4], refs[4:]
     mean, inverse = mean_and_inverse(jnp.concatenate([ref[...] for ref in totals], axis=0))
     gain = inverse * (1.0 + scale_ref[...])
     bias = shift_ref[...] - mean * gain
@@ -215,23 +223,21 @@
     for step in range(PARTICLES // each):
         active, raw = [], []
         for n in range(step * each, (step + 1) * each):
-            which, j = n // HALF, n % HALF
-            x = slabs[which][j]
-            raw.append(x)
-            act = lambda v: silu(v.astype(F32) * gain[n : n + 1] + bias[n : n + 1])
-            at = beside(place_ref, j)
-            above, below = act(edges[which][at, 0]), act(edges[which][at, 1])
-            active += [jnp.where(top, 0.0, above), act(x), jnp.where(bottom, 0.0, below)]
-        active = jnp.concatenate(active, axis=0).astype(BF16)
+            x = slabs[n // HALF][n % HALF]
+            raw.append(x[:TOKENS])
+            active.append(silu(x.astype(F32) * gain[n : n + 1] + bias[n : n + 1]).astype(BF16))
+        active = jnp.concatenate(active, axis=0)
         raw = jnp.concatenate(raw, axis=0)
         taps = lax.dot_general(active, weights, NT, preferred_element_type=F32)
         field = lax.dot_general(raw, chosen, NT, preferred_element_type=F32)
         for k in range(each):
-            at = k * (TOKENS + 2 * WIDTH)
-            full = field[k * TOKENS : (k + 1) * TOKENS]
-            for a in range(3):
-                rows = slice(at + a * WIDTH, at + a * WIDTH + TOKENS)
-                full = full + taps[rows, a * LANES : (a + 1) * LANES]
+            here = taps[k * ALL : (k + 1) * ALL]
+            t0, t1, t2 = (here[:, a * LANES : (a + 1) * LANES] for a in range(3))
+            above = jnp.where(top, 0.0, t0[TOKENS : TOKENS + WIDTH])
+            below = jnp.where(bottom, 0.0, t2[TOKENS + WIDTH :])
+            full = field[k * TOKENS : (k + 1) * TOKENS] + t1[:TOKENS]
+            full = full + jnp.concatenate([above, t0[:LAST]], axis=0)
+            full = full + jnp.concatenate([t2[WIDTH:TOKENS], below], axis=0)
             done_ref[step * each + k] = packed(across(full)).astype(BF16)
     for p in range(PARTICLES):
         out_ref[p] = done_ref[spot(place_ref, anc_ref[p])]
@@ -348,7 +354,6 @@
         spread_kernel, [shaped(HALF, TOKENS, CHANS), row, row], [VMEM], 10**5, 10**6
     )(slab)
     here = exchange(copies, CHIPS)
-    slabs = [here, lax.ppermute(here, "core", swap)]
     above = lax.ppermute(last, ROWS, [(i, i + 1) for i in range(ROW_DEVS - 1)])
     below = lax.ppermute(first, ROWS, [(i + 1, i) for i in range(ROW_DEVS - 1)])
     mine = jnp.stack([above, below])
@@ -365,7 +370,10 @@
     )
     turns = [[((i + d) % 4, i) for i in range(4)] for d in STEPS[1:]]
     edges = jnp.concatenate([pair] + [lax.ppermute(pair, "x", turn) for turn in turns])
-    edges = [edges, lax.ppermute(edges, "core", swap)]
+    merged = call(merge_kernel, shaped(HALF, ALL, CHANS), [SMEM, VMEM, VMEM], 10**6, 10**6)(
+        place, here, edges
+    )
+    slabs = [merged, lax.ppermute(merged, "core", swap)]
     picked = exchange(picked, ROWS)
     totals = call(total_kernel, shaped(HALF, LANES, dtype=F32), [VMEM], 10**5, 10**5)(picked)
     totals = [totals, lax.ppermute(totals, "core", swap)]
@@ -373,7 +381,7 @@
         weights_kernel,
         shaped(3 * LANES, CHANS),
         [VMEM],
-        10**6,
+        3 * 10**10,
         10**6,
         scratch=(
             pltpu.VMEM((SLICE, 9 * CHANS + 2 * LANES), F32),
@@ -383,12 +391,12 @@
     pieces = call(
         conv_kernel,
         shaped(PARTICLES, 32, LANES),
-        [SMEM, SMEM] + [VMEM] * 9,
+        [SMEM, SMEM] + [VMEM] * 7,
         2 * 10**9,
         4 * 10**6,
         vmem=20,
         scratch=(pltpu.VMEM((PARTICLES, 32, LANES), BF16),),
-    )(place, ancestors, ada_scale[None], ada_shift[None], weights, *totals, *slabs, *edges)
+    )(place, ancestors, ada_scale[None], ada_shift[None], weights, *totals, *slabs)
     pieces = exchange(pieces, PART)
 
     resid, sums = call(

time: 162 us -> 162 us (level)
    pallas_call x2 -> x3, Pallas kernels: 5.83 us -> 7.46 us  [the longest x1 5.27 us: per_device(): call(conv_kernel, shaped(PARTICLES, 32, LANES), [SMEM, SMEM] + [VMEM] * 7...]
    ppermute x2 -> x1, starting transfers between devices: 8.57 us -> 7.08 us  [per_device(): slabs = [merged, lax.ppermute(merged, 'core', swap)]]
  transfers between devices with their start and end apart: 11 -> 10, of which waited for: 4 -> 4; matrix products, arithmetic and copies ran while one was open for 0% -> 0% of each run, Pallas kernels for 2% -> 2%
where the time goes in v10:
time: 162 us; the launch traced here: 159 us
  blocking collectives  81.9 us (51%)
  starting transfers between devices  50.1 us (31%)
  Pallas kernels  18.3 us (11%)
  waiting for transfers between devices  7.2 us (4%)
    all_to_all x4, blocking collectives, exchange(): return lax.all_to_all(values, axes, split_axis=0, concat_axis=0, tiled=True)  81.9 us
    all_to_all x2, starting transfers between devices, exchange(): return lax.all_to_all(values, axes, split_axis=0, concat_axis=0, tiled=True)  21.6 us
    ppermute x3, starting transfers between devices, per_device(): lax.ppermute(pair, 'x', turn)  10.9 us
    ppermute x1, starting transfers between devices, per_device(): slabs = [merged, lax.ppermute(merged, 'core', swap)]  7.08 us
    pallas_call x1, Pallas kernels, per_device(): call(conv_kernel, shaped(PARTICLES, 32, LANES), [SMEM, SMEM] + [VMEM] * 7...  5.27 us
    pallas_call x1, Pallas kernels, per_device(): call(attend_kernel, shaped(ROW_DEVS, 16, LANES), [VMEM], 2 * 10 ** 9, 2 *...  4.23 us
    ppermute x1, waiting for transfers between devices, per_device(): below = lax.ppermute(first, ROWS, [(i + 1, i) for i in range(ROW_DEVS - 1)])  3.62 us
    ppermute x1, starting transfers between devices, per_device(): opposite = lax.ppermute(mine, 'z_lo', swap)  3.37 us
  transfers between devices with their start and end apart: 10, of which 4 were waited for; matrix products, arithmetic and copies ran while one was open for 0% of the time, Pallas kernels for 2%

profile of v10, /device:TPU:1, one launch (start us, length us, event | category | flops | bytes accessed | tf_op | source)
XLA Modules:
  0.0 158.9 jit_solution(12957863738488948234)
XLA Ops:
  0.0 0.0 copy-start.2
  0.0 0.0 copy-start.3
  0.0 0.9 copy-done.3
  0.9 1.0 shard_map.73
  2.0 6.7 %all-to-all-start = ((bf16[8,96,640]{2,1,0:T(8,128)(2,1)}), bf16[8,96,640]{2,1,0:T(8,128)(2,1)S(1)}, u32[]{:S(2)}, u32[]{:S(2)}) async-start(bf16[8,96,640]{2,1,0:T(8,128)(2,1)} %get-tuple-element.10), calls=%async_computation | async-start | bytes 1966080 | tf_op jit(solution)/shard_map/all_to_all | solution.py:341
  8.6 3.2 %collective-permute-start = (bf16[24,640]{1,0:T(8,128)(2,1)S(1)}, bf16[24,640]{1,0:T(8,128)(2,1)S(1)}, u32[]{:S(2)}, u32[]{:S(2)}) collective-permute-start(bf16[24,640]{1,0:T(8,128)(2,1)S(1)} %get-tuple-element.11), channel_id=1, source_target_pairs={{0,1},{1,2},{2,3},{3,4},{4,5},{5,6},{6,7},{7,8},{8,9},{9,10},{10,1... | collective-permute-start | bytes 92168 | tf_op jit(solution)/shard_map/ppermute | solution.py:357
  11.8 1.3 collective-permute-start.1
  13.1 0.0 collective-permute-done
  13.1 3.6 %collective-permute-done.1 = bf16[24,640]{1,0:T(8,128)(2,1)S(1)} collective-permute-done((bf16[24,640]{1,0:T(8,128)(2,1)S(1)}, bf16[24,640]{1,0:T(8,128)(2,1)S(1)}, u32[]{:S(2)}, u32[]{:S(2)}) %collective-permute-start.1) | collective-permute-done | bytes 30752 | tf_op jit(solution)/shard_map/ppermute | solution.py:358
  16.8 3.4 %collective-permute-start.2 = (bf16[2,24,640]{2,1,0:T(8,128)(2,1)S(1)}, bf16[2,24,640]{2,1,0:T(8,128)(2,1)S(1)}, u32[]{:S(2)}, u32[]{:S(2)}) collective-permute-start(bf16[2,24,640]{2,1,0:T(8,128)(2,1)S(1)} %pad_maximum_fusion.1.mine_ref), channel_id=1, source_target_pairs={{0,64},{64,0},{1,65},{65,1},{2,66},{66,2},{3,67},{67,3},{4,68},{68... | collective-permute-start | bytes 184328 | tf_op jit(solution)/shard_map/ppermute | solution.py:360
  20.2 0.1 stack.32.place_ref
  20.3 0.0 copy-done.2
  20.3 0.8 shard_map.74.part_ref
  21.1 0.0 copy-start.5
  21.1 1.4 collective-permute-done.2._.opposite_ref
  22.5 0.0 all-to-all-done.x_ref
  22.5 1.7 %shard_map.75._ = bf16[32,72,128]{2,1,0:T(8,128)(2,1)} custom-call(bf16[8,96,640]{2,1,0:T(8,128)(2,1)S(1)} %all-to-all-done.x_ref, f32[72,128]{1,0:T(8,128)S(1)} %shard_map.74.part_ref, bf16[2,24,640]{2,1,0:T(8,128)(2,1)S(1)} %collective-permute-done.2._.opposite_ref), custom_call_target="tpu_custom_call" | custom-call | flops 10000000 | bytes 1000000 | tf_op jit(solution)/shard_map/pallas_call | solution.py:365
  24.3 14.9 %all-to-all-start.1 = ((bf16[32,72,128]{2,1,0:T(8,128)(2,1)}), bf16[32,72,128]{2,1,0:T(8,128)(2,1)S(1)}, u32[]{:S(2)}, u32[]{:S(2)}) async-start(bf16[32,72,128]{2,1,0:T(8,128)(2,1)} %shard_map.75._), calls=%async_computation.1 | async-start | bytes 1179648 | tf_op jit(solution)/shard_map/all_to_all | solution.py:341
  39.2 4.4 %collective-permute-start.6 = (bf16[2,2,24,640]{3,2,1,0:T(8,128)(2,1)S(1)}, bf16[2,2,24,640]{3,2,1,0:T(8,128)(2,1)S(1)}, u32[]{:S(2)}, u32[]{:S(2)}) collective-permute-start(bf16[2,2,24,640]{3,2,1,0:T(8,128)(2,1)S(1)} %shard_map.78), channel_id=1, source_target_pairs={{256,0},{384,128},{0,256},{128,384},{257,1},{385,129},{1,257},{129... | collective-permute-start | bytes 368648 | tf_op jit(solution)/shard_map/ppermute | solution.py:372
  43.7 2.2 %collective-permute-start.5 = (bf16[2,2,24,640]{3,2,1,0:T(8,128)(2,1)S(1)}, bf16[2,2,24,640]{3,2,1,0:T(8,128)(2,1)S(1)}, u32[]{:S(2)}, u32[]{:S(2)}) collective-permute-start(bf16[2,2,24,640]{3,2,1,0:T(8,128)(2,1)S(1)} %shard_map.78), channel_id=1, source_target_pairs={{384,0},{0,128},{128,256},{256,384},{385,1},{1,129},{129,257},{257... | collective-permute-start | bytes 368648 | tf_op jit(solution)/shard_map/ppermute | solution.py:372
  45.9 4.3 %collective-permute-start.4 = (bf16[2,2,24,640]{3,2,1,0:T(8,128)(2,1)S(1)}, bf16[2,2,24,640]{3,2,1,0:T(8,128)(2,1)S(1)}, u32[]{:S(2)}, u32[]{:S(2)}) collective-permute-start(bf16[2,2,24,640]{3,2,1,0:T(8,128)(2,1)S(1)} %shard_map.78), channel_id=1, source_target_pairs={{128,0},{256,128},{384,256},{0,384},{129,1},{257,129},{385,257},{1... | collective-permute-start | bytes 368648 | tf_op jit(solution)/shard_map/ppermute | solution.py:372
  50.2 0.0 copy-done.5
  50.2 0.0 copy-done.6
  50.2 0.0 collective-permute-done.6
  50.2 1.7 %collective-permute-done.5 = bf16[2,2,24,640]{3,2,1,0:T(8,128)(2,1)S(1)} collective-permute-done((bf16[2,2,24,640]{3,2,1,0:T(8,128)(2,1)S(1)}, bf16[2,2,24,640]{3,2,1,0:T(8,128)(2,1)S(1)}, u32[]{:S(2)}, u32[]{:S(2)}) %collective-permute-start.5) | collective-permute-done | bytes 122912 | tf_op jit(solution)/shard_map/ppermute | solution.py:372
  52.0 0.4 collective-permute-done.4
  52.4 0.1 pad_maximum_fusion.edge_ref
  52.4 0.7 shard_map.79.refs_2_
  53.1 7.1 %collective-permute-start.7 = (bf16[8,144,640]{2,1,0:T(8,128)(2,1)S(1)}, bf16[8,144,640]{2,1,0:T(8,128)(2,1)}, u32[]{:S(2)}, u32[]{:S(2)}) collective-permute-start(bf16[8,144,640]{2,1,0:T(8,128)(2,1)S(1)} %shard_map.79.refs_2_), channel_id=1, source_target_pairs={{0,32},{32,0},{1,33},{33,1},{2,34},{34,2},{3,35},{35,3},{4,36},{36... | collective-permute-start | bytes 4423688 | tf_op jit(solution)/shard_map/ppermute | solution.py:376
  60.2 0.0 all-to-all-done.1.x_ref
  60.2 0.1 shard_map.77.refs_0_
  60.3 2.7 %collective-permute-start.3 = (f32[8,128]{1,0:T(8,128)S(1)}, f32[8,128]{1,0:T(8,128)S(1)}, u32[]{:S(2)}, u32[]{:S(2)}) collective-permute-start(f32[8,128]{1,0:T(8,128)S(1)} %shard_map.77.refs_0_), channel_id=1, source_target_pairs={{0,32},{32,0},{1,33},{33,1},{2,34},{34,2},{3,35},{35,3},{4,36},{36... | collective-permute-start | bytes 12296 | tf_op jit(solution)/shard_map/ppermute | solution.py:379
  63.0 1.5 shard_map.76.w_ref
  64.6 0.0 collective-permute-done.3.refs_1_
  64.6 0.0 collective-permute-done.7.refs_3_
  64.6 0.0 copy-done.4
  64.6 0.0 copy-start
  64.6 5.3 %shard_map.80 = bf16[16,32,128]{2,1,0:T(8,128)(2,1)S(1)} custom-call(s32[5]{0:T(128)S(1)} %stack.32.place_ref, s32[16]{0:T(128)S(1)} %copy-done.4, f32[1,640]{1,0:T(1,128)S(1)} %broadcast_in_dim.6.scale_ref, f32[1,640]{1,0:T(1,128)S(1)} %broadcast_in_dim.7.shift_ref, bf16[384,640]{1,0:T(8,128)(2,1)S(1)} %shard_map.76.w_ref, f32[8,128]{1,0:T(8,128)S(1)} %shard_map.77.refs_0_, ...), custom_call_target="tpu_custom_call" | custom-call | flops 2000000000 | bytes 4000000 | tf_op jit(solution)/shard_map/pallas_call | solution.py:391
  69.9 11.6 %all_to_all.30.x_ref = bf16[16,32,128]{2,1,0:T(8,128)(2,1)S(1)} all-to-all(bf16[16,32,128]{2,1,0:T(8,128)(2,1)S(1)} %shard_map.80), channel_id=1, replica_groups=mesh['x'=4,'z_lo'=2,'core'=2,'z_hi'=4,'y'=8] {'x','z_lo','core'}, dimensions={0} | all-to-all | bytes 262144 | tf_op jit(solution)/shard_map/all_to_all | solution.py:341
  81.5 0.7 shard_map.81
  82.2 23.3 %all_to_all.31.totals_ref = f32[32,8,128]{2,1,0:T(8,128)S(1)} all-to-all(f32[32,8,128]{2,1,0:T(8,128)S(1)} %get-tuple-element.13), channel_id=1, replica_groups=mesh['x'=4,'z_lo'=2,'core'=2,'z_hi'=4,'y'=8] {'z_hi','y'}, dimensions={0} | all-to-all | bytes 262144 | tf_op jit(solution)/shard_map/all_to_all | solution.py:341
  105.5 0.0 copy-done
  105.5 1.1 shard_map.82
  106.7 26.5 %all_to_all.32.x_ref = bf16[32,112,128]{2,1,0:T(8,128)(2,1)S(1)} all-to-all(bf16[32,112,128]{2,1,0:T(8,128)(2,1)S(1)} %shard_map.82), channel_id=1, replica_groups=mesh['x'=4,'z_lo'=2,'core'=2,'z_hi'=4,'y'=8] {'z_hi','y'}, dimensions={0} | all-to-all | bytes 1835008 | tf_op jit(solution)/shard_map/all_to_all | solution.py:341
  133.1 4.2 %shard_map.83 = bf16[32,16,128]{2,1,0:T(8,128)(2,1)S(1)} custom-call(bf16[32,112,128]{2,1,0:T(8,128)(2,1)S(1)} %all_to_all.32.x_ref), custom_call_target="tpu_custom_call" | custom-call | flops 2000000000 | bytes 2000000 | tf_op jit(solution)/shard_map/pallas_call | solution.py:421
  137.4 20.5 %all_to_all.33.x_ref = bf16[32,16,128]{2,1,0:T(8,128)(2,1)S(1)} all-to-all(bf16[32,16,128]{2,1,0:T(8,128)(2,1)S(1)} %shard_map.83), channel_id=1, replica_groups=mesh['x'=4,'z_lo'=2,'core'=2,'z_hi'=4,'y'=8] {'z_hi','y'}, dimensions={0} | all-to-all | bytes 262144 | tf_op jit(solution)/shard_map/all_to_all | solution.py:341
  157.9 0.0 copy-done.1
  157.9 1.0 shard_map.84
  (7 shorter events, 0.0 us)
Async XLA Ops:
  0.0 20.3 %copy-start.2 = (bf16[180,640]{1,0:T(8,128)(2,1)S(1)}, bf16[180,640]{1,0:T(8,128)(2,1)}, u32[]{:S(2)}) copy-start(bf16[180,640]{1,0:T(8,128)(2,1)} %w_ref.3) | copy-start | bytes 691204
  0.0 0.9 copy-start.3
  2.0 20.6 %all-to-all-start = ((bf16[8,96,640]{2,1,0:T(8,128)(2,1)}), bf16[8,96,640]{2,1,0:T(8,128)(2,1)S(1)}, u32[]{:S(2)}, u32[]{:S(2)}) async-start(bf16[8,96,640]{2,1,0:T(8,128)(2,1)} %get-tuple-element.10), calls=%async_computation | async-start | bytes 1966080 | tf_op jit(solution)/shard_map/all_to_all | solution.py:341
  8.6 4.5 %collective-permute-start = (bf16[24,640]{1,0:T(8,128)(2,1)S(1)}, bf16[24,640]{1,0:T(8,128)(2,1)S(1)}, u32[]{:S(2)}, u32[]{:S(2)}) collective-permute-start(bf16[24,640]{1,0:T(8,128)(2,1)S(1)} %get-tuple-element.11), channel_id=1, source_target_pairs={{0,1},{1,2},{2,3},{3,4},{4,5},{5,6},{6,7},{7,8},{8,9},{9,10},{10,1... | collective-permute-start | bytes 92168 | tf_op jit(solution)/shard_map/ppermute | solution.py:357
  11.8 4.9 %collective-permute-start.1 = (bf16[24,640]{1,0:T(8,128)(2,1)S(1)}, bf16[24,640]{1,0:T(8,128)(2,1)S(1)}, u32[]{:S(2)}, u32[]{:S(2)}) collective-permute-start(bf16[24,640]{1,0:T(8,128)(2,1)S(1)} %get-tuple-element.12), channel_id=1, source_target_pairs={{1,0},{2,1},{3,2},{4,3},{5,4},{6,5},{7,6},{8,7},{9,8},{10,9},{11,1... | collective-permute-start | bytes 92168 | tf_op jit(solution)/shard_map/ppermute | solution.py:358
  16.8 5.8 %collective-permute-start.2 = (bf16[2,24,640]{2,1,0:T(8,128)(2,1)S(1)}, bf16[2,24,640]{2,1,0:T(8,128)(2,1)S(1)}, u32[]{:S(2)}, u32[]{:S(2)}) collective-permute-start(bf16[2,24,640]{2,1,0:T(8,128)(2,1)S(1)} %pad_maximum_fusion.1.mine_ref), channel_id=1, source_target_pairs={{0,64},{64,0},{1,65},{65,1},{2,66},{66,2},{3,67},{67,3},{4,68},{68... | collective-permute-start | bytes 184328 | tf_op jit(solution)/shard_map/ppermute | solution.py:360
  21.1 29.1 %copy-start.5 = (f32[640]{0:T(1024)S(1)}, f32[640]{0:T(1024)}, u32[]{:S(2)}) copy-start(f32[640]{0:T(1024)} %param.8) | copy-start | bytes 7684
  21.1 29.1 %copy-start.6 = (f32[640]{0:T(1024)S(1)}, f32[640]{0:T(1024)}, u32[]{:S(2)}) copy-start(f32[640]{0:T(1024)} %param.9) | copy-start | bytes 7684
  24.3 35.9 %all-to-all-start.1 = ((bf16[32,72,128]{2,1,0:T(8,128)(2,1)}), bf16[32,72,128]{2,1,0:T(8,128)(2,1)S(1)}, u32[]{:S(2)}, u32[]{:S(2)}) async-start(bf16[32,72,128]{2,1,0:T(8,128)(2,1)} %shard_map.75._), calls=%async_computation.1 | async-start | bytes 1179648 | tf_op jit(solution)/shard_map/all_to_all | solution.py:341
  39.2 11.0 %collective-permute-start.6 = (bf16[2,2,24,640]{3,2,1,0:T(8,128)(2,1)S(1)}, bf16[2,2,24,640]{3,2,1,0:T(8,128)(2,1)S(1)}, u32[]{:S(2)}, u32[]{:S(2)}) collective-permute-start(bf16[2,2,24,640]{3,2,1,0:T(8,128)(2,1)S(1)} %shard_map.78), channel_id=1, source_target_pairs={{256,0},{384,128},{0,256},{128,384},{257,1},{385,129},{1,257},{129... | collective-permute-start | bytes 368648 | tf_op jit(solution)/shard_map/ppermute | solution.py:372
  43.7 8.3 %collective-permute-start.5 = (bf16[2,2,24,640]{3,2,1,0:T(8,128)(2,1)S(1)}, bf16[2,2,24,640]{3,2,1,0:T(8,128)(2,1)S(1)}, u32[]{:S(2)}, u32[]{:S(2)}) collective-permute-start(bf16[2,2,24,640]{3,2,1,0:T(8,128)(2,1)S(1)} %shard_map.78), channel_id=1, source_target_pairs={{384,0},{0,128},{128,256},{256,384},{385,1},{1,129},{129,257},{257... | collective-permute-start | bytes 368648 | tf_op jit(solution)/shard_map/ppermute | solution.py:372
  45.9 6.5 %collective-permute-start.4 = (bf16[2,2,24,640]{3,2,1,0:T(8,128)(2,1)S(1)}, bf16[2,2,24,640]{3,2,1,0:T(8,128)(2,1)S(1)}, u32[]{:S(2)}, u32[]{:S(2)}) collective-permute-start(bf16[2,2,24,640]{3,2,1,0:T(8,128)(2,1)S(1)} %shard_map.78), channel_id=1, source_target_pairs={{128,0},{256,128},{384,256},{0,384},{129,1},{257,129},{385,257},{1... | collective-permute-start | bytes 368648 | tf_op jit(solution)/shard_map/ppermute | solution.py:372
  53.1 11.5 %collective-permute-start.7 = (bf16[8,144,640]{2,1,0:T(8,128)(2,1)S(1)}, bf16[8,144,640]{2,1,0:T(8,128)(2,1)}, u32[]{:S(2)}, u32[]{:S(2)}) collective-permute-start(bf16[8,144,640]{2,1,0:T(8,128)(2,1)S(1)} %shard_map.79.refs_2_), channel_id=1, source_target_pairs={{0,32},{32,0},{1,33},{33,1},{2,34},{34,2},{3,35},{35,3},{4,36},{36... | collective-permute-start | bytes 4423688 | tf_op jit(solution)/shard_map/ppermute | solution.py:376
  60.3 4.3 %copy-start.4 = (s32[16]{0:T(128)S(1)}, s32[16]{0:T(128)}, u32[]{:S(2)}) copy-start(s32[16]{0:T(128)} %anc_ref.1) | copy-start | bytes 196
  60.3 4.2 %collective-permute-start.3 = (f32[8,128]{1,0:T(8,128)S(1)}, f32[8,128]{1,0:T(8,128)S(1)}, u32[]{:S(2)}, u32[]{:S(2)}) collective-permute-start(f32[8,128]{1,0:T(8,128)S(1)} %shard_map.77.refs_0_), channel_id=1, source_target_pairs={{0,32},{32,0},{1,33},{33,1},{2,34},{34,2},{3,35},{35,3},{4,36},{36... | collective-permute-start | bytes 12296 | tf_op jit(solution)/shard_map/ppermute | solution.py:379
  64.6 40.9 %copy-start = (bf16[640,1920]{1,0:T(8,128)(2,1)S(1)}, bf16[640,1920]{1,0:T(8,128)(2,1)}, u32[]{:S(2)}) copy-start(bf16[640,1920]{1,0:T(8,128)(2,1)} %w_ref.4) | copy-start | bytes 7372804
  133.1 24.7 %copy-start.1 = (bf16[640,640]{1,0:T(8,128)(2,1)S(1)}, bf16[640,640]{1,0:T(8,128)(2,1)}, u32[]{:S(2)}) copy-start(bf16[640,640]{1,0:T(8,128)(2,1)} %w_ref.5) | copy-start | bytes 2457604

commit v11 on v10

--- a/solution.py
+++ b/solution.py
@@ -211,7 +211,10 @@
 
 
 def conv_kernel(place_ref, anc_ref, scale_ref, shift_ref, w_ref, *refs):
-    totals, slabs, (out_ref, done_ref) = refs[:2], refs[2:4], refs[4:]
+    totals, own_ref, far_ref, (out_ref, done_ref, other_ref, sem) = refs[:2], *refs[2:4], refs[4:]
+    copy = pltpu.make_async_copy(far_ref, other_ref, sem)
+    copy.start()
+    slabs = (own_ref, other_ref)
     mean, inverse = mean_and_inverse(jnp.concatenate([ref[...] for ref in totals], axis=0))
     gain = inverse * (1.0 + scale_ref[...])
     bias = shift_ref[...] - mean * gain
@@ -221,6 +224,8 @@
     top, bottom = place_ref[4] == 0, place_ref[4] == ROW_DEVS - 1
     each = 2
     for step in range(PARTICLES // each):
+        if step * each == HALF:
+            copy.wait()
         active, raw = [], []
         for n in range(step * each, (step + 1) * each):
             x = slabs[n // HALF][n % HALF]
@@ -261,11 +266,12 @@
             wide_ref[32 * t : 32 * (t + 1), n * LANES : (n + 1) * LANES] = value
     wide = wide_ref[...]
     resid_ref[...] = wide.astype(BF16)
-    out_ref[...] = jnp.broadcast_to(group_rows([wide])[None], out_ref.shape)
+    out_ref[...] = jnp.broadcast_to(group_rows([wide])[None, :1], out_ref.shape)
 
 
 def project_kernel(totals_ref, resid_ref, w_ref, out_ref, both_ref):
-    mean, inverse = mean_and_inverse(jnp.sum(totals_ref[...], axis=0))
+    totals = jnp.broadcast_to(jnp.sum(totals_ref[...], axis=0), (8, LANES))
+    mean, inverse = mean_and_inverse(totals)
     normed = ((resid_ref[...].astype(F32) - mean[:1]) * inverse[:1]).astype(BF16)
     both_ref[...] = jnp.dot(normed, w_ref[...], preferred_element_type=F32)
     low = iota((TOKENS, LANES), 1) < 64
@@ -391,17 +397,21 @@
     pieces = call(
         conv_kernel,
         shaped(PARTICLES, 32, LANES),
-        [SMEM, SMEM] + [VMEM] * 7,
+        [SMEM, SMEM] + [VMEM] * 6 + [ANY],
         2 * 10**9,
         4 * 10**6,
         vmem=20,
-        scratch=(pltpu.VMEM((PARTICLES, 32, LANES), BF16),),
+        scratch=(
+            pltpu.VMEM((PARTICLES, 32, LANES), BF16),
+            pltpu.VMEM((HALF, ALL, CHANS), BF16),
+            pltpu.SemaphoreType.DMA,
+        ),
     )(place, ancestors, ada_scale[None], ada_shift[None], weights, *totals, *slabs)
     pieces = exchange(pieces, PART)
 
     resid, sums = call(
         gather_kernel,
-        [shaped(TOKENS, CHANS), shaped(ROW_DEVS, 8, LANES, dtype=F32)],
+        [shaped(TOKENS, CHANS), shaped(ROW_DEVS, 1, LANES, dtype=F32)],
         [VMEM],
         10**6,
         10**6,

time: 162 us -> 161 us (level)
  no operation moved by 1% of the time
where the time goes in v11:
time: 161 us; the launch traced here: 158 us
  blocking collectives  81 us (50%)
  starting transfers between devices  50.1 us (31%)
  Pallas kernels  18.6 us (12%)
  waiting for transfers between devices  7.2 us (4%)
    all_to_all x4, blocking collectives, exchange(): return lax.all_to_all(values, axes, split_axis=0, concat_axis=0, tiled=True)  81 us
    all_to_all x2, starting transfers between devices, exchange(): return lax.all_to_all(values, axes, split_axis=0, concat_axis=0, tiled=True)  21.6 us
    ppermute x3, starting transfers between devices, per_device(): lax.ppermute(pair, 'x', turn)  10.9 us
    ppermute x1, starting transfers between devices, per_device(): slabs = [merged, lax.ppermute(merged, 'core', swap)]  7.08 us
    pallas_call x1, Pallas kernels, per_device(): call(conv_kernel, shaped(PARTICLES, 32, LANES), [SMEM, SMEM] + [VMEM] * 6...  5.59 us
    pallas_call x1, Pallas kernels, per_device(): call(attend_kernel, shaped(ROW_DEVS, 16, LANES), [VMEM], 2 * 10 ** 9, 2 *...  4.22 us
    ppermute x1, waiting for transfers between devices, per_device(): below = lax.ppermute(first, ROWS, [(i + 1, i) for i in range(ROW_DEVS - 1)])  3.62 us
    ppermute x1, starting transfers between devices, per_device(): opposite = lax.ppermute(mine, 'z_lo', swap)  3.37 us
  transfers between devices with their start and end apart: 10, of which 4 were waited for; matrix products, arithmetic and copies ran while one was open for 0% of the time, Pallas kernels for 2%

profile of v11, /device:TPU:1, one launch (start us, length us, event | category | flops | bytes accessed | tf_op | source)
XLA Modules:
  0.0 158.3 jit_solution(2286712975015897736)
XLA Ops:
  0.0 0.0 copy-start.2
  0.0 0.0 copy-start.3
  0.0 0.9 copy-done.3
  0.9 1.0 shard_map.73
  2.0 6.7 %all-to-all-start = ((bf16[8,96,640]{2,1,0:T(8,128)(2,1)}), bf16[8,96,640]{2,1,0:T(8,128)(2,1)S(1)}, u32[]{:S(2)}, u32[]{:S(2)}) async-start(bf16[8,96,640]{2,1,0:T(8,128)(2,1)} %get-tuple-element.10), calls=%async_computation | async-start | bytes 1966080 | tf_op jit(solution)/shard_map/all_to_all | solution.py:347
  8.6 3.2 %collective-permute-start = (bf16[24,640]{1,0:T(8,128)(2,1)S(1)}, bf16[24,640]{1,0:T(8,128)(2,1)S(1)}, u32[]{:S(2)}, u32[]{:S(2)}) collective-permute-start(bf16[24,640]{1,0:T(8,128)(2,1)S(1)} %get-tuple-element.11), channel_id=1, source_target_pairs={{0,1},{1,2},{2,3},{3,4},{4,5},{5,6},{6,7},{7,8},{8,9},{9,10},{10,1... | collective-permute-start | bytes 92168 | tf_op jit(solution)/shard_map/ppermute | solution.py:363
  11.8 1.3 collective-permute-start.1
  13.1 0.0 collective-permute-done
  13.1 3.6 %collective-permute-done.1 = bf16[24,640]{1,0:T(8,128)(2,1)S(1)} collective-permute-done((bf16[24,640]{1,0:T(8,128)(2,1)S(1)}, bf16[24,640]{1,0:T(8,128)(2,1)S(1)}, u32[]{:S(2)}, u32[]{:S(2)}) %collective-permute-start.1) | collective-permute-done | bytes 30752 | tf_op jit(solution)/shard_map/ppermute | solution.py:364
  16.8 3.4 %collective-permute-start.2 = (bf16[2,24,640]{2,1,0:T(8,128)(2,1)S(1)}, bf16[2,24,640]{2,1,0:T(8,128)(2,1)S(1)}, u32[]{:S(2)}, u32[]{:S(2)}) collective-permute-start(bf16[2,24,640]{2,1,0:T(8,128)(2,1)S(1)} %pad_maximum_fusion.1.mine_ref), channel_id=1, source_target_pairs={{0,64},{64,0},{1,65},{65,1},{2,66},{66,2},{3,67},{67,3},{4,68},{68... | collective-permute-start | bytes 184328 | tf_op jit(solution)/shard_map/ppermute | solution.py:366
  20.2 0.1 stack.32.place_ref
  20.3 0.0 copy-done.2
  20.3 0.8 shard_map.74.part_ref
  21.1 0.0 copy-start.5
  21.1 1.4 collective-permute-done.2._.opposite_ref
  22.5 0.0 all-to-all-done.x_ref
  22.5 1.7 %shard_map.75._ = bf16[32,72,128]{2,1,0:T(8,128)(2,1)} custom-call(bf16[8,96,640]{2,1,0:T(8,128)(2,1)S(1)} %all-to-all-done.x_ref, f32[72,128]{1,0:T(8,128)S(1)} %shard_map.74.part_ref, bf16[2,24,640]{2,1,0:T(8,128)(2,1)S(1)} %collective-permute-done.2._.opposite_ref), custom_call_target="tpu_custom_call" | custom-call | flops 10000000 | bytes 1000000 | tf_op jit(solution)/shard_map/pallas_call | solution.py:371
  24.3 14.9 %all-to-all-start.1 = ((bf16[32,72,128]{2,1,0:T(8,128)(2,1)}), bf16[32,72,128]{2,1,0:T(8,128)(2,1)S(1)}, u32[]{:S(2)}, u32[]{:S(2)}) async-start(bf16[32,72,128]{2,1,0:T(8,128)(2,1)} %shard_map.75._), calls=%async_computation.1 | async-start | bytes 1179648 | tf_op jit(solution)/shard_map/all_to_all | solution.py:347
  39.2 4.4 %collective-permute-start.6 = (bf16[2,2,24,640]{3,2,1,0:T(8,128)(2,1)S(1)}, bf16[2,2,24,640]{3,2,1,0:T(8,128)(2,1)S(1)}, u32[]{:S(2)}, u32[]{:S(2)}) collective-permute-start(bf16[2,2,24,640]{3,2,1,0:T(8,128)(2,1)S(1)} %shard_map.78), channel_id=1, source_target_pairs={{256,0},{384,128},{0,256},{128,384},{257,1},{385,129},{1,257},{129... | collective-permute-start | bytes 368648 | tf_op jit(solution)/shard_map/ppermute | solution.py:378
  43.7 2.2 %collective-permute-start.5 = (bf16[2,2,24,640]{3,2,1,0:T(8,128)(2,1)S(1)}, bf16[2,2,24,640]{3,2,1,0:T(8,128)(2,1)S(1)}, u32[]{:S(2)}, u32[]{:S(2)}) collective-permute-start(bf16[2,2,24,640]{3,2,1,0:T(8,128)(2,1)S(1)} %shard_map.78), channel_id=1, source_target_pairs={{384,0},{0,128},{128,256},{256,384},{385,1},{1,129},{129,257},{257... | collective-permute-start | bytes 368648 | tf_op jit(solution)/shard_map/ppermute | solution.py:378
  45.9 4.3 %collective-permute-start.4 = (bf16[2,2,24,640]{3,2,1,0:T(8,128)(2,1)S(1)}, bf16[2,2,24,640]{3,2,1,0:T(8,128)(2,1)S(1)}, u32[]{:S(2)}, u32[]{:S(2)}) collective-permute-start(bf16[2,2,24,640]{3,2,1,0:T(8,128)(2,1)S(1)} %shard_map.78), channel_id=1, source_target_pairs={{128,0},{256,128},{384,256},{0,384},{129,1},{257,129},{385,257},{1... | collective-permute-start | bytes 368648 | tf_op jit(solution)/shard_map/ppermute | solution.py:378
  50.2 0.0 copy-done.5
  50.2 0.0 copy-done.6
  50.2 0.0 collective-permute-done.6
  50.2 1.7 %collective-permute-done.5 = bf16[2,2,24,640]{3,2,1,0:T(8,128)(2,1)S(1)} collective-permute-done((bf16[2,2,24,640]{3,2,1,0:T(8,128)(2,1)S(1)}, bf16[2,2,24,640]{3,2,1,0:T(8,128)(2,1)S(1)}, u32[]{:S(2)}, u32[]{:S(2)}) %collective-permute-start.5) | collective-permute-done | bytes 122912 | tf_op jit(solution)/shard_map/ppermute | solution.py:378
  52.0 0.4 collective-permute-done.4
  52.4 0.1 pad_maximum_fusion.edge_ref
  52.4 0.7 shard_map.79.refs_2_
  53.1 7.1 %collective-permute-start.7 = (bf16[8,144,640]{2,1,0:T(8,128)(2,1)S(1)}, bf16[8,144,640]{2,1,0:T(8,128)(2,1)}, u32[]{:S(2)}, u32[]{:S(2)}) collective-permute-start(bf16[8,144,640]{2,1,0:T(8,128)(2,1)S(1)} %shard_map.79.refs_2_), channel_id=1, source_target_pairs={{0,32},{32,0},{1,33},{33,1},{2,34},{34,2},{3,35},{35,3},{4,36},{36... | collective-permute-start | bytes 4423688 | tf_op jit(solution)/shard_map/ppermute | solution.py:382
  60.2 0.0 all-to-all-done.1.x_ref
  60.2 0.1 shard_map.77.refs_0_
  60.3 2.7 %collective-permute-start.3 = (f32[8,128]{1,0:T(8,128)S(1)}, f32[8,128]{1,0:T(8,128)S(1)}, u32[]{:S(2)}, u32[]{:S(2)}) collective-permute-start(f32[8,128]{1,0:T(8,128)S(1)} %shard_map.77.refs_0_), channel_id=1, source_target_pairs={{0,32},{32,0},{1,33},{33,1},{2,34},{34,2},{3,35},{35,3},{4,36},{36... | collective-permute-start | bytes 12296 | tf_op jit(solution)/shard_map/ppermute | solution.py:385
  63.0 1.5 shard_map.76.w_ref
  64.6 0.0 collective-permute-done.3.refs_1_
  64.6 0.0 collective-permute-done.7.refs_3_
  64.6 0.0 copy-done.4
  64.6 0.0 copy-start
  64.6 5.6 %shard_map.80 = bf16[16,32,128]{2,1,0:T(8,128)(2,1)S(1)} custom-call(s32[5]{0:T(128)S(1)} %stack.32.place_ref, s32[16]{0:T(128)S(1)} %copy-done.4, f32[1,640]{1,0:T(1,128)S(1)} %broadcast_in_dim.6.scale_ref, f32[1,640]{1,0:T(1,128)S(1)} %broadcast_in_dim.7.shift_ref, bf16[384,640]{1,0:T(8,128)(2,1)S(1)} %shard_map.76.w_ref, f32[8,128]{1,0:T(8,128)S(1)} %shard_map.77.refs_0_, ...), custom_call_target="tpu_custom_call" | custom-call | flops 2000000000 | bytes 4000000 | tf_op jit(solution)/shard_map/pallas_call | solution.py:397
  70.2 11.6 %all_to_all.30.x_ref = bf16[16,32,128]{2,1,0:T(8,128)(2,1)S(1)} all-to-all(bf16[16,32,128]{2,1,0:T(8,128)(2,1)S(1)} %shard_map.80), channel_id=1, replica_groups=mesh['x'=4,'z_lo'=2,'core'=2,'z_hi'=4,'y'=8] {'x','z_lo','core'}, dimensions={0} | all-to-all | bytes 262144 | tf_op jit(solution)/shard_map/all_to_all | solution.py:347
  81.8 0.7 shard_map.81
  82.5 22.7 %all_to_all.31.totals_ref = f32[32,1,128]{2,1,0:T(1,128)S(1)} all-to-all(f32[32,1,128]{2,1,0:T(1,128)S(1)} %get-tuple-element.13), channel_id=1, replica_groups=mesh['x'=4,'z_lo'=2,'core'=2,'z_hi'=4,'y'=8] {'z_hi','y'}, dimensions={0} | all-to-all | bytes 32768 | tf_op jit(solution)/shard_map/all_to_all | solution.py:347
  105.3 0.0 copy-done
  105.3 1.1 shard_map.82
  106.4 26.5 %all_to_all.32.x_ref = bf16[32,112,128]{2,1,0:T(8,128)(2,1)S(1)} all-to-all(bf16[32,112,128]{2,1,0:T(8,128)(2,1)S(1)} %shard_map.82), channel_id=1, replica_groups=mesh['x'=4,'z_lo'=2,'core'=2,'z_hi'=4,'y'=8] {'z_hi','y'}, dimensions={0} | all-to-all | bytes 1835008 | tf_op jit(solution)/shard_map/all_to_all | solution.py:347
  132.9 4.2 %shard_map.83 = bf16[32,16,128]{2,1,0:T(8,128)(2,1)S(1)} custom-call(bf16[32,112,128]{2,1,0:T(8,128)(2,1)S(1)} %all_to_all.32.x_ref), custom_call_target="tpu_custom_call" | custom-call | flops 2000000000 | bytes 2000000 | tf_op jit(solution)/shard_map/pallas_call | solution.py:431
  137.1 20.2 %all_to_all.33.x_ref = bf16[32,16,128]{2,1,0:T(8,128)(2,1)S(1)} all-to-all(bf16[32,16,128]{2,1,0:T(8,128)(2,1)S(1)} %shard_map.83), channel_id=1, replica_groups=mesh['x'=4,'z_lo'=2,'core'=2,'z_hi'=4,'y'=8] {'z_hi','y'}, dimensions={0} | all-to-all | bytes 262144 | tf_op jit(solution)/shard_map/all_to_all | solution.py:347
  157.3 0.0 copy-done.1
  157.3 1.0 shard_map.84
  (7 shorter events, 0.0 us)
Async XLA Ops:
  0.0 20.3 %copy-start.2 = (bf16[180,640]{1,0:T(8,128)(2,1)S(1)}, bf16[180,640]{1,0:T(8,128)(2,1)}, u32[]{:S(2)}) copy-start(bf16[180,640]{1,0:T(8,128)(2,1)} %w_ref.3) | copy-start | bytes 691204
  0.0 0.9 copy-start.3
  2.0 20.6 %all-to-all-start = ((bf16[8,96,640]{2,1,0:T(8,128)(2,1)}), bf16[8,96,640]{2,1,0:T(8,128)(2,1)S(1)}, u32[]{:S(2)}, u32[]{:S(2)}) async-start(bf16[8,96,640]{2,1,0:T(8,128)(2,1)} %get-tuple-element.10), calls=%async_computation | async-start | bytes 1966080 | tf_op jit(solution)/shard_map/all_to_all | solution.py:347
  8.6 4.5 %collective-permute-start = (bf16[24,640]{1,0:T(8,128)(2,1)S(1)}, bf16[24,640]{1,0:T(8,128)(2,1)S(1)}, u32[]{:S(2)}, u32[]{:S(2)}) collective-permute-start(bf16[24,640]{1,0:T(8,128)(2,1)S(1)} %get-tuple-element.11), channel_id=1, source_target_pairs={{0,1},{1,2},{2,3},{3,4},{4,5},{5,6},{6,7},{7,8},{8,9},{9,10},{10,1... | collective-permute-start | bytes 92168 | tf_op jit(solution)/shard_map/ppermute | solution.py:363
  11.8 4.9 %collective-permute-start.1 = (bf16[24,640]{1,0:T(8,128)(2,1)S(1)}, bf16[24,640]{1,0:T(8,128)(2,1)S(1)}, u32[]{:S(2)}, u32[]{:S(2)}) collective-permute-start(bf16[24,640]{1,0:T(8,128)(2,1)S(1)} %get-tuple-element.12), channel_id=1, source_target_pairs={{1,0},{2,1},{3,2},{4,3},{5,4},{6,5},{7,6},{8,7},{9,8},{10,9},{11,1... | collective-permute-start | bytes 92168 | tf_op jit(solution)/shard_map/ppermute | solution.py:364
  16.8 5.8 %collective-permute-start.2 = (bf16[2,24,640]{2,1,0:T(8,128)(2,1)S(1)}, bf16[2,24,640]{2,1,0:T(8,128)(2,1)S(1)}, u32[]{:S(2)}, u32[]{:S(2)}) collective-permute-start(bf16[2,24,640]{2,1,0:T(8,128)(2,1)S(1)} %pad_maximum_fusion.1.mine_ref), channel_id=1, source_target_pairs={{0,64},{64,0},{1,65},{65,1},{2,66},{66,2},{3,67},{67,3},{4,68},{68... | collective-permute-start | bytes 184328 | tf_op jit(solution)/shard_map/ppermute | solution.py:366
  21.1 29.1 %copy-start.5 = (f32[640]{0:T(1024)S(1)}, f32[640]{0:T(1024)}, u32[]{:S(2)}) copy-start(f32[640]{0:T(1024)} %param.8) | copy-start | bytes 7684
  21.1 29.1 %copy-start.6 = (f32[640]{0:T(1024)S(1)}, f32[640]{0:T(1024)}, u32[]{:S(2)}) copy-start(f32[640]{0:T(1024)} %param.9) | copy-start | bytes 7684
  24.3 35.9 %all-to-all-start.1 = ((bf16[32,72,128]{2,1,0:T(8,128)(2,1)}), bf16[32,72,128]{2,1,0:T(8,128)(2,1)S(1)}, u32[]{:S(2)}, u32[]{:S(2)}) async-start(bf16[32,72,128]{2,1,0:T(8,128)(2,1)} %shard_map.75._), calls=%async_computation.1 | async-start | bytes 1179648 | tf_op jit(solution)/shard_map/all_to_all | solution.py:347
  39.2 11.0 %collective-permute-start.6 = (bf16[2,2,24,640]{3,2,1,0:T(8,128)(2,1)S(1)}, bf16[2,2,24,640]{3,2,1,0:T(8,128)(2,1)S(1)}, u32[]{:S(2)}, u32[]{:S(2)}) collective-permute-start(bf16[2,2,24,640]{3,2,1,0:T(8,128)(2,1)S(1)} %shard_map.78), channel_id=1, source_target_pairs={{256,0},{384,128},{0,256},{128,384},{257,1},{385,129},{1,257},{129... | collective-permute-start | bytes 368648 | tf_op jit(solution)/shard_map/ppermute | solution.py:378
  43.7 8.3 %collective-permute-start.5 = (bf16[2,2,24,640]{3,2,1,0:T(8,128)(2,1)S(1)}, bf16[2,2,24,640]{3,2,1,0:T(8,128)(2,1)S(1)}, u32[]{:S(2)}, u32[]{:S(2)}) collective-permute-start(bf16[2,2,24,640]{3,2,1,0:T(8,128)(2,1)S(1)} %shard_map.78), channel_id=1, source_target_pairs={{384,0},{0,128},{128,256},{256,384},{385,1},{1,129},{129,257},{257... | collective-permute-start | bytes 368648 | tf_op jit(solution)/shard_map/ppermute | solution.py:378
  45.9 6.5 %collective-permute-start.4 = (bf16[2,2,24,640]{3,2,1,0:T(8,128)(2,1)S(1)}, bf16[2,2,24,640]{3,2,1,0:T(8,128)(2,1)S(1)}, u32[]{:S(2)}, u32[]{:S(2)}) collective-permute-start(bf16[2,2,24,640]{3,2,1,0:T(8,128)(2,1)S(1)} %shard_map.78), channel_id=1, source_target_pairs={{128,0},{256,128},{384,256},{0,384},{129,1},{257,129},{385,257},{1... | collective-permute-start | bytes 368648 | tf_op jit(solution)/shard_map/ppermute | solution.py:378
  53.1 11.5 %collective-permute-start.7 = (bf16[8,144,640]{2,1,0:T(8,128)(2,1)S(1)}, bf16[8,144,640]{2,1,0:T(8,128)(2,1)}, u32[]{:S(2)}, u32[]{:S(2)}) collective-permute-start(bf16[8,144,640]{2,1,0:T(8,128)(2,1)S(1)} %shard_map.79.refs_2_), channel_id=1, source_target_pairs={{0,32},{32,0},{1,33},{33,1},{2,34},{34,2},{3,35},{35,3},{4,36},{36... | collective-permute-start | bytes 4423688 | tf_op jit(solution)/shard_map/ppermute | solution.py:382
  60.3 4.3 %copy-start.4 = (s32[16]{0:T(128)S(1)}, s32[16]{0:T(128)}, u32[]{:S(2)}) copy-start(s32[16]{0:T(128)} %anc_ref.1) | copy-start | bytes 196
  60.3 4.2 %collective-permute-start.3 = (f32[8,128]{1,0:T(8,128)S(1)}, f32[8,128]{1,0:T(8,128)S(1)}, u32[]{:S(2)}, u32[]{:S(2)}) collective-permute-start(f32[8,128]{1,0:T(8,128)S(1)} %shard_map.77.refs_0_), channel_id=1, source_target_pairs={{0,32},{32,0},{1,33},{33,1},{2,34},{34,2},{3,35},{35,3},{4,36},{36... | collective-permute-start | bytes 12296 | tf_op jit(solution)/shard_map/ppermute | solution.py:385
  64.6 40.7 %copy-start = (bf16[640,1920]{1,0:T(8,128)(2,1)S(1)}, bf16[640,1920]{1,0:T(8,128)(2,1)}, u32[]{:S(2)}) copy-start(bf16[640,1920]{1,0:T(8,128)(2,1)} %w_ref.4) | copy-start | bytes 7372804
  132.9 24.4 %copy-start.1 = (bf16[640,640]{1,0:T(8,128)(2,1)S(1)}, bf16[640,640]{1,0:T(8,128)(2,1)}, u32[]{:S(2)}) copy-start(bf16[640,640]{1,0:T(8,128)(2,1)} %w_ref.5) | copy-start | bytes 2457604

commit v12 on v10

--- a/solution.py
+++ b/solution.py
@@ -261,11 +261,12 @@
             wide_ref[32 * t : 32 * (t + 1), n * LANES : (n + 1) * LANES] = value
     wide = wide_ref[...]
     resid_ref[...] = wide.astype(BF16)
-    out_ref[...] = jnp.broadcast_to(group_rows([wide])[None], out_ref.shape)
+    out_ref[...] = jnp.broadcast_to(group_rows([wide])[None, :1], out_ref.shape)
 
 
 def project_kernel(totals_ref, resid_ref, w_ref, out_ref, both_ref):
-    mean, inverse = mean_and_inverse(jnp.sum(totals_ref[...], axis=0))
+    totals = jnp.broadcast_to(jnp.sum(totals_ref[...], axis=0), (8, LANES))
+    mean, inverse = mean_and_inverse(totals)
     normed = ((resid_ref[...].astype(F32) - mean[:1]) * inverse[:1]).astype(BF16)
     both_ref[...] = jnp.dot(normed, w_ref[...], preferred_element_type=F32)
     low = iota((TOKENS, LANES), 1) < 64
@@ -401,7 +402,7 @@
 
     resid, sums = call(
         gather_kernel,
-        [shaped(TOKENS, CHANS), shaped(ROW_DEVS, 8, LANES, dtype=F32)],
+        [shaped(TOKENS, CHANS), shaped(ROW_DEVS, 1, LANES, dtype=F32)],
         [VMEM],
         10**6,
         10**6,

time: 162 us -> 160 us (0.988)
  no operation moved by 1% of the time
where the time goes in v12:
time: 160 us; the launch traced here: 158 us
  blocking collectives  80.8 us (50%)
  starting transfers between devices  50.1 us (31%)
  Pallas kernels  18.3 us (11%)
  waiting for transfers between devices  7.2 us (4%)
    all_to_all x4, blocking collectives, exchange(): return lax.all_to_all(values, axes, split_axis=0, concat_axis=0, tiled=True)  80.8 us
    all_to_all x2, starting transfers between devices, exchange(): return lax.all_to_all(values, axes, split_axis=0, concat_axis=0, tiled=True)  21.6 us
    ppermute x3, starting transfers between devices, per_device(): lax.ppermute(pair, 'x', turn)  10.9 us
    ppermute x1, starting transfers between devices, per_device(): slabs = [merged, lax.ppermute(merged, 'core', swap)]  7.08 us
    pallas_call x1, Pallas kernels, per_device(): call(conv_kernel, shaped(PARTICLES, 32, LANES), [SMEM, SMEM] + [VMEM] * 7...  5.27 us
    pallas_call x1, Pallas kernels, per_device(): call(attend_kernel, shaped(ROW_DEVS, 16, LANES), [VMEM], 2 * 10 ** 9, 2 *...  4.23 us
    ppermute x1, waiting for transfers between devices, per_device(): below = lax.ppermute(first, ROWS, [(i + 1, i) for i in range(ROW_DEVS - 1)])  3.62 us
    ppermute x1, starting transfers between devices, per_device(): opposite = lax.ppermute(mine, 'z_lo', swap)  3.37 us
  transfers between devices with their start and end apart: 10, of which 4 were waited for; matrix products, arithmetic and copies ran while one was open for 0% of the time, Pallas kernels for 2%

profile of v12, /device:TPU:1, one launch (start us, length us, event | category | flops | bytes accessed | tf_op | source)
XLA Modules:
  0.0 157.8 jit_solution(15929265387509234053)
XLA Ops:
  0.0 0.0 copy-start.2
  0.0 0.0 copy-start.3
  0.0 0.9 copy-done.3
  0.9 1.0 shard_map.73
  2.0 6.7 %all-to-all-start = ((bf16[8,96,640]{2,1,0:T(8,128)(2,1)}), bf16[8,96,640]{2,1,0:T(8,128)(2,1)S(1)}, u32[]{:S(2)}, u32[]{:S(2)}) async-start(bf16[8,96,640]{2,1,0:T(8,128)(2,1)} %get-tuple-element.10), calls=%async_computation | async-start | bytes 1966080 | tf_op jit(solution)/shard_map/all_to_all | solution.py:342
  8.6 3.2 %collective-permute-start = (bf16[24,640]{1,0:T(8,128)(2,1)S(1)}, bf16[24,640]{1,0:T(8,128)(2,1)S(1)}, u32[]{:S(2)}, u32[]{:S(2)}) collective-permute-start(bf16[24,640]{1,0:T(8,128)(2,1)S(1)} %get-tuple-element.11), channel_id=1, source_target_pairs={{0,1},{1,2},{2,3},{3,4},{4,5},{5,6},{6,7},{7,8},{8,9},{9,10},{10,1... | collective-permute-start | bytes 92168 | tf_op jit(solution)/shard_map/ppermute | solution.py:358
  11.8 1.3 collective-permute-start.1
  13.1 0.0 collective-permute-done
  13.1 3.6 %collective-permute-done.1 = bf16[24,640]{1,0:T(8,128)(2,1)S(1)} collective-permute-done((bf16[24,640]{1,0:T(8,128)(2,1)S(1)}, bf16[24,640]{1,0:T(8,128)(2,1)S(1)}, u32[]{:S(2)}, u32[]{:S(2)}) %collective-permute-start.1) | collective-permute-done | bytes 30752 | tf_op jit(solution)/shard_map/ppermute | solution.py:359
  16.8 3.4 %collective-permute-start.2 = (bf16[2,24,640]{2,1,0:T(8,128)(2,1)S(1)}, bf16[2,24,640]{2,1,0:T(8,128)(2,1)S(1)}, u32[]{:S(2)}, u32[]{:S(2)}) collective-permute-start(bf16[2,24,640]{2,1,0:T(8,128)(2,1)S(1)} %pad_maximum_fusion.1.mine_ref), channel_id=1, source_target_pairs={{0,64},{64,0},{1,65},{65,1},{2,66},{66,2},{3,67},{67,3},{4,68},{68... | collective-permute-start | bytes 184328 | tf_op jit(solution)/shard_map/ppermute | solution.py:361
  20.2 0.1 stack.32.place_ref
  20.3 0.0 copy-done.2
  20.3 0.8 shard_map.74.part_ref
  21.1 0.0 copy-start.6
  21.1 1.4 collective-permute-done.2._.opposite_ref
  22.5 0.0 all-to-all-done.x_ref
  22.5 1.7 %shard_map.75._ = bf16[32,72,128]{2,1,0:T(8,128)(2,1)} custom-call(bf16[8,96,640]{2,1,0:T(8,128)(2,1)S(1)} %all-to-all-done.x_ref, f32[72,128]{1,0:T(8,128)S(1)} %shard_map.74.part_ref, bf16[2,24,640]{2,1,0:T(8,128)(2,1)S(1)} %collective-permute-done.2._.opposite_ref), custom_call_target="tpu_custom_call" | custom-call | flops 10000000 | bytes 1000000 | tf_op jit(solution)/shard_map/pallas_call | solution.py:366
  24.3 14.9 %all-to-all-start.1 = ((bf16[32,72,128]{2,1,0:T(8,128)(2,1)}), bf16[32,72,128]{2,1,0:T(8,128)(2,1)S(1)}, u32[]{:S(2)}, u32[]{:S(2)}) async-start(bf16[32,72,128]{2,1,0:T(8,128)(2,1)} %shard_map.75._), calls=%async_computation.1 | async-start | bytes 1179648 | tf_op jit(solution)/shard_map/all_to_all | solution.py:342
  39.2 4.4 %collective-permute-start.6 = (bf16[2,2,24,640]{3,2,1,0:T(8,128)(2,1)S(1)}, bf16[2,2,24,640]{3,2,1,0:T(8,128)(2,1)S(1)}, u32[]{:S(2)}, u32[]{:S(2)}) collective-permute-start(bf16[2,2,24,640]{3,2,1,0:T(8,128)(2,1)S(1)} %shard_map.78), channel_id=1, source_target_pairs={{256,0},{384,128},{0,256},{128,384},{257,1},{385,129},{1,257},{129... | collective-permute-start | bytes 368648 | tf_op jit(solution)/shard_map/ppermute | solution.py:373
  43.7 2.2 %collective-permute-start.5 = (bf16[2,2,24,640]{3,2,1,0:T(8,128)(2,1)S(1)}, bf16[2,2,24,640]{3,2,1,0:T(8,128)(2,1)S(1)}, u32[]{:S(2)}, u32[]{:S(2)}) collective-permute-start(bf16[2,2,24,640]{3,2,1,0:T(8,128)(2,1)S(1)} %shard_map.78), channel_id=1, source_target_pairs={{384,0},{0,128},{128,256},{256,384},{385,1},{1,129},{129,257},{257... | collective-permute-start | bytes 368648 | tf_op jit(solution)/shard_map/ppermute | solution.py:373
  45.9 4.3 %collective-permute-start.4 = (bf16[2,2,24,640]{3,2,1,0:T(8,128)(2,1)S(1)}, bf16[2,2,24,640]{3,2,1,0:T(8,128)(2,1)S(1)}, u32[]{:S(2)}, u32[]{:S(2)}) collective-permute-start(bf16[2,2,24,640]{3,2,1,0:T(8,128)(2,1)S(1)} %shard_map.78), channel_id=1, source_target_pairs={{128,0},{256,128},{384,256},{0,384},{129,1},{257,129},{385,257},{1... | collective-permute-start | bytes 368648 | tf_op jit(solution)/shard_map/ppermute | solution.py:373
  50.2 0.0 copy-done.5
  50.2 0.0 copy-done.6
  50.2 0.0 collective-permute-done.6
  50.2 1.7 %collective-permute-done.5 = bf16[2,2,24,640]{3,2,1,0:T(8,128)(2,1)S(1)} collective-permute-done((bf16[2,2,24,640]{3,2,1,0:T(8,128)(2,1)S(1)}, bf16[2,2,24,640]{3,2,1,0:T(8,128)(2,1)S(1)}, u32[]{:S(2)}, u32[]{:S(2)}) %collective-permute-start.5) | collective-permute-done | bytes 122912 | tf_op jit(solution)/shard_map/ppermute | solution.py:373
  52.0 0.4 collective-permute-done.4
  52.4 0.1 pad_maximum_fusion.edge_ref
  52.4 0.7 shard_map.79.refs_2_
  53.1 7.1 %collective-permute-start.7 = (bf16[8,144,640]{2,1,0:T(8,128)(2,1)S(1)}, bf16[8,144,640]{2,1,0:T(8,128)(2,1)}, u32[]{:S(2)}, u32[]{:S(2)}) collective-permute-start(bf16[8,144,640]{2,1,0:T(8,128)(2,1)S(1)} %shard_map.79.refs_2_), channel_id=1, source_target_pairs={{0,32},{32,0},{1,33},{33,1},{2,34},{34,2},{3,35},{35,3},{4,36},{36... | collective-permute-start | bytes 4423688 | tf_op jit(solution)/shard_map/ppermute | solution.py:377
  60.2 0.0 all-to-all-done.1.x_ref
  60.2 0.1 shard_map.77.refs_0_
  60.3 2.7 %collective-permute-start.3 = (f32[8,128]{1,0:T(8,128)S(1)}, f32[8,128]{1,0:T(8,128)S(1)}, u32[]{:S(2)}, u32[]{:S(2)}) collective-permute-start(f32[8,128]{1,0:T(8,128)S(1)} %shard_map.77.refs_0_), channel_id=1, source_target_pairs={{0,32},{32,0},{1,33},{33,1},{2,34},{34,2},{3,35},{35,3},{4,36},{36... | collective-permute-start | bytes 12296 | tf_op jit(solution)/shard_map/ppermute | solution.py:380
  63.0 1.5 shard_map.76.w_ref
  64.6 0.0 collective-permute-done.3.refs_1_
  64.6 0.0 collective-permute-done.7.refs_3_
  64.6 0.0 copy-done.4
  64.6 0.0 copy-start
  64.6 5.3 %shard_map.80 = bf16[16,32,128]{2,1,0:T(8,128)(2,1)S(1)} custom-call(s32[5]{0:T(128)S(1)} %stack.32.place_ref, s32[16]{0:T(128)S(1)} %copy-done.4, f32[1,640]{1,0:T(1,128)S(1)} %broadcast_in_dim.6.scale_ref, f32[1,640]{1,0:T(1,128)S(1)} %broadcast_in_dim.7.shift_ref, bf16[384,640]{1,0:T(8,128)(2,1)S(1)} %shard_map.76.w_ref, f32[8,128]{1,0:T(8,128)S(1)} %shard_map.77.refs_0_, ...), custom_call_target="tpu_custom_call" | custom-call | flops 2000000000 | bytes 4000000 | tf_op jit(solution)/shard_map/pallas_call | solution.py:392
  69.9 11.6 %all_to_all.30.x_ref = bf16[16,32,128]{2,1,0:T(8,128)(2,1)S(1)} all-to-all(bf16[16,32,128]{2,1,0:T(8,128)(2,1)S(1)} %shard_map.80), channel_id=1, replica_groups=mesh['x'=4,'z_lo'=2,'core'=2,'z_hi'=4,'y'=8] {'x','z_lo','core'}, dimensions={0} | all-to-all | bytes 262144 | tf_op jit(solution)/shard_map/all_to_all | solution.py:342
  81.5 0.7 shard_map.81
  82.2 22.8 %all_to_all.31.totals_ref = f32[32,1,128]{2,1,0:T(1,128)S(1)} all-to-all(f32[32,1,128]{2,1,0:T(1,128)S(1)} %get-tuple-element.13), channel_id=1, replica_groups=mesh['x'=4,'z_lo'=2,'core'=2,'z_hi'=4,'y'=8] {'z_hi','y'}, dimensions={0} | all-to-all | bytes 32768 | tf_op jit(solution)/shard_map/all_to_all | solution.py:342
  105.0 0.0 copy-done
  105.0 1.1 shard_map.82
  106.1 26.5 %all_to_all.32.x_ref = bf16[32,112,128]{2,1,0:T(8,128)(2,1)S(1)} all-to-all(bf16[32,112,128]{2,1,0:T(8,128)(2,1)S(1)} %shard_map.82), channel_id=1, replica_groups=mesh['x'=4,'z_lo'=2,'core'=2,'z_hi'=4,'y'=8] {'z_hi','y'}, dimensions={0} | all-to-all | bytes 1835008 | tf_op jit(solution)/shard_map/all_to_all | solution.py:342
  132.6 4.2 %shard_map.83 = bf16[32,16,128]{2,1,0:T(8,128)(2,1)S(1)} custom-call(bf16[32,112,128]{2,1,0:T(8,128)(2,1)S(1)} %all_to_all.32.x_ref), custom_call_target="tpu_custom_call" | custom-call | flops 2000000000 | bytes 2000000 | tf_op jit(solution)/shard_map/pallas_call | solution.py:422
  136.8 20.0 %all_to_all.33.x_ref = bf16[32,16,128]{2,1,0:T(8,128)(2,1)S(1)} all-to-all(bf16[32,16,128]{2,1,0:T(8,128)(2,1)S(1)} %shard_map.83), channel_id=1, replica_groups=mesh['x'=4,'z_lo'=2,'core'=2,'z_hi'=4,'y'=8] {'z_hi','y'}, dimensions={0} | all-to-all | bytes 262144 | tf_op jit(solution)/shard_map/all_to_all | solution.py:342
  156.8 0.0 copy-done.1
  156.8 1.0 shard_map.84
  (7 shorter events, 0.0 us)
Async XLA Ops:
  0.0 20.3 %copy-start.2 = (bf16[180,640]{1,0:T(8,128)(2,1)S(1)}, bf16[180,640]{1,0:T(8,128)(2,1)}, u32[]{:S(2)}) copy-start(bf16[180,640]{1,0:T(8,128)(2,1)} %w_ref.3) | copy-start | bytes 691204
  0.0 0.9 copy-start.3
  2.0 20.6 %all-to-all-start = ((bf16[8,96,640]{2,1,0:T(8,128)(2,1)}), bf16[8,96,640]{2,1,0:T(8,128)(2,1)S(1)}, u32[]{:S(2)}, u32[]{:S(2)}) async-start(bf16[8,96,640]{2,1,0:T(8,128)(2,1)} %get-tuple-element.10), calls=%async_computation | async-start | bytes 1966080 | tf_op jit(solution)/shard_map/all_to_all | solution.py:342
  8.6 4.5 %collective-permute-start = (bf16[24,640]{1,0:T(8,128)(2,1)S(1)}, bf16[24,640]{1,0:T(8,128)(2,1)S(1)}, u32[]{:S(2)}, u32[]{:S(2)}) collective-permute-start(bf16[24,640]{1,0:T(8,128)(2,1)S(1)} %get-tuple-element.11), channel_id=1, source_target_pairs={{0,1},{1,2},{2,3},{3,4},{4,5},{5,6},{6,7},{7,8},{8,9},{9,10},{10,1... | collective-permute-start | bytes 92168 | tf_op jit(solution)/shard_map/ppermute | solution.py:358
  11.8 4.9 %collective-permute-start.1 = (bf16[24,640]{1,0:T(8,128)(2,1)S(1)}, bf16[24,640]{1,0:T(8,128)(2,1)S(1)}, u32[]{:S(2)}, u32[]{:S(2)}) collective-permute-start(bf16[24,640]{1,0:T(8,128)(2,1)S(1)} %get-tuple-element.12), channel_id=1, source_target_pairs={{1,0},{2,1},{3,2},{4,3},{5,4},{6,5},{7,6},{8,7},{9,8},{10,9},{11,1... | collective-permute-start | bytes 92168 | tf_op jit(solution)/shard_map/ppermute | solution.py:359
  16.8 5.8 %collective-permute-start.2 = (bf16[2,24,640]{2,1,0:T(8,128)(2,1)S(1)}, bf16[2,24,640]{2,1,0:T(8,128)(2,1)S(1)}, u32[]{:S(2)}, u32[]{:S(2)}) collective-permute-start(bf16[2,24,640]{2,1,0:T(8,128)(2,1)S(1)} %pad_maximum_fusion.1.mine_ref), channel_id=1, source_target_pairs={{0,64},{64,0},{1,65},{65,1},{2,66},{66,2},{3,67},{67,3},{4,68},{68... | collective-permute-start | bytes 184328 | tf_op jit(solution)/shard_map/ppermute | solution.py:361
  21.1 29.1 %copy-start.5 = (f32[640]{0:T(1024)S(1)}, f32[640]{0:T(1024)}, u32[]{:S(2)}) copy-start(f32[640]{0:T(1024)} %param.8) | copy-start | bytes 7684
  21.1 29.1 %copy-start.6 = (f32[640]{0:T(1024)S(1)}, f32[640]{0:T(1024)}, u32[]{:S(2)}) copy-start(f32[640]{0:T(1024)} %param.9) | copy-start | bytes 7684
  24.3 35.9 %all-to-all-start.1 = ((bf16[32,72,128]{2,1,0:T(8,128)(2,1)}), bf16[32,72,128]{2,1,0:T(8,128)(2,1)S(1)}, u32[]{:S(2)}, u32[]{:S(2)}) async-start(bf16[32,72,128]{2,1,0:T(8,128)(2,1)} %shard_map.75._), calls=%async_computation.1 | async-start | bytes 1179648 | tf_op jit(solution)/shard_map/all_to_all | solution.py:342
  39.2 11.0 %collective-permute-start.6 = (bf16[2,2,24,640]{3,2,1,0:T(8,128)(2,1)S(1)}, bf16[2,2,24,640]{3,2,1,0:T(8,128)(2,1)S(1)}, u32[]{:S(2)}, u32[]{:S(2)}) collective-permute-start(bf16[2,2,24,640]{3,2,1,0:T(8,128)(2,1)S(1)} %shard_map.78), channel_id=1, source_target_pairs={{256,0},{384,128},{0,256},{128,384},{257,1},{385,129},{1,257},{129... | collective-permute-start | bytes 368648 | tf_op jit(solution)/shard_map/ppermute | solution.py:373
  43.7 8.3 %collective-permute-start.5 = (bf16[2,2,24,640]{3,2,1,0:T(8,128)(2,1)S(1)}, bf16[2,2,24,640]{3,2,1,0:T(8,128)(2,1)S(1)}, u32[]{:S(2)}, u32[]{:S(2)}) collective-permute-start(bf16[2,2,24,640]{3,2,1,0:T(8,128)(2,1)S(1)} %shard_map.78), channel_id=1, source_target_pairs={{384,0},{0,128},{128,256},{256,384},{385,1},{1,129},{129,257},{257... | collective-permute-start | bytes 368648 | tf_op jit(solution)/shard_map/ppermute | solution.py:373
  45.9 6.5 %collective-permute-start.4 = (bf16[2,2,24,640]{3,2,1,0:T(8,128)(2,1)S(1)}, bf16[2,2,24,640]{3,2,1,0:T(8,128)(2,1)S(1)}, u32[]{:S(2)}, u32[]{:S(2)}) collective-permute-start(bf16[2,2,24,640]{3,2,1,0:T(8,128)(2,1)S(1)} %shard_map.78), channel_id=1, source_target_pairs={{128,0},{256,128},{384,256},{0,384},{129,1},{257,129},{385,257},{1... | collective-permute-start | bytes 368648 | tf_op jit(solution)/shard_map/ppermute | solution.py:373
  53.1 11.5 %collective-permute-start.7 = (bf16[8,144,640]{2,1,0:T(8,128)(2,1)S(1)}, bf16[8,144,640]{2,1,0:T(8,128)(2,1)}, u32[]{:S(2)}, u32[]{:S(2)}) collective-permute-start(bf16[8,144,640]{2,1,0:T(8,128)(2,1)S(1)} %shard_map.79.refs_2_), channel_id=1, source_target_pairs={{0,32},{32,0},{1,33},{33,1},{2,34},{34,2},{3,35},{35,3},{4,36},{36... | collective-permute-start | bytes 4423688 | tf_op jit(solution)/shard_map/ppermute | solution.py:377
  60.3 4.3 %copy-start.4 = (s32[16]{0:T(128)S(1)}, s32[16]{0:T(128)}, u32[]{:S(2)}) copy-start(s32[16]{0:T(128)} %anc_ref.1) | copy-start | bytes 196
  60.3 4.2 %collective-permute-start.3 = (f32[8,128]{1,0:T(8,128)S(1)}, f32[8,128]{1,0:T(8,128)S(1)}, u32[]{:S(2)}, u32[]{:S(2)}) collective-permute-start(f32[8,128]{1,0:T(8,128)S(1)} %shard_map.77.refs_0_), channel_id=1, source_target_pairs={{0,32},{32,0},{1,33},{33,1},{2,34},{34,2},{3,35},{35,3},{4,36},{36... | collective-permute-start | bytes 12296 | tf_op jit(solution)/shard_map/ppermute | solution.py:380
  64.6 40.4 %copy-start = (bf16[640,1920]{1,0:T(8,128)(2,1)S(1)}, bf16[640,1920]{1,0:T(8,128)(2,1)}, u32[]{:S(2)}) copy-start(bf16[640,1920]{1,0:T(8,128)(2,1)} %w_ref.4) | copy-start | bytes 7372804
  132.6 24.3 %copy-start.1 = (bf16[640,640]{1,0:T(8,128)(2,1)S(1)}, bf16[640,640]{1,0:T(8,128)(2,1)}, u32[]{:S(2)}) copy-start(bf16[640,640]{1,0:T(8,128)(2,1)} %w_ref.5) | copy-start | bytes 2457604
